TPU v7x, 32 devices: a whole 2x2x4 slice. The times are simulated.
32 devices in a mesh: replica: 2 (over y), expert: 4 (over z), tensor: 4 (over x, core).
Axes of the slice: x: 2, y: 2, z: 4, core: 2. Of those that a mesh axis runs over, the one named last changes fastest.
Arguments:
- tokens: bfloat16 [2, 256, 2048], P(None, ('replica', 'expert'), 'tensor'), parts along dimension 1, may hold values from -6 to 6
- expert_ids: int32 [2, 256, 6], P(None, ('replica', 'expert')), parts along dimension 1, may hold values from 0 to 63, all different within a row; in each aligned block of 32 rows (0 to 31, 32 to 63, ..., all dimensions but the last counted through in order) at most 6 rows name the same one
- route_weights: float32 [2, 256, 6], P(None, ('replica', 'expert')), parts along dimension 1, may hold values from 0.05 to 0.5
- w_gate: bfloat16 [64, 2048, 1408], P('expert', None, 'tensor'), may hold values from -0.125 to 0.125
- w_up: bfloat16 [64, 2048, 1408], P('expert', None, 'tensor'), may hold values from -0.125 to 0.125
- w_down: bfloat16 [64, 1408, 2048], P('expert', 'tensor'), may hold values from -0.15625 to 0.15625
Outputs:
- combined: bfloat16 [2, 256, 2048], P(None, ('replica', 'expert'), 'tensor'), parts along dimension 1
There are 2 independent parts, one for each index of `replica`. A program takes and returns all parts, laid end to end along the dimension named above; an argument that names none is the same for every part. Nothing has to cross between parts.
Inputs may be any that keep to these rules, and one draw needn't show every extreme that they name: `expert_ids`: each row names 6 different experts. In each aligned block of 32 rows (the rows of one index of expert at one step) no expert is named by more than 6 rows, a bound that some block reaches.
All inputs are finite; a program needn't handle non-finite values.
Results may differ from a plain program's by a relative error of at most 0.014.
Values may be sent and summed in bfloat16 or wider, within the bound.
No kernel may reach another device: no remote copies, remote signals or barrier semaphores. Data moves between devices by JAX's collectives and lax.ppermute only.
A program may use at most 320 MiB of HBM per device.

v0:
```python
import jax
import jax.numpy as jnp
from jax import lax
from jax.sharding import PartitionSpec as P

EXPERTS = 64
CAP = 6


def slot_numbers(choice_ids):
    nblocks, nrows, npicks = choice_ids.shape
    flat_ids = choice_ids.reshape(nblocks, nrows * npicks)
    labels = lax.broadcasted_iota(jnp.int32, (1, 1, EXPERTS), 2)
    onehot = (flat_ids[:, :, None] == labels).astype(jnp.int32)
    earlier = jnp.cumsum(onehot, axis=1) - onehot
    position = jnp.sum(earlier * onehot, axis=2)
    return (flat_ids * CAP + position).reshape(nblocks, nrows, npicks)


def dispatch(slot_ids, row_data, slot_total):
    labels = lax.broadcasted_iota(jnp.int32, (1, slot_total, 1, 1), 1)
    chosen = jnp.sum((slot_ids[:, None, :, :] == labels).astype(jnp.int32), axis=3)
    placed = jnp.einsum(
        "bsr,brw->bsw", chosen.astype(jnp.bfloat16), row_data, preferred_element_type=jnp.float32
    )
    return placed.astype(jnp.bfloat16)


def expert_work(arrived_rows, w_gate, w_up, w_down):
    features = lax.all_gather(arrived_rows, "tensor", axis=3, tiled=True)
    decode_step_count, expert_holders, slot_count, feature_width = features.shape
    resident_weights = w_gate.shape[0]
    per_expert = slot_count // resident_weights
    grouped = features.reshape(
        decode_step_count, expert_holders, resident_weights, per_expert, feature_width
    )
    gate_val = jnp.einsum("bhecd,edf->bhecf", grouped, w_gate, preferred_element_type=jnp.float32)
    up_val = jnp.einsum("bhecd,edf->bhecf", grouped, w_up, preferred_element_type=jnp.float32)
    hidden = (jax.nn.silu(gate_val) * up_val).astype(jnp.bfloat16)
    partial_output_value = jnp.einsum(
        "bhecf,efd->bhecd", hidden, w_down, preferred_element_type=jnp.float32
    )
    partial_output_value = partial_output_value.astype(jnp.bfloat16)
    restored = partial_output_value.reshape(
        decode_step_count, expert_holders, slot_count, feature_width
    )
    summed = lax.psum_scatter(
        restored.astype(jnp.float32).astype(jnp.bfloat16), "tensor", scatter_dimension=3, tiled=True
    )
    return lax.all_to_all(summed, "expert", split_axis=1, concat_axis=1, tiled=True)


def per_device(tokens, expert_ids, route_weights, w_gate, w_up, w_down):
    expert_holders = lax.axis_size("expert")
    resident_weights = w_gate.shape[0]
    decode_step_count, nrows, share_width = tokens.shape
    slot_ids = slot_numbers(expert_ids)
    outgoing = dispatch(slot_ids, tokens, EXPERTS * CAP)
    outgoing = outgoing.reshape(
        decode_step_count, expert_holders, resident_weights * CAP, share_width
    )
    returned = expert_work(
        lax.all_to_all(outgoing, "expert", split_axis=1, concat_axis=1, tiled=True),
        w_gate,
        w_up,
        w_down,
    )
    returned = returned.reshape(decode_step_count, EXPERTS * CAP, share_width)
    labels = lax.broadcasted_iota(jnp.int32, (1, 1, 1, EXPERTS * CAP), 3)
    selector = (slot_ids[..., None] == labels).astype(jnp.bfloat16)
    picked = jnp.einsum("brks,bsw->brkw", selector, returned, preferred_element_type=jnp.float32)
    combined = jnp.sum(picked * route_weights[..., None], axis=2)
    return combined.astype(jnp.bfloat16)


def solution(mesh):
    return jax.shard_map(
        per_device,
        mesh=mesh,
        in_specs=(
            P(None, ("replica", "expert"), "tensor"),
            P(None, ("replica", "expert"), None),
            P(None, ("replica", "expert"), None),
            P("expert", None, "tensor"),
            P("expert", None, "tensor"),
            P("expert", "tensor", None),
        ),
        out_specs=P(None, ("replica", "expert"), "tensor"),
        check_vma=False,
    )
```

profile of v0, /device:TPU:0, one launch (start us, length us, event | category | flops | bytes accessed | tf_op | source)
XLA Modules:
  0.0 603.1 jit_solution(7442339044536907267)
XLA Ops:
  6.5 0.0 copy-start
  6.5 0.0 all-gather.2.cloned.1.call-start
  6.5 0.8 copy.47
  7.3 0.1 eq.48
  7.5 1.2 reduce-window.6
  8.7 0.2 slice_reduce_fusion
  9.0 0.1 bitcast_bitcast_fusion
  9.2 0.1 reduce_sum.30
  9.3 0.1 copy.50
  9.4 0.7 multiply_add_fusion
  10.1 0.1 convert_reduce_fusion
  10.2 0.0 copy-done
  10.2 0.4 convolution_convert_fusion
  10.6 0.1 copy.53
  10.7 26.3 %all_to_all.10 = bf16[2,4,96,512]{3,2,0,1:T(8,128)(2,1)} all-to-all(bf16[2,4,96,512]{3,2,0,1:T(8,128)(2,1)S(1)} %copy.53), channel_id=1, replica_groups=mesh['replica'=2,'expert'=4,'tensor'=4] {'expert'}, dimensions={1} | all-to-all | bytes 1572864 | tf_op jit(solution)/shard_map/all_to_all | solution.py:63
  37.0 0.0 all-gather.2.cloned.1.call-update
  37.0 0.0 reduce-scatter.4.cloned.1.call-start
  37.1 27.7 %all-gather.2.cloned.1.call-done = bf16[2,4,96,2048]{3,2,0,1:T(8,128)(2,1)} async-done(((bf16[2,4,96,512]{3,2,0,1:T(8,128)(2,1)}), bf16[2,4,96,2048]{3,2,0,1:T(8,128)(2,1)}) %all-gather.2.cloned.1.call-update) | async-done | bytes 3145744 | tf_op jit(solution)/shard_map/all_gather | solution.py:30
  64.8 4.3 copy.54
  69.2 13.7 %fusion.4 = f32[16,2,4,6,352]{4,3,2,1,0:T(8,128)} fusion(bf16[16,2048,352]{1,2,0:T(8,128)(2,1)} %param.9, bf16[2,4,16,6,2048]{4,1,3,2,0:T(4,128)(2,1)S(1)} %bitcast.67), kind=kOutput, calls=%fused_computation.4 | convolution fusion | flops 1107296256 | bytes 27295744 | tf_op jit(solution)/shard_map/bhecd,edf->bhecf/dot_general | solution.py:37
  82.9 14.3 %fusion.10 = bf16[2,4,16,6,352]{4,3,1,0,2:T(8,128)(2,1)} fusion(f32[16,2,4,6,352]{4,3,2,1,0:T(8,128)} %fusion.4, bf16[16,2048,352]{1,2,0:T(8,128)(2,1)} %param.10, bf16[2,4,16,6,2048]{4,1,3,2,0:T(4,128)(2,1)S(1)} %bitcast.68), kind=kOutput, calls=%fused_computation.10 | convolution fusion | flops 1108918272 | bytes 27836416 | tf_op jit(solution)/shard_map/bhecd,edf->bhecf/dot_general | solution.py:38
  97.2 12.2 %convert_bitcast_fusion = bf16[2,4,16,6,2048]{4,3,1,0,2:T(8,128)(2,1)S(1)} fusion(bf16[2,4,16,6,352]{4,3,1,0,2:T(8,128)(2,1)} %fusion.10, bf16[16,352,2048]{2,1,0:T(8,128)(2,1)} %param.11), kind=kOutput, calls=%fused_computation.8 | convolution fusion | flops 1108869120 | bytes 26755072 | tf_op jit(solution)/shard_map/bhecf,efd->bhecd/dot_general | solution.py:40
  109.4 3.0 copy.57
  112.4 156.7 %copy.65 = bf16[2,4,96,2048]{1,2,0,3:T(8,128)(2,1)} copy(bf16[2,4,96,2048]{3,1,2,0:T(4,128)(2,1)S(1)} %bitcast.69) | data formatting | bytes 6291456
  269.1 180.1 %reshape.49 = bf16[2048,768]{1,0:T(8,128)(2,1)} reshape(bf16[2048,2,96,4]{3,2,1,0:T(8,128)(2,1)} %bitcast.17) | data formatting | bytes 6291456
  449.2 0.0 reduce-scatter.4.cloned.1.call-update
  449.2 38.1 %reduce-scatter.4.cloned.1.call-done = bf16[512,768]{1,0:T(8,128)(2,1)} async-done(((bf16[2048,768]{1,0:T(8,128)(2,1)}), bf16[512,768]{1,0:T(8,128)(2,1)}) %reduce-scatter.4.cloned.1.call-update) | async-done | bytes 786448
  487.3 56.7 %reshape.50 = bf16[512,2,96,4]{3,2,1,0:T(8,128)(2,1)} reshape(bf16[512,768]{1,0:T(8,128)(2,1)} %reduce-scatter.4.cloned.1.call-done) | data formatting | bytes 1572864
  544.0 0.0 copy-start.2
  544.0 0.0 copy-start.1
  544.0 26.3 %copy.58 = bf16[2,4,96,512]{3,2,0,1:T(8,128)(2,1)} copy(bf16[2,4,96,512]{1,2,0,3:T(8,128)(2,1)} %bitcast.66) | data formatting | bytes 1572864 | tf_op jit(solution)/shard_map/reduce_scatter | solution.py:47
  570.4 4.6 all-to-all-start.1
  575.0 0.0 copy-done.2
  575.0 20.1 %all-to-all-done.1 = bf16[2,4,96,512]{3,2,0,1:T(8,128)(2,1)S(1)} async-done(((bf16[2,4,96,512]{3,2,0,1:T(8,128)(2,1)}), bf16[2,4,96,512]{3,2,0,1:T(8,128)(2,1)S(1)}, u32[]{:S(2)}, u32[]{:S(2)}) %all-to-all-start.1) | async-done | bytes 786464 | tf_op jit(solution)/shard_map/all_to_all | solution.py:50
  595.1 0.1 copy.59
  595.2 1.1 fusion.18
  596.2 0.0 copy-done.1
  (7 shorter events, 0.1 us)
Async XLA Ops:
  6.5 3.7 copy-start
  6.5 58.3 %all-gather.2.cloned.1.call-start = ((), (), s32[]{:S(2)}) async-start(), calls=%async_computation.3 | async-start | bytes 3932160 | tf_op jit(solution)/shard_map/all_gather | solution.py:30
  37.0 450.3 %reduce-scatter.4.cloned.1.call-start = ((), (), s32[]{:S(2)}) async-start(), calls=%async_computation.4 | async-start | bytes 3932160
  544.0 30.9 %copy-start.2 = (f32[2,32,6]{1,0,2:T(2,128)S(1)}, f32[2,32,6]{1,0,2:T(2,128)}, u32[]{:S(2)}) copy-start(f32[2,32,6]{1,0,2:T(2,128)} %param.8) | copy-start | bytes 4612
  544.0 52.2 %copy-start.1 = (bf16[2,32,512]{2,1,0:T(8,128)(2,1)S(1)}, bf16[2,32,512]{2,1,0:T(8,128)(2,1)}, u32[]{:S(2)}) copy-start(bf16[2,32,512]{2,1,0:T(8,128)(2,1)} %param.6) | copy-start | bytes 196612
  570.4 24.7 %all-to-all-start.1 = ((bf16[2,4,96,512]{3,2,0,1:T(8,128)(2,1)}), bf16[2,4,96,512]{3,2,0,1:T(8,128)(2,1)S(1)}, u32[]{:S(2)}, u32[]{:S(2)}) async-start(bf16[2,4,96,512]{3,2,0,1:T(8,128)(2,1)} %copy.58), calls=%async_computation.1 | async-start | bytes 1572864 | tf_op jit(solution)/shard_map/all_to_all | solution.py:50
Sparse Core Ops, SparseCore 0:
  37.2 27.6 all-gather.1
  449.3 37.9 reduce-scatter.3
where the time goes:
time: 604 us; the launch traced here: 603 us
  local copies, waits for them, and re-layouts  429 us (71%)
  waiting for transfers between devices  86 us (14%)
  matrix products  41.7 us (7%)
  blocking collectives  26.3 us (4%)
  between operations  13.5 us (2%)
    unnamed x11, local copies, waits for them, and re-layouts  394 us
    unnamed x3, waiting for transfers between devices  38.1 us
    all_gather x1, waiting for transfers between devices, expert_work(): features = lax.all_gather(arrived_rows, 'tensor', axis=3, tiled=True)  27.7 us
    all_to_all x1, blocking collectives, per_device(): lax.all_to_all(outgoing, 'expert', split_axis=1, concat_axis=1, tiled=True)  26.3 us
    reduce_scatter x1, local copies, waits for them, and re-layouts, expert_work(): lax.psum_scatter(restored.astype(jnp.float32).astype(jnp.bfloat16), 'tens...  26.3 us
    all_to_all x1, waiting for transfers between devices, expert_work(): lax.all_to_all(summed, 'expert', split_axis=1, concat_axis=1, tiled=True)  20.1 us
    dot_general x1, matrix products, expert_work(): jnp.einsum('bhecd,edf->bhecf', grouped, w_up, preferred_element_type=jnp....  14.3 us
    dot_general x1, matrix products, expert_work(): jnp.einsum('bhecd,edf->bhecf', grouped, w_gate, preferred_element_type=jn...  13.7 us
  transfers between devices with their start and end apart: 3, of which 3 were waited for; matrix products, arithmetic and copies ran while one was open for 0% of the time, Pallas kernels for 0%

commit v1 on v0

--- a/solution.py
+++ b/solution.py
@@ -1,6 +1,10 @@
+import functools
+
 import jax
 import jax.numpy as jnp
 from jax import lax
+from jax.experimental import pallas as pl
+from jax.experimental.pallas import tpu as pltpu
 from jax.sharding import PartitionSpec as P
 
 EXPERTS = 64
@@ -73,9 +77,136 @@
     return combined.astype(jnp.bfloat16)
 
 
+NT = (((1,), (1,)), ((), ()))
+NN = (((1,), (0,)), ((), ()))
+TN = (((0,), (0,)), ((), ()))
+META = 128
+
+
+def dot(a, b, dims):
+    return lax.dot_general(a, b, dims, preferred_element_type=jnp.float32)
+
+
+def route(place, meta, picks, slots, residents, pick_mat, slot_weight):
+    rows = meta.shape[0]
+    by_pick = meta.astype(jnp.float32).T
+    labels = (place[0] + lax.broadcasted_iota(jnp.int32, (residents, rows), 0)).astype(jnp.float32)
+    chosen = jnp.zeros((residents, rows), jnp.float32)
+    weight = jnp.zeros((residents, rows), jnp.float32)
+    for k in range(picks):
+        hit = by_pick[k : k + 1, :] == labels
+        share = by_pick[picks + k : picks + k + 1, :] + by_pick[2 * picks + k : 2 * picks + k + 1, :]
+        chosen = jnp.where(hit, 1.0, chosen)
+        weight = jnp.where(hit, share, weight)
+    before = lax.broadcasted_iota(jnp.int32, (rows, rows), 0) < lax.broadcasted_iota(jnp.int32, (rows, rows), 1)
+    rank = dot(chosen.astype(jnp.bfloat16), before.astype(jnp.bfloat16), NN)
+    rank = jnp.where(chosen > 0.0, rank, -1.0)
+    numbers = lax.broadcasted_iota(jnp.int32, (slots, rows), 0).astype(jnp.float32)
+    for e in range(residents):
+        hit = numbers == rank[e : e + 1, :]
+        pick_mat[e * slots : (e + 1) * slots, :] = hit.astype(jnp.bfloat16)
+        spread = jnp.sum(jnp.where(hit, weight[e : e + 1, :], 0.0), axis=1, keepdims=True)
+        slot_weight[e * slots : (e + 1) * slots, :] = jnp.broadcast_to(spread, (slots, 128))
+
+
+def expert_kernel(picks, slots, place, own, other, meta, wg, wu, wd, out, pick_mat, slot_weight, taken, given):
+    e = pl.program_id(0)
+    residents = pl.num_programs(0)
+    share = own.shape[2]
+
+    def columns(j):
+        return pl.ds(pl.multiple_of((place[1] ^ j) * share, share), share)
+
+    @pl.when(e == 0)
+    def _():
+        route(place, meta[...], picks, slots, pick_mat.shape[0] // slots, pick_mat, slot_weight)
+        for j, piece in enumerate((own[0], other[0], own[1], other[1])):
+            taken[:, columns(j)] = dot(pick_mat[...], piece, NN).astype(jnp.bfloat16)
+
+    mine = pl.ds(pl.multiple_of(e * slots, slots), slots)
+    x = taken[mine, :]
+    gate = dot(x, wg[0], NT)
+    up = dot(x, wu[0], NT)
+    hidden = gate * jax.nn.sigmoid(gate) * up * slot_weight[mine, :1]
+    given[mine, :] = dot(hidden.astype(jnp.bfloat16), wd[0], NN).astype(jnp.bfloat16)
+
+    @pl.when(e == residents - 1)
+    def _():
+        for j in range(4):
+            out[j] = dot(pick_mat[...], given[:, columns(j)], TN).astype(jnp.bfloat16)
+
+
+def experts(place, own, other, meta, wg, wu, wd, picks, slots):
+    residents, hidden_units, width = wg.shape
+    rows, share = own.shape[1], own.shape[2]
+    whole = lambda a: pl.BlockSpec(a.shape, lambda e, *_: (0,) * a.ndim)
+    each = lambda a: pl.BlockSpec((1,) + a.shape[1:], lambda e, *_: (e, 0, 0))
+    return pl.pallas_call(
+        functools.partial(expert_kernel, picks, slots),
+        grid_spec=pltpu.PrefetchScalarGridSpec(
+            num_scalar_prefetch=1,
+            grid=(residents,),
+            in_specs=[whole(own), whole(other), whole(meta), each(wg), each(wu), each(wd)],
+            out_specs=pl.BlockSpec((4, rows, share), lambda e, *_: (0, 0, 0)),
+            scratch_shapes=[
+                pltpu.VMEM((residents * slots, rows), jnp.bfloat16),
+                pltpu.VMEM((residents * slots, 128), jnp.float32),
+                pltpu.VMEM((residents * slots, width), jnp.bfloat16),
+                pltpu.VMEM((residents * slots, width), jnp.bfloat16),
+            ],
+        ),
+        out_shape=jax.ShapeDtypeStruct((4, rows, share), jnp.bfloat16),
+        compiler_params=pltpu.CompilerParams(vmem_limit_bytes=44 << 20),
+    )(place, own, other, meta, wg, wu, wd)
+
+
+def swap(a, axis, bits):
+    n = lax.axis_size(axis)
+    return lax.ppermute(a, axis, [(i, i ^ bits) for i in range(n)])
+
+
+def small_group(tokens, expert_ids, route_weights, w_gate, w_up, w_down):
+    steps, nrows, share = tokens.shape
+    picks = expert_ids.shape[-1]
+    holders = lax.axis_size("expert")
+    residents = w_gate.shape[0]
+    block = steps * nrows
+    slots = steps * holders * CAP
+    high = lax.reduce_precision(route_weights, 8, 7)
+    meta = jnp.concatenate([expert_ids.astype(jnp.float32), high, route_weights - high], axis=2)
+    meta = jnp.pad(meta, ((0, 0), (0, 0), (0, META - 3 * picks))).reshape(block, META).astype(jnp.bfloat16)
+    mine = tokens.reshape(block, share)
+    pair = jnp.concatenate([mine, swap(mine, "tensor", 2), meta], axis=1)
+    held = jnp.stack([pair] + [swap(pair, "expert", k) for k in range(1, holders)])
+    held = held.reshape(holders * block, 2 * share + META)
+    own = jnp.stack([held[:, :share], held[:, share : 2 * share]])
+    other = swap(own, "tensor", 1)
+    place = jnp.stack([lax.axis_index("expert") * residents, lax.axis_index("tensor")]).astype(jnp.int32)
+    parts = experts(
+        place, own, other, held[:, 2 * share :], w_gate.swapaxes(1, 2), w_up.swapaxes(1, 2), w_down, picks, slots
+    )
+    wide = lambda a: a.astype(jnp.float32)
+    came = swap(jnp.stack([parts[1], parts[3]]), "tensor", 1)
+    away = (wide(parts[2]) + wide(came[1])).astype(jnp.bfloat16)
+    home = wide(parts[0]) + wide(came[0]) + wide(swap(away, "tensor", 2))
+    home = home.reshape(holders, block, share)
+    sent = home.astype(jnp.bfloat16)
+    total = home[0]
+    for k in range(1, holders):
+        total = total + wide(swap(sent[k], "expert", k))
+    return total.reshape(steps, nrows, share).astype(jnp.bfloat16)
+
+
+def pick_plan(*arrays):
+    holders, splits = lax.axis_size("expert"), lax.axis_size("tensor")
+    residents = arrays[3].shape[0]
+    small = holders == 4 and splits == 4 and residents == 16
+    return (small_group if small else per_device)(*arrays)
+
+
 def solution(mesh):
     return jax.shard_map(
-        per_device,
+        pick_plan,
         mesh=mesh,
         in_specs=(
             P(None, ("replica", "expert"), "tensor"),

time: 604 us -> 77.8 us (0.13)
  local copies, waits for them, and re-layouts: 429 us -> 0.21 us
  waiting for transfers between devices: 86 us -> 25.2 us
  matrix products: 41.7 us -> 0 us
  Pallas kernels: 0 us -> 33 us
  blocking collectives: 26.3 us -> 0 us
  between operations: 13.5 us -> 0.09 us
  starting transfers between devices: 4.65 us -> 15.6 us
    unnamed x11 -> x1, local copies, waits for them, and re-layouts: 394 us -> 0.11 us
    dot_general x5 -> x0, matrix products: 41.7 us -> none  [the longest x1 14.3 us: expert_work(): jnp.einsum('bhecd,edf->bhecf', grouped, w_up, preferred_element_type=jnp....]
    unnamed x3 -> x0, waiting for transfers between devices: 38.1 us -> none
    pallas_call x0 -> x1, Pallas kernels: none -> 33 us  [experts(): pl.pallas_call(functools.partial(expert_kernel, picks, slots), grid_spec=...]
    all_gather x1 -> x0, waiting for transfers between devices: 27.7 us -> none  [expert_work(): features = lax.all_gather(arrived_rows, 'tensor', axis=3, tiled=True)]
    all_to_all x1 -> x0, blocking collectives: 26.3 us -> none  [per_device(): lax.all_to_all(outgoing, 'expert', split_axis=1, concat_axis=1, tiled=True)]
    reduce_scatter x1 -> x0, local copies, waits for them, and re-layouts: 26.3 us -> none  [expert_work(): lax.psum_scatter(restored.astype(jnp.float32).astype(jnp.bfloat16), 'tens...]
    ppermute x0 -> x10, waiting for transfers between devices: none -> 25.2 us  [swap(): return lax.ppermute(a, axis, [(i, i ^ bits) for i in range(n)])]
  transfers between devices with their start and end apart: 3 -> 10, of which waited for: 3 -> 8; matrix products, arithmetic and copies ran while one was open for 0% -> 2% of each run, Pallas kernels for 0% -> 0%
where the time goes in v1:
time: 77.8 us; the launch traced here: 77.5 us
  Pallas kernels  33 us (42%)
  waiting for transfers between devices  25.2 us (32%)
  starting transfers between devices  15.6 us (20%)
  other arithmetic  3.37 us (4%)
    pallas_call x1, Pallas kernels, experts(): pl.pallas_call(functools.partial(expert_kernel, picks, slots), grid_spec=...  33 us
    ppermute x10, waiting for transfers between devices, swap(): return lax.ppermute(a, axis, [(i, i ^ bits) for i in range(n)])  25.2 us
    ppermute x10, starting transfers between devices, swap(): return lax.ppermute(a, axis, [(i, i ^ bits) for i in range(n)])  15.6 us
  transfers between devices with their start and end apart: 10, of which 8 were waited for; matrix products, arithmetic and copies ran while one was open for 2% of the time, Pallas kernels for 0%

profile of v1, /device:TPU:0, one launch (start us, length us, event | category | flops | bytes accessed | tf_op | source)
XLA Modules:
  0.0 77.5 jit_solution(17267563686310198988)
XLA Ops:
  0.0 2.9 %collective-permute-start = (bf16[64,512]{1,0:T(8,128)(2,1)}, bf16[64,512]{1,0:T(8,128)(2,1)S(1)}, u32[]{:S(2)}, u32[]{:S(2)}) collective-permute-start(bf16[64,512]{1,0:T(8,128)(2,1)} %bitcast.30), channel_id=1, source_target_pairs={{0,2},{1,3},{2,0},{3,1},{4,6},{5,7},{6,4},{7,5},{8,10},{9,11},{10,... | collective-permute-start | bytes 196616 | tf_op jit(solution)/shard_map/ppermute | solution.py:165
  2.9 0.7 convert_convert_fusion
  3.6 0.7 reduce-precision_convert_fusion
  4.4 0.1 copy.12
  4.5 0.9 %collective-permute-done = bf16[64,512]{1,0:T(8,128)(2,1)S(1)} collective-permute-done((bf16[64,512]{1,0:T(8,128)(2,1)}, bf16[64,512]{1,0:T(8,128)(2,1)S(1)}, u32[]{:S(2)}, u32[]{:S(2)}) %collective-permute-start) | collective-permute-done | bytes 65568 | tf_op jit(solution)/shard_map/ppermute | solution.py:165
  5.4 0.9 %fusion.5 = (bf16[1,64,1152]{2,1,0:T(8,128)(2,1)S(1)}, bf16[64,1152]{1,0:T(8,128)(2,1)S(1)}) fusion(bf16[64,128]{1,0:T(8,128)(2,1)S(1)} %bitcast.29, bf16[64,512]{1,0:T(8,128)(2,1)S(1)} %collective-permute-done, bf16[64,512]{1,0:T(8,128)(2,1)} %bitcast.31), kind=kLoop, calls=%fused_computation.19 | loop fusion | flops 442368 | bytes 442368 | tf_op jit(solution)/shard_map/stack | solution.py:180
  6.3 3.2 %collective-permute-start.2 = (bf16[64,1152]{1,0:T(8,128)(2,1)S(1)}, bf16[64,1152]{1,0:T(8,128)(2,1)S(1)}, u32[]{:S(2)}, u32[]{:S(2)}) collective-permute-start(bf16[64,1152]{1,0:T(8,128)(2,1)S(1)} %get-tuple-element.15), channel_id=1, source_target_pairs={{0,8},{4,12},{8,0},{12,4},{1,9},{5,13},{9,1},{13,5},{2,10},{6,14},... | collective-permute-start | bytes 442376 | tf_op jit(solution)/shard_map/ppermute | solution.py:165
  9.4 1.6 %collective-permute-start.1 = (bf16[64,1152]{1,0:T(8,128)(2,1)S(1)}, bf16[64,1152]{1,0:T(8,128)(2,1)S(1)}, u32[]{:S(2)}, u32[]{:S(2)}) collective-permute-start(bf16[64,1152]{1,0:T(8,128)(2,1)S(1)} %get-tuple-element.15), channel_id=1, source_target_pairs={{0,4},{4,0},{8,12},{12,8},{1,5},{5,1},{9,13},{13,9},{2,6},{6,2},{1... | collective-permute-start | bytes 442376 | tf_op jit(solution)/shard_map/ppermute | solution.py:165
  11.0 0.0 collective-permute-start.3
  11.0 7.1 %collective-permute-done.2 = bf16[64,1152]{1,0:T(8,128)(2,1)S(1)} collective-permute-done((bf16[64,1152]{1,0:T(8,128)(2,1)S(1)}, bf16[64,1152]{1,0:T(8,128)(2,1)S(1)}, u32[]{:S(2)}, u32[]{:S(2)}) %collective-permute-start.2) | collective-permute-done | bytes 147488 | tf_op jit(solution)/shard_map/ppermute | solution.py:165
  18.1 0.0 collective-permute-done.1
  18.1 1.6 %collective-permute-done.3 = bf16[64,1152]{1,0:T(8,128)(2,1)S(1)} collective-permute-done((bf16[64,1152]{1,0:T(8,128)(2,1)S(1)}, bf16[64,1152]{1,0:T(8,128)(2,1)S(1)}, u32[]{:S(2)}, u32[]{:S(2)}) %collective-permute-start.3) | collective-permute-done | bytes 147488 | tf_op jit(solution)/shard_map/ppermute | solution.py:165
  19.7 0.1 pad_maximum_fusion
  19.9 0.1 pad_maximum_fusion.1.own
  19.9 0.1 collective-permute-start.4
  20.0 0.1 pad_add_fusion.place
  20.1 1.8 %collective-permute-done.4.other = bf16[2,256,512]{2,1,0:T(8,128)(2,1)S(1)} collective-permute-done((bf16[2,256,512]{2,1,0:T(8,128)(2,1)S(1)}, bf16[2,256,512]{2,1,0:T(8,128)(2,1)S(1)}, u32[]{:S(2)}, u32[]{:S(2)}) %collective-permute-start.4) | collective-permute-done | bytes 524320 | tf_op jit(solution)/shard_map/ppermute | solution.py:165
  21.9 33.0 %shard_map.64 = bf16[4,256,512]{2,1,0:T(8,128)(2,1)S(1)} custom-call(s32[2]{0:T(128)S(1)} %pad_add_fusion.place, bf16[2,256,512]{2,1,0:T(8,128)(2,1)S(1)} %pad_maximum_fusion.1.own, bf16[2,256,512]{2,1,0:T(8,128)(2,1)S(1)} %collective-permute-done.4.other, bf16[256,128]{1,0:T(8,128)(2,1)S(1)} %slice.58.meta, bf16[16,352,2048]{2,1,0:T(8,128)(2,1)} %bitcast.22, ...), custom_call_target="tpu_custom_call" | custom-call | tf_op jit(solution)/shard_map/pallas_call | solution.py:144
  55.0 0.1 pad_maximum_fusion.2
  55.0 0.2 collective-permute-start.5
  55.2 1.8 %collective-permute-done.5 = bf16[2,256,512]{2,1,0:T(8,128)(2,1)S(1)} collective-permute-done((bf16[2,256,512]{2,1,0:T(8,128)(2,1)S(1)}, bf16[2,256,512]{2,1,0:T(8,128)(2,1)S(1)}, u32[]{:S(2)}, u32[]{:S(2)}) %collective-permute-start.5) | collective-permute-done | bytes 524320 | tf_op jit(solution)/shard_map/ppermute | solution.py:165
  57.0 0.1 fusion
  57.1 1.6 %collective-permute-start.6 = (bf16[256,512]{1,0:T(8,128)(2,1)S(1)}, bf16[256,512]{1,0:T(8,128)(2,1)S(1)}, u32[]{:S(2)}, u32[]{:S(2)}) collective-permute-start(bf16[256,512]{1,0:T(8,128)(2,1)S(1)} %fusion), channel_id=1, source_target_pairs={{0,2},{1,3},{2,0},{3,1},{4,6},{5,7},{6,4},{7,5},{8,10},{9,11},{10,... | collective-permute-start | bytes 786440 | tf_op jit(solution)/shard_map/ppermute | solution.py:165
  58.6 6.9 %collective-permute-done.6 = bf16[256,512]{1,0:T(8,128)(2,1)S(1)} collective-permute-done((bf16[256,512]{1,0:T(8,128)(2,1)S(1)}, bf16[256,512]{1,0:T(8,128)(2,1)S(1)}, u32[]{:S(2)}, u32[]{:S(2)}) %collective-permute-start.6) | collective-permute-done | bytes 262176 | tf_op jit(solution)/shard_map/ppermute | solution.py:165
  65.5 0.1 fusion.6
  65.6 2.7 %collective-permute-start.7 = (bf16[64,512]{1,0:T(8,128)(2,1)S(1)}, bf16[64,512]{1,0:T(8,128)(2,1)S(1)}, u32[]{:S(2)}, u32[]{:S(2)}) collective-permute-start(bf16[64,512]{1,0:T(8,128)(2,1)S(1)} %get-tuple-element.11), channel_id=1, source_target_pairs={{0,4},{4,0},{8,12},{12,8},{1,5},{5,1},{9,13},{13,9},{2,6},{6,2},{1... | collective-permute-start | bytes 196616 | tf_op jit(solution)/shard_map/ppermute | solution.py:165
  68.3 3.4 %collective-permute-start.9 = (bf16[64,512]{1,0:T(8,128)(2,1)S(1)}, bf16[64,512]{1,0:T(8,128)(2,1)S(1)}, u32[]{:S(2)}, u32[]{:S(2)}) collective-permute-start(bf16[64,512]{1,0:T(8,128)(2,1)S(1)} %get-tuple-element.12), channel_id=1, source_target_pairs={{0,12},{4,8},{8,4},{12,0},{1,13},{5,9},{9,5},{13,1},{2,14},{6,10},... | collective-permute-start | bytes 196616 | tf_op jit(solution)/shard_map/ppermute | solution.py:165
  71.7 0.0 collective-permute-start.8
  71.7 0.0 collective-permute-done.7
  71.7 3.4 %collective-permute-done.9 = bf16[64,512]{1,0:T(8,128)(2,1)S(1)} collective-permute-done((bf16[64,512]{1,0:T(8,128)(2,1)S(1)}, bf16[64,512]{1,0:T(8,128)(2,1)S(1)}, u32[]{:S(2)}, u32[]{:S(2)}) %collective-permute-start.9) | collective-permute-done | bytes 65568 | tf_op jit(solution)/shard_map/ppermute | solution.py:165
  75.1 1.7 %collective-permute-done.8 = bf16[64,512]{1,0:T(8,128)(2,1)S(1)} collective-permute-done((bf16[64,512]{1,0:T(8,128)(2,1)S(1)}, bf16[64,512]{1,0:T(8,128)(2,1)S(1)}, u32[]{:S(2)}, u32[]{:S(2)}) %collective-permute-start.8) | collective-permute-done | bytes 65568 | tf_op jit(solution)/shard_map/ppermute | solution.py:165
  76.9 0.7 fusion.3
  (6 shorter events, 0.1 us)
Async XLA Ops:
  0.0 5.4 %collective-permute-start = (bf16[64,512]{1,0:T(8,128)(2,1)}, bf16[64,512]{1,0:T(8,128)(2,1)S(1)}, u32[]{:S(2)}, u32[]{:S(2)}) collective-permute-start(bf16[64,512]{1,0:T(8,128)(2,1)} %bitcast.30), channel_id=1, source_target_pairs={{0,2},{1,3},{2,0},{3,1},{4,6},{5,7},{6,4},{7,5},{8,10},{9,11},{10,... | collective-permute-start | bytes 196616 | tf_op jit(solution)/shard_map/ppermute | solution.py:165
  6.3 11.9 %collective-permute-start.2 = (bf16[64,1152]{1,0:T(8,128)(2,1)S(1)}, bf16[64,1152]{1,0:T(8,128)(2,1)S(1)}, u32[]{:S(2)}, u32[]{:S(2)}) collective-permute-start(bf16[64,1152]{1,0:T(8,128)(2,1)S(1)} %get-tuple-element.15), channel_id=1, source_target_pairs={{0,8},{4,12},{8,0},{12,4},{1,9},{5,13},{9,1},{13,5},{2,10},{6,14},... | collective-permute-start | bytes 442376 | tf_op jit(solution)/shard_map/ppermute | solution.py:165
  9.4 8.7 %collective-permute-start.1 = (bf16[64,1152]{1,0:T(8,128)(2,1)S(1)}, bf16[64,1152]{1,0:T(8,128)(2,1)S(1)}, u32[]{:S(2)}, u32[]{:S(2)}) collective-permute-start(bf16[64,1152]{1,0:T(8,128)(2,1)S(1)} %get-tuple-element.15), channel_id=1, source_target_pairs={{0,4},{4,0},{8,12},{12,8},{1,5},{5,1},{9,13},{13,9},{2,6},{6,2},{1... | collective-permute-start | bytes 442376 | tf_op jit(solution)/shard_map/ppermute | solution.py:165
  11.0 8.7 %collective-permute-start.3 = (bf16[64,1152]{1,0:T(8,128)(2,1)S(1)}, bf16[64,1152]{1,0:T(8,128)(2,1)S(1)}, u32[]{:S(2)}, u32[]{:S(2)}) collective-permute-start(bf16[64,1152]{1,0:T(8,128)(2,1)S(1)} %get-tuple-element.15), channel_id=1, source_target_pairs={{0,12},{4,8},{8,4},{12,0},{1,13},{5,9},{9,5},{13,1},{2,14},{6,10},... | collective-permute-start | bytes 442376 | tf_op jit(solution)/shard_map/ppermute | solution.py:165
  19.9 2.0 %collective-permute-start.4 = (bf16[2,256,512]{2,1,0:T(8,128)(2,1)S(1)}, bf16[2,256,512]{2,1,0:T(8,128)(2,1)S(1)}, u32[]{:S(2)}, u32[]{:S(2)}) collective-permute-start(bf16[2,256,512]{2,1,0:T(8,128)(2,1)S(1)} %pad_maximum_fusion.1.own), channel_id=1, source_target_pairs={{0,1},{1,0},{2,3},{3,2},{4,5},{5,4},{6,7},{7,6},{8,9},{9,8},{10,11... | collective-permute-start | bytes 1572872 | tf_op jit(solution)/shard_map/ppermute | solution.py:165
  55.0 2.0 %collective-permute-start.5 = (bf16[2,256,512]{2,1,0:T(8,128)(2,1)S(1)}, bf16[2,256,512]{2,1,0:T(8,128)(2,1)S(1)}, u32[]{:S(2)}, u32[]{:S(2)}) collective-permute-start(bf16[2,256,512]{2,1,0:T(8,128)(2,1)S(1)} %pad_maximum_fusion.2), channel_id=1, source_target_pairs={{0,1},{1,0},{2,3},{3,2},{4,5},{5,4},{6,7},{7,6},{8,9},{9,8},{10,11... | collective-permute-start | bytes 1572872 | tf_op jit(solution)/shard_map/ppermute | solution.py:165
  57.1 8.4 %collective-permute-start.6 = (bf16[256,512]{1,0:T(8,128)(2,1)S(1)}, bf16[256,512]{1,0:T(8,128)(2,1)S(1)}, u32[]{:S(2)}, u32[]{:S(2)}) collective-permute-start(bf16[256,512]{1,0:T(8,128)(2,1)S(1)} %fusion), channel_id=1, source_target_pairs={{0,2},{1,3},{2,0},{3,1},{4,6},{5,7},{6,4},{7,5},{8,10},{9,11},{10,... | collective-permute-start | bytes 786440 | tf_op jit(solution)/shard_map/ppermute | solution.py:165
  65.6 6.1 %collective-permute-start.7 = (bf16[64,512]{1,0:T(8,128)(2,1)S(1)}, bf16[64,512]{1,0:T(8,128)(2,1)S(1)}, u32[]{:S(2)}, u32[]{:S(2)}) collective-permute-start(bf16[64,512]{1,0:T(8,128)(2,1)S(1)} %get-tuple-element.11), channel_id=1, source_target_pairs={{0,4},{4,0},{8,12},{12,8},{1,5},{5,1},{9,13},{13,9},{2,6},{6,2},{1... | collective-permute-start | bytes 196616 | tf_op jit(solution)/shard_map/ppermute | solution.py:165
  68.3 6.8 %collective-permute-start.9 = (bf16[64,512]{1,0:T(8,128)(2,1)S(1)}, bf16[64,512]{1,0:T(8,128)(2,1)S(1)}, u32[]{:S(2)}, u32[]{:S(2)}) collective-permute-start(bf16[64,512]{1,0:T(8,128)(2,1)S(1)} %get-tuple-element.12), channel_id=1, source_target_pairs={{0,12},{4,8},{8,4},{12,0},{1,13},{5,9},{9,5},{13,1},{2,14},{6,10},... | collective-permute-start | bytes 196616 | tf_op jit(solution)/shard_map/ppermute | solution.py:165
  71.7 5.2 %collective-permute-start.8 = (bf16[64,512]{1,0:T(8,128)(2,1)S(1)}, bf16[64,512]{1,0:T(8,128)(2,1)S(1)}, u32[]{:S(2)}, u32[]{:S(2)}) collective-permute-start(bf16[64,512]{1,0:T(8,128)(2,1)S(1)} %get-tuple-element.13), channel_id=1, source_target_pairs={{0,8},{4,12},{8,0},{12,4},{1,9},{5,13},{9,1},{13,5},{2,10},{6,14},... | collective-permute-start | bytes 196616 | tf_op jit(solution)/shard_map/ppermute | solution.py:165

commit v2 on v0

--- a/solution.py
+++ b/solution.py
@@ -1,6 +1,10 @@
+import functools
+
 import jax
 import jax.numpy as jnp
 from jax import lax
+from jax.experimental import pallas as pl
+from jax.experimental.pallas import tpu as pltpu
 from jax.sharding import PartitionSpec as P
 
 EXPERTS = 64
@@ -73,9 +77,221 @@
     return combined.astype(jnp.bfloat16)
 
 
+NT = (((1,), (1,)), ((), ()))
+NN = (((1,), (0,)), ((), ()))
+TN = (((0,), (0,)), ((), ()))
+META = 128
+TOPK = 6
+GROUP = 2
+
+
+def dot(a, b, dims):
+    return lax.dot_general(a, b, dims, preferred_element_type=jnp.float32)
+
+
+def route(place, meta, picks, slots, residents, pick_mat, slot_weight):
+    rows = meta.shape[0]
+    by_pick = meta.astype(jnp.float32).T
+    labels = (place[0] + lax.broadcasted_iota(jnp.int32, (residents, rows), 0)).astype(jnp.float32)
+    chosen = jnp.zeros((residents, rows), jnp.float32)
+    weight = jnp.zeros((residents, rows), jnp.float32)
+    for k in range(picks):
+        hit = by_pick[k : k + 1, :] == labels
+        share = by_pick[picks + k : picks + k + 1, :] + by_pick[2 * picks + k : 2 * picks + k + 1, :]
+        chosen = jnp.where(hit, 1.0, chosen)
+        weight = jnp.where(hit, share, weight)
+    before = lax.broadcasted_iota(jnp.int32, (rows, rows), 0) < lax.broadcasted_iota(jnp.int32, (rows, rows), 1)
+    rank = dot(chosen.astype(jnp.bfloat16), before.astype(jnp.bfloat16), NN)
+    rank = jnp.where(chosen > 0.0, rank, -1.0)
+    numbers = lax.broadcasted_iota(jnp.int32, (slots, rows), 0).astype(jnp.float32)
+    for e in range(residents):
+        hit = numbers == rank[e : e + 1, :]
+        pick_mat[e * slots : (e + 1) * slots, :] = hit.astype(jnp.bfloat16)
+        spread = jnp.sum(jnp.where(hit, weight[e : e + 1, :], 0.0), axis=1, keepdims=True)
+        slot_weight[e * slots : (e + 1) * slots, :] = jnp.broadcast_to(spread, (slots, 128))
+
+
+def fetch(weights, buffers, sems, column, e):
+    width = buffers[0].shape[2]
+    return [
+        pltpu.make_async_copy(w.at[e, :, pl.ds(column, width)], b.at[e], sems.at[i, e])
+        for i, (w, b) in enumerate(zip(weights, buffers))
+    ]
+
+
+def fetch_all(weights, buffers, sems, column):
+    for e in range(buffers[0].shape[0]):
+        for copy in fetch(weights, buffers, sems, column, e):
+            copy.start()
+
+
+def place_rows(place, pick_mat, near, far, taken):
+    share = near.shape[1]
+    low = place[1] & 1
+    for column, piece in ((low, near), (1 - low, far)):
+        rows = dot(pick_mat[...], piece[...], NN).astype(jnp.bfloat16)
+        taken[:, pl.ds(pl.multiple_of(column * share, share), share)] = rows
+
+
+def add_up(place, pick_back, given, out):
+    share = out.shape[2]
+    low = place[1] & 1
+    for j, column in enumerate((low, 1 - low)):
+        block = given[:, pl.ds(pl.multiple_of(column * share, share), share)]
+        out[j] = dot(pick_back[...], block, NN).astype(jnp.bfloat16)
+
+
+def over_experts(residents, slots, work):
+    def some(step, carry):
+        for g in range(GROUP):
+            e = step * GROUP + g
+            work(e, pl.ds(pl.multiple_of(e * slots, slots), slots))
+        return carry
+
+    lax.fori_loop(0, residents // GROUP, some, 0)
+
+
+def half_kernel(slots, place, near, far, meta, wg, wu, *rest):
+    pick_mat, pick_back, slot_weight, gate, up, taken, bg, bu, sems = rest
+    column = pl.multiple_of((place[1] >> 1) * bg.shape[2], bg.shape[2])
+    fetch_all((wg, wu), (bg, bu), sems, column)
+    route(place, meta[...], TOPK, slots, pick_mat.shape[0] // slots, pick_mat, slot_weight)
+    place_rows(place, pick_mat, near, far, taken)
+    pick_back[...] = pick_mat[...].T
+
+    def work(e, mine):
+        for copy in fetch((wg, wu), (bg, bu), sems, column, e):
+            copy.wait()
+        x = taken[mine, :]
+        gate[mine, :] = dot(x, bg[e], NT)
+        up[mine, :] = dot(x, bu[e], NT)
+
+    over_experts(bg.shape[0], slots, work)
+
+
+def rest_kernel(slots, place, near, far, pick_mat, pick_back, slot_weight, gate, up, wg, wu, wd, *rest):
+    hidden, out, taken, given, bg, bu, bd, sems = rest
+    column = pl.multiple_of(((place[1] >> 1) ^ 1) * bg.shape[2], bg.shape[2])
+    fetch_all((wg, wu, wd), (bg, bu, bd), sems, column)
+    place_rows(place, pick_mat, near, far, taken)
+
+    def work(e, mine):
+        for copy in fetch((wg, wu, wd), (bg, bu, bd), sems, column, e):
+            copy.wait()
+        x = taken[mine, :]
+        gate_val = gate[mine, :] + dot(x, bg[e], NT)
+        up_val = up[mine, :] + dot(x, bu[e], NT)
+        scaled = gate_val * jax.nn.sigmoid(gate_val) * up_val * slot_weight[mine, :1]
+        scaled = scaled.astype(jnp.bfloat16)
+        hidden[mine, :] = scaled
+        given[mine, :] = dot(scaled, bd[e], NN).astype(jnp.bfloat16)
+
+    over_experts(bg.shape[0], slots, work)
+    add_up(place, pick_back, given, out)
+
+
+def down_kernel(slots, place, hidden, pick_back, wd, out, given, bd, sems):
+    column = pl.multiple_of((place[1] >> 1) * bd.shape[2], bd.shape[2])
+    fetch_all((wd,), (bd,), sems, column)
+
+    def work(e, mine):
+        for copy in fetch((wd,), (bd,), sems, column, e):
+            copy.wait()
+        given[mine, :] = dot(hidden[mine, :], bd[e], NN).astype(jnp.bfloat16)
+
+    over_experts(bd.shape[0], slots, work)
+    add_up(place, pick_back, given, out)
+
+
+def call(kernel, args, fetched, outs, scratch, micros):
+    vmem, there = pl.BlockSpec(memory_space=pltpu.VMEM), pl.BlockSpec(memory_space=pl.ANY)
+    local = len(args) - fetched - 1
+    return pl.pallas_call(
+        kernel,
+        in_specs=[pl.BlockSpec(memory_space=pltpu.SMEM)] + [vmem] * local + [there] * fetched,
+        out_specs=jax.tree.map(lambda _: vmem, outs),
+        out_shape=outs,
+        scratch_shapes=scratch,
+        compiler_params=pltpu.CompilerParams(vmem_limit_bytes=48 << 20),
+        cost_estimate=pl.CostEstimate(flops=micros * 10**9, bytes_accessed=micros * 3 * 10**6, transcendentals=0),
+    )(*args)
+
+
+def swap(a, axis, bits):
+    n = lax.axis_size(axis)
+    return lax.ppermute(a, axis, [(i, i ^ bits) for i in range(n)])
+
+
+def small_group(tokens, expert_ids, route_weights, w_gate, w_up, w_down):
+    steps, nrows, share = tokens.shape
+    picks = expert_ids.shape[-1]
+    holders = lax.axis_size("expert")
+    residents = w_gate.shape[0]
+    block = steps * nrows
+    slots = steps * holders * CAP
+    high = lax.reduce_precision(route_weights, 8, 7)
+    meta = jnp.concatenate([expert_ids.astype(jnp.float32), high, route_weights - high], axis=2)
+    meta = jnp.pad(meta, ((0, 0), (0, 0), (0, META - 3 * picks))).reshape(block, META).astype(jnp.bfloat16)
+    mine = jnp.concatenate([tokens.reshape(block, share), meta], axis=1)
+    came = {k: swap(mine, "expert", k) for k in (3, 2, 1)}
+    held = jnp.concatenate([mine, came[1], came[2], came[3]], axis=0)
+    own, meta = held[:, :share], held[:, share:]
+    core = swap(own, "tensor", 1)
+    across = swap(own, "tensor", 2)
+    place = jnp.stack([lax.axis_index("expert") * residents, lax.axis_index("tensor")]).astype(jnp.int32)
+    wg, wu, wd = w_gate.swapaxes(1, 2), w_up.swapaxes(1, 2), w_down
+    units, width, rows, total = wg.shape[1], wg.shape[2], holders * block, residents * slots
+    shape = jax.ShapeDtypeStruct
+    pick_mat, pick_back = shape((total, rows), jnp.bfloat16), shape((rows, total), jnp.bfloat16)
+    slot_weight, part = shape((total, 128), jnp.float32), shape((total, units), jnp.float32)
+    hidden, parts = shape((total, units), jnp.bfloat16), shape((2, rows, share), jnp.bfloat16)
+    taken = pltpu.VMEM((total, 2 * share), jnp.bfloat16)
+    blocks = pltpu.VMEM((residents, units, 2 * share), jnp.bfloat16)
+    sems = lambda n: pltpu.SemaphoreType.DMA((n, residents))
+    pick_mat, pick_back, slot_weight, gate, up = call(
+        functools.partial(half_kernel, slots),
+        (place, own, core, meta, wg, wu),
+        2,
+        (pick_mat, pick_back, slot_weight, part, part),
+        [taken, blocks, blocks, sems(2)],
+        9,
+    )
+    across_late, gate = lax.optimization_barrier((across, gate))
+    across_core = swap(across_late, "tensor", 1)
+    hidden, away_parts = call(
+        functools.partial(rest_kernel, slots),
+        (place, across, across_core, pick_mat, pick_back, slot_weight, gate, up, wg, wu, wd),
+        3,
+        (hidden, parts),
+        [taken, taken, blocks, blocks, blocks, sems(3)],
+        12,
+    )
+    wide = lambda a: a.astype(jnp.float32)
+    away = (wide(away_parts[0]) + wide(swap(away_parts[1], "tensor", 1))).astype(jnp.bfloat16)
+    away, hidden = lax.optimization_barrier((away, hidden))
+    back = swap(away, "tensor", 2)
+    home_parts = call(
+        functools.partial(down_kernel, slots), (place, hidden, pick_back, wd), 1, parts, [taken, blocks, sems(1)], 5
+    )
+    home_parts, back = lax.optimization_barrier((home_parts, back))
+    home = wide(home_parts[0]) + wide(swap(home_parts[1], "tensor", 1)) + wide(back)
+    home = home.reshape(holders, block, share)
+    sent = home.astype(jnp.bfloat16)
+    came = {k: swap(sent[k], "expert", k) for k in (3, 2, 1)}
+    result = home[0] + wide(came[1]) + wide(came[2]) + wide(came[3])
+    return result.reshape(steps, nrows, share).astype(jnp.bfloat16)
+
+
+def pick_plan(*arrays):
+    holders, splits = lax.axis_size("expert"), lax.axis_size("tensor")
+    residents = arrays[3].shape[0]
+    small = holders == 4 and splits == 4 and residents == 16
+    return (small_group if small else per_device)(*arrays)
+
+
 def solution(mesh):
     return jax.shard_map(
-        per_device,
+        pick_plan,
         mesh=mesh,
         in_specs=(
             P(None, ("replica", "expert"), "tensor"),

time: 604 us -> 67.1 us (0.11)
  local copies, waits for them, and re-layouts: 429 us -> 0.19 us
  waiting for transfers between devices: 86 us -> 17.5 us
  matrix products: 41.7 us -> 0 us
  Pallas kernels: 0 us -> 32 us
  blocking collectives: 26.3 us -> 0 us
  between operations: 13.5 us -> 0.11 us
  starting transfers between devices: 4.65 us -> 12.9 us
    unnamed x11 -> x1, local copies, waits for them, and re-layouts: 394 us -> 0.11 us
    dot_general x5 -> x0, matrix products: 41.7 us -> none  [the longest x1 14.3 us: expert_work(): jnp.einsum('bhecd,edf->bhecf', grouped, w_up, preferred_element_type=jnp....]
    unnamed x3 -> x0, waiting for transfers between devices: 38.1 us -> none
    pallas_call x0 -> x3, Pallas kernels: none -> 32 us  [call(): pl.pallas_call(kernel, in_specs=[pl.BlockSpec(memory_space=pltpu.SMEM)] +...]
    all_gather x1 -> x0, waiting for transfers between devices: 27.7 us -> none  [expert_work(): features = lax.all_gather(arrived_rows, 'tensor', axis=3, tiled=True)]
    all_to_all x1 -> x0, blocking collectives: 26.3 us -> none  [per_device(): lax.all_to_all(outgoing, 'expert', split_axis=1, concat_axis=1, tiled=True)]
    reduce_scatter x1 -> x0, local copies, waits for them, and re-layouts: 26.3 us -> none  [expert_work(): lax.psum_scatter(restored.astype(jnp.float32).astype(jnp.bfloat16), 'tens...]
    all_to_all x1 -> x0, waiting for transfers between devices: 20.1 us -> none  [expert_work(): lax.all_to_all(summed, 'expert', split_axis=1, concat_axis=1, tiled=True)]
  transfers between devices with their start and end apart: 3 -> 12, of which waited for: 3 -> 9; matrix products, arithmetic and copies ran while one was open for 0% -> 0% of each run, Pallas kernels for 0% -> 26%
where the time goes in v2:
time: 67.1 us; the launch traced here: 66.8 us
  Pallas kernels  32 us (48%)
  waiting for transfers between devices  17.5 us (26%)
  starting transfers between devices  12.9 us (19%)
  other arithmetic  4.04 us (6%)
    pallas_call x3, Pallas kernels, call(): pl.pallas_call(kernel, in_specs=[pl.BlockSpec(memory_space=pltpu.SMEM)] +...  32 us
    ppermute x12, waiting for transfers between devices, swap(): return lax.ppermute(a, axis, [(i, i ^ bits) for i in range(n)])  17.5 us
    ppermute x12, starting transfers between devices, swap(): return lax.ppermute(a, axis, [(i, i ^ bits) for i in range(n)])  12.9 us
    another operation x2, other arithmetic  1.39 us
  transfers between devices with their start and end apart: 12, of which 9 were waited for; matrix products, arithmetic and copies ran while one was open for 0% of the time, Pallas kernels for 26%

profile of v2, /device:TPU:0, one launch (start us, length us, event | category | flops | bytes accessed | tf_op | source)
XLA Modules:
  0.0 66.8 jit_solution(7485071742158223001)
XLA Ops:
  0.0 0.7 %convert_convert_fusion = bf16[2,32,6]{1,0,2:T(2,128)(2,1)S(1)} fusion(s32[2,32,6]{1,0,2:T(2,128)} %param.7), kind=kLoop, calls=%fused_computation.17 | loop fusion | flops 768 | bytes 2304 | tf_op jit(solution)/shard_map/convert.4
  0.7 0.7 %reduce-precision_convert_fusion = (bf16[2,32,6]{1,0,2:T(2,128)(2,1)S(1)}, bf16[2,32,6]{1,0,2:T(2,128)(2,1)S(1)}) fusion(f32[2,32,6]{1,0,2:T(2,128)} %param.8), kind=kLoop, calls=%fused_computation.15 | loop fusion | flops 1536 | bytes 3072 | tf_op jit(solution)/shard_map/convert.5
  1.4 0.1 copy.8
  1.5 0.8 %pad_maximum_fusion.1 = bf16[64,640]{1,0:T(8,128)(2,1)S(1)} fusion(bf16[64,128]{1,0:T(8,128)(2,1)S(1)} %bitcast.25, bf16[64,512]{1,0:T(8,128)(2,1)} %bitcast.22), kind=kLoop, calls=%fused_computation.11 | loop fusion | flops 163840 | bytes 163840 | tf_op jit(solution)/shard_map/concatenate | solution.py:235
  2.4 5.0 %collective-permute-start.2 = (bf16[64,640]{1,0:T(8,128)(2,1)S(1)}, bf16[64,640]{1,0:T(8,128)(2,1)S(1)}, u32[]{:S(2)}, u32[]{:S(2)}) collective-permute-start(bf16[64,640]{1,0:T(8,128)(2,1)S(1)} %pad_maximum_fusion.1), channel_id=1, source_target_pairs={{0,12},{4,8},{8,4},{12,0},{1,13},{5,9},{9,5},{13,1},{2,14},{6,10},... | collective-permute-start | bytes 245768 | tf_op jit(solution)/shard_map/ppermute | solution.py:222
  7.4 0.0 collective-permute-start.1
  7.4 0.6 collective-permute-start
  8.1 2.4 %collective-permute-done.2 = bf16[64,640]{1,0:T(8,128)(2,1)S(1)} collective-permute-done((bf16[64,640]{1,0:T(8,128)(2,1)S(1)}, bf16[64,640]{1,0:T(8,128)(2,1)S(1)}, u32[]{:S(2)}, u32[]{:S(2)}) %collective-permute-start.2) | collective-permute-done | bytes 81952 | tf_op jit(solution)/shard_map/ppermute | solution.py:222
  10.5 3.8 %collective-permute-done.1 = bf16[64,640]{1,0:T(8,128)(2,1)S(1)} collective-permute-done((bf16[64,640]{1,0:T(8,128)(2,1)S(1)}, bf16[64,640]{1,0:T(8,128)(2,1)S(1)}, u32[]{:S(2)}, u32[]{:S(2)}) %collective-permute-start.1) | collective-permute-done | bytes 81952 | tf_op jit(solution)/shard_map/ppermute | solution.py:222
  14.3 0.0 collective-permute-done
  14.3 0.9 %pad_maximum_fusion = bf16[256,640]{1,0:T(8,128)(2,1)S(1)} fusion(bf16[64,640]{1,0:T(8,128)(2,1)S(1)} %collective-permute-done.2, bf16[64,640]{1,0:T(8,128)(2,1)S(1)} %collective-permute-done.1, bf16[64,640]{1,0:T(8,128)(2,1)S(1)} %collective-permute-done, bf16[64,128]{1,0:T(8,128)(2,1)S(1)} %bitcast.26, bf16[64,512]{1,0:T(8,128)(2,1)} %bitcast.23), kind=kLoop, calls=%fused_computation.4 | loop fusion | flops 1638400 | bytes 655360 | tf_op jit(solution)/shard_map/concatenate | solution.py:237
  15.2 0.1 collective-permute-start.4
  15.3 0.1 pad_add_fusion.place
  15.4 1.5 %collective-permute-start.3 = (bf16[256,512]{1,0:T(8,128)(2,1)S(1)}, bf16[256,512]{1,0:T(8,128)(2,1)S(1)}, u32[]{:S(2)}, u32[]{:S(2)}) collective-permute-start(bf16[256,512]{1,0:T(8,128)(2,1)S(1)} %slice.44.near), channel_id=1, source_target_pairs={{0,2},{1,3},{2,0},{3,1},{4,6},{5,7},{6,4},{7,5},{8,10},{9,11},{10,... | collective-permute-start | bytes 786440 | tf_op jit(solution)/shard_map/ppermute | solution.py:222
  16.9 0.0 collective-permute-done.4.far
  16.9 10.8 %shard_map.64 = (bf16[768,256]{1,0:T(8,128)(2,1)S(1)}, bf16[256,768]{1,0:T(8,128)(2,1)S(1)}, f32[768,128]{1,0:T(8,128)S(1)}, f32[768,352]{1,0:T(8,128)S(1)}, f32[768,352]{1,0:T(8,128)S(1)}) custom-call(s32[2]{0:T(128)S(1)} %pad_add_fusion.place, bf16[256,512]{1,0:T(8,128)(2,1)S(1)} %slice.44.near, bf16[256,512]{1,0:T(8,128)(2,1)S(1)} %collective-permute-done.4.far, ...), custom_call_target="tpu_custom_call" | custom-call | flops 8999999488 | bytes 27000000 | tf_op jit(solution)/shard_map/pallas_call | solution.py:209
  27.7 0.0 collective-permute-done.3.near
  27.7 0.3 collective-permute-start.5
  28.0 1.3 %collective-permute-done.5.far = bf16[256,512]{1,0:T(8,128)(2,1)S(1)} collective-permute-done((bf16[256,512]{1,0:T(8,128)(2,1)S(1)}, bf16[256,512]{1,0:T(8,128)(2,1)S(1)}, u32[]{:S(2)}, u32[]{:S(2)}) %collective-permute-start.5) | collective-permute-done | bytes 262176 | tf_op jit(solution)/shard_map/ppermute | solution.py:222
  29.3 14.9 %shard_map.65 = (bf16[768,352]{1,0:T(8,128)(2,1)S(1)}, bf16[2,256,512]{2,1,0:T(8,128)(2,1)S(1)}) custom-call(s32[2]{0:T(128)S(1)} %pad_add_fusion.place, bf16[256,512]{1,0:T(8,128)(2,1)S(1)} %collective-permute-done.3.near, bf16[256,512]{1,0:T(8,128)(2,1)S(1)} %collective-permute-done.5.far, bf16[768,256]{1,0:T(8,128)(2,1)S(1)} %get-tuple-element.20.pick_mat, ...), custom_call_target="tpu_custom_call" | custom-call | flops 12000000000 | bytes 36000000 | tf_op jit(solution)/shard_map/pallas_call | solution.py:209
  44.2 0.3 collective-permute-start.6
  44.5 1.3 %collective-permute-done.6 = bf16[256,512]{1,0:T(8,128)(2,1)S(1)} collective-permute-done((bf16[256,512]{1,0:T(8,128)(2,1)S(1)}, bf16[256,512]{1,0:T(8,128)(2,1)S(1)}, u32[]{:S(2)}, u32[]{:S(2)}) %collective-permute-start.6) | collective-permute-done | bytes 262176 | tf_op jit(solution)/shard_map/ppermute | solution.py:222
  45.8 0.1 fusion.1
  45.9 1.5 %collective-permute-start.7 = (bf16[256,512]{1,0:T(8,128)(2,1)S(1)}, bf16[256,512]{1,0:T(8,128)(2,1)S(1)}, u32[]{:S(2)}, u32[]{:S(2)}) collective-permute-start(bf16[256,512]{1,0:T(8,128)(2,1)S(1)} %fusion.1), channel_id=1, source_target_pairs={{0,2},{1,3},{2,0},{3,1},{4,6},{5,7},{6,4},{7,5},{8,10},{9,11},{10,... | collective-permute-start | bytes 786440 | tf_op jit(solution)/shard_map/ppermute | solution.py:222
  47.4 6.3 %shard_map.66 = bf16[2,256,512]{2,1,0:T(8,128)(2,1)S(1)} custom-call(s32[2]{0:T(128)S(1)} %pad_add_fusion.place, bf16[768,352]{1,0:T(8,128)(2,1)S(1)} %get-tuple-element.27.hidden, bf16[256,768]{1,0:T(8,128)(2,1)S(1)} %get-tuple-element.21.pick_back, bf16[16,352,2048]{2,1,0:T(8,128)(2,1)} %wd.3), custom_call_target="tpu_custom_call" | custom-call | flops 5000000000 | bytes 15000000 | tf_op jit(solution)/shard_map/pallas_call | solution.py:209
  53.7 0.7 %collective-permute-done.7 = bf16[256,512]{1,0:T(8,128)(2,1)S(1)} collective-permute-done((bf16[256,512]{1,0:T(8,128)(2,1)S(1)}, bf16[256,512]{1,0:T(8,128)(2,1)S(1)}, u32[]{:S(2)}, u32[]{:S(2)}) %collective-permute-start.7) | collective-permute-done | bytes 262176 | tf_op jit(solution)/shard_map/ppermute | solution.py:222
  54.4 0.1 collective-permute-start.8
  54.5 1.5 %collective-permute-done.8 = bf16[256,512]{1,0:T(8,128)(2,1)S(1)} collective-permute-done((bf16[256,512]{1,0:T(8,128)(2,1)S(1)}, bf16[256,512]{1,0:T(8,128)(2,1)S(1)}, u32[]{:S(2)}, u32[]{:S(2)}) %collective-permute-start.8) | collective-permute-done | bytes 262176 | tf_op jit(solution)/shard_map/ppermute | solution.py:222
  56.0 0.1 fusion.6
  56.1 0.9 %collective-permute-start.9 = (bf16[64,512]{1,0:T(8,128)(2,1)S(1)}, bf16[64,512]{1,0:T(8,128)(2,1)S(1)}, u32[]{:S(2)}, u32[]{:S(2)}) collective-permute-start(bf16[64,512]{1,0:T(8,128)(2,1)S(1)} %get-tuple-element.33), channel_id=1, source_target_pairs={{0,4},{4,0},{8,12},{12,8},{1,5},{5,1},{9,13},{13,9},{2,6},{6,2},{1... | collective-permute-start | bytes 196616 | tf_op jit(solution)/shard_map/ppermute | solution.py:222
  57.1 1.9 %collective-permute-start.11 = (bf16[64,512]{1,0:T(8,128)(2,1)S(1)}, bf16[64,512]{1,0:T(8,128)(2,1)S(1)}, u32[]{:S(2)}, u32[]{:S(2)}) collective-permute-start(bf16[64,512]{1,0:T(8,128)(2,1)S(1)} %get-tuple-element.34), channel_id=1, source_target_pairs={{0,12},{4,8},{8,4},{12,0},{1,13},{5,9},{9,5},{13,1},{2,14},{6,10},... | collective-permute-start | bytes 196616 | tf_op jit(solution)/shard_map/ppermute | solution.py:222
  59.0 0.7 %collective-permute-start.10 = (bf16[64,512]{1,0:T(8,128)(2,1)S(1)}, bf16[64,512]{1,0:T(8,128)(2,1)S(1)}, u32[]{:S(2)}, u32[]{:S(2)}) collective-permute-start(bf16[64,512]{1,0:T(8,128)(2,1)S(1)} %get-tuple-element.35), channel_id=1, source_target_pairs={{0,8},{4,12},{8,0},{12,4},{1,9},{5,13},{9,1},{13,5},{2,10},{6,14},... | collective-permute-start | bytes 196616 | tf_op jit(solution)/shard_map/ppermute | solution.py:222
  59.7 0.8 %collective-permute-done.9 = bf16[64,512]{1,0:T(8,128)(2,1)S(1)} collective-permute-done((bf16[64,512]{1,0:T(8,128)(2,1)S(1)}, bf16[64,512]{1,0:T(8,128)(2,1)S(1)}, u32[]{:S(2)}, u32[]{:S(2)}) %collective-permute-start.9) | collective-permute-done | bytes 65568 | tf_op jit(solution)/shard_map/ppermute | solution.py:222
  60.5 3.3 %collective-permute-done.11 = bf16[64,512]{1,0:T(8,128)(2,1)S(1)} collective-permute-done((bf16[64,512]{1,0:T(8,128)(2,1)S(1)}, bf16[64,512]{1,0:T(8,128)(2,1)S(1)}, u32[]{:S(2)}, u32[]{:S(2)}) %collective-permute-start.11) | collective-permute-done | bytes 65568 | tf_op jit(solution)/shard_map/ppermute | solution.py:222
  63.8 2.4 %collective-permute-done.10 = bf16[64,512]{1,0:T(8,128)(2,1)S(1)} collective-permute-done((bf16[64,512]{1,0:T(8,128)(2,1)S(1)}, bf16[64,512]{1,0:T(8,128)(2,1)S(1)}, u32[]{:S(2)}, u32[]{:S(2)}) %collective-permute-start.10) | collective-permute-done | bytes 65568 | tf_op jit(solution)/shard_map/ppermute | solution.py:222
  66.1 0.7 fusion.4
  (7 shorter events, 0.1 us)
Async XLA Ops:
  2.4 8.1 %collective-permute-start.2 = (bf16[64,640]{1,0:T(8,128)(2,1)S(1)}, bf16[64,640]{1,0:T(8,128)(2,1)S(1)}, u32[]{:S(2)}, u32[]{:S(2)}) collective-permute-start(bf16[64,640]{1,0:T(8,128)(2,1)S(1)} %pad_maximum_fusion.1), channel_id=1, source_target_pairs={{0,12},{4,8},{8,4},{12,0},{1,13},{5,9},{9,5},{13,1},{2,14},{6,10},... | collective-permute-start | bytes 245768 | tf_op jit(solution)/shard_map/ppermute | solution.py:222
  7.4 6.9 %collective-permute-start.1 = (bf16[64,640]{1,0:T(8,128)(2,1)S(1)}, bf16[64,640]{1,0:T(8,128)(2,1)S(1)}, u32[]{:S(2)}, u32[]{:S(2)}) collective-permute-start(bf16[64,640]{1,0:T(8,128)(2,1)S(1)} %pad_maximum_fusion.1), channel_id=1, source_target_pairs={{0,8},{4,12},{8,0},{12,4},{1,9},{5,13},{9,1},{13,5},{2,10},{6,14},... | collective-permute-start | bytes 245768 | tf_op jit(solution)/shard_map/ppermute | solution.py:222
  7.4 6.9 %collective-permute-start = (bf16[64,640]{1,0:T(8,128)(2,1)S(1)}, bf16[64,640]{1,0:T(8,128)(2,1)S(1)}, u32[]{:S(2)}, u32[]{:S(2)}) collective-permute-start(bf16[64,640]{1,0:T(8,128)(2,1)S(1)} %pad_maximum_fusion.1), channel_id=1, source_target_pairs={{0,4},{4,0},{8,12},{12,8},{1,5},{5,1},{9,13},{13,9},{2,6},{6,2},{1... | collective-permute-start | bytes 245768 | tf_op jit(solution)/shard_map/ppermute | solution.py:222
  15.2 1.7 %collective-permute-start.4 = (bf16[256,512]{1,0:T(8,128)(2,1)S(1)}, bf16[256,512]{1,0:T(8,128)(2,1)S(1)}, u32[]{:S(2)}, u32[]{:S(2)}) collective-permute-start(bf16[256,512]{1,0:T(8,128)(2,1)S(1)} %slice.44.near), channel_id=1, source_target_pairs={{0,1},{1,0},{2,3},{3,2},{4,5},{5,4},{6,7},{7,6},{8,9},{9,8},{10,11... | collective-permute-start | bytes 786440 | tf_op jit(solution)/shard_map/ppermute | solution.py:222
  15.4 12.3 %collective-permute-start.3 = (bf16[256,512]{1,0:T(8,128)(2,1)S(1)}, bf16[256,512]{1,0:T(8,128)(2,1)S(1)}, u32[]{:S(2)}, u32[]{:S(2)}) collective-permute-start(bf16[256,512]{1,0:T(8,128)(2,1)S(1)} %slice.44.near), channel_id=1, source_target_pairs={{0,2},{1,3},{2,0},{3,1},{4,6},{5,7},{6,4},{7,5},{8,10},{9,11},{10,... | collective-permute-start | bytes 786440 | tf_op jit(solution)/shard_map/ppermute | solution.py:222
  27.7 1.6 %collective-permute-start.5 = (bf16[256,512]{1,0:T(8,128)(2,1)S(1)}, bf16[256,512]{1,0:T(8,128)(2,1)S(1)}, u32[]{:S(2)}, u32[]{:S(2)}) collective-permute-start(bf16[256,512]{1,0:T(8,128)(2,1)S(1)} %collective-permute-done.3.near), channel_id=1, source_target_pairs={{0,1},{1,0},{2,3},{3,2},{4,5},{5,4},{6,7},{7,6},{8,9},{9,8},{10,11... | collective-permute-start | bytes 786440 | tf_op jit(solution)/shard_map/ppermute | solution.py:222
  44.2 1.6 %collective-permute-start.6 = (bf16[256,512]{1,0:T(8,128)(2,1)S(1)}, bf16[256,512]{1,0:T(8,128)(2,1)S(1)}, u32[]{:S(2)}, u32[]{:S(2)}) collective-permute-start(bf16[256,512]{1,0:T(8,128)(2,1)S(1)} %slice_bitcast_fusion.1), channel_id=1, source_target_pairs={{0,1},{1,0},{2,3},{3,2},{4,5},{5,4},{6,7},{7,6},{8,9},{9,8},{10,11... | collective-permute-start | bytes 786440 | tf_op jit(solution)/shard_map/ppermute | solution.py:222
  45.9 8.5 %collective-permute-start.7 = (bf16[256,512]{1,0:T(8,128)(2,1)S(1)}, bf16[256,512]{1,0:T(8,128)(2,1)S(1)}, u32[]{:S(2)}, u32[]{:S(2)}) collective-permute-start(bf16[256,512]{1,0:T(8,128)(2,1)S(1)} %fusion.1), channel_id=1, source_target_pairs={{0,2},{1,3},{2,0},{3,1},{4,6},{5,7},{6,4},{7,5},{8,10},{9,11},{10,... | collective-permute-start | bytes 786440 | tf_op jit(solution)/shard_map/ppermute | solution.py:222
  54.4 1.6 %collective-permute-start.8 = (bf16[256,512]{1,0:T(8,128)(2,1)S(1)}, bf16[256,512]{1,0:T(8,128)(2,1)S(1)}, u32[]{:S(2)}, u32[]{:S(2)}) collective-permute-start(bf16[256,512]{1,0:T(8,128)(2,1)S(1)} %slice_bitcast_fusion), channel_id=1, source_target_pairs={{0,1},{1,0},{2,3},{3,2},{4,5},{5,4},{6,7},{7,6},{8,9},{9,8},{10,11... | collective-permute-start | bytes 786440 | tf_op jit(solution)/shard_map/ppermute | solution.py:222
  56.1 4.3 %collective-permute-start.9 = (bf16[64,512]{1,0:T(8,128)(2,1)S(1)}, bf16[64,512]{1,0:T(8,128)(2,1)S(1)}, u32[]{:S(2)}, u32[]{:S(2)}) collective-permute-start(bf16[64,512]{1,0:T(8,128)(2,1)S(1)} %get-tuple-element.33), channel_id=1, source_target_pairs={{0,4},{4,0},{8,12},{12,8},{1,5},{5,1},{9,13},{13,9},{2,6},{6,2},{1... | collective-permute-start | bytes 196616 | tf_op jit(solution)/shard_map/ppermute | solution.py:222
  57.1 6.7 %collective-permute-start.11 = (bf16[64,512]{1,0:T(8,128)(2,1)S(1)}, bf16[64,512]{1,0:T(8,128)(2,1)S(1)}, u32[]{:S(2)}, u32[]{:S(2)}) collective-permute-start(bf16[64,512]{1,0:T(8,128)(2,1)S(1)} %get-tuple-element.34), channel_id=1, source_target_pairs={{0,12},{4,8},{8,4},{12,0},{1,13},{5,9},{9,5},{13,1},{2,14},{6,10},... | collective-permute-start | bytes 196616 | tf_op jit(solution)/shard_map/ppermute | solution.py:222
  59.0 7.2 %collective-permute-start.10 = (bf16[64,512]{1,0:T(8,128)(2,1)S(1)}, bf16[64,512]{1,0:T(8,128)(2,1)S(1)}, u32[]{:S(2)}, u32[]{:S(2)}) collective-permute-start(bf16[64,512]{1,0:T(8,128)(2,1)S(1)} %get-tuple-element.35), channel_id=1, source_target_pairs={{0,8},{4,12},{8,0},{12,4},{1,9},{5,13},{9,1},{13,5},{2,10},{6,14},... | collective-permute-start | bytes 196616 | tf_op jit(solution)/shard_map/ppermute | solution.py:222

commit v3 on v2

--- a/solution.py
+++ b/solution.py
@@ -80,24 +80,65 @@
 NT = (((1,), (1,)), ((), ()))
 NN = (((1,), (0,)), ((), ()))
 TN = (((0,), (0,)), ((), ()))
-META = 128
+TILE = 16
 TOPK = 6
-GROUP = 2
+GROUP = 4
 
 
 def dot(a, b, dims):
     return lax.dot_general(a, b, dims, preferred_element_type=jnp.float32)
 
 
-def route(place, meta, picks, slots, residents, pick_mat, slot_weight):
-    rows = meta.shape[0]
-    by_pick = meta.astype(jnp.float32).T
+def pack_kernel(tokens, ids_there, weights_there, out, table, ids, weights, sems):
+    nrows = tokens.shape[0]
+    copies = [
+        pltpu.make_async_copy(ids_there, ids, sems.at[0]),
+        pltpu.make_async_copy(weights_there, weights, sems.at[1]),
+        pltpu.make_async_copy(tokens, out.at[:nrows], sems.at[2]),
+    ]
+    for copy in copies:
+        copy.start()
+    table[...] = jnp.zeros_like(table)
+    for copy in copies[:2]:
+        copy.wait()
+    picks, steps, step_rows = ids.shape
+    for s in range(steps):
+        high = weights[:, s, :].astype(jnp.bfloat16).astype(jnp.float32)
+        low = weights[:, s, :] - high
+        for c, part in enumerate((ids[:, s, :].astype(jnp.float32), high, low)):
+            table[:picks, c * 128 + s * step_rows : c * 128 + (s + 1) * step_rows] = part
+    out[nrows:, :] = table[...].astype(jnp.bfloat16)
+    copies[2].wait()
+
+
+def early_kernel(place, packed, wd, down, sems):
+    width = down.shape[2]
+    column = pl.multiple_of(((place[1] >> 1) ^ 1) * width, width)
+    fetch_all((wd,), (down,), sems, column)
+    for e in range(down.shape[0]):
+        for copy in fetch((wd,), (down,), sems, column, e):
+            copy.wait()
+
+
+def join_kernel(first, second, third, fourth, out):
+    block = out.shape[0] // 4
+    for j, piece in enumerate((first, second, third, fourth)):
+        out[j * block : (j + 1) * block, :] = piece[:block, :]
+
+
+def route(place, pieces, picks, slots, residents, table, pick_mat, slot_weight):
+    block = pieces[0].shape[0] - TILE
+    rows = block * len(pieces)
+    for j, piece in enumerate(pieces):
+        for c in range(3):
+            part = piece[block:, c * 128 : c * 128 + block].astype(jnp.float32)
+            table[c * TILE : (c + 1) * TILE, j * block : (j + 1) * block] = part
     labels = (place[0] + lax.broadcasted_iota(jnp.int32, (residents, rows), 0)).astype(jnp.float32)
     chosen = jnp.zeros((residents, rows), jnp.float32)
     weight = jnp.zeros((residents, rows), jnp.float32)
     for k in range(picks):
-        hit = by_pick[k : k + 1, :] == labels
-        share = by_pick[picks + k : picks + k + 1, :] + by_pick[2 * picks + k : 2 * picks + k + 1, :]
+        hit = table[k : k + 1, :] == labels
+        share = table[TILE + k : TILE + k + 1, :] + table[2 * TILE + k : 2 * TILE + k + 1, :]
         chosen = jnp.where(hit, 1.0, chosen)
         weight = jnp.where(hit, share, weight)
     before = lax.broadcasted_iota(jnp.int32, (rows, rows), 0) < lax.broadcasted_iota(jnp.int32, (rows, rows), 1)
@@ -141,52 +182,64 @@
         out[j] = dot(pick_back[...], block, NN).astype(jnp.bfloat16)
 
 
-def over_experts(residents, slots, work):
+def over_experts(residents, slots, arrive, work):
     def some(step, carry):
-        for g in range(GROUP):
-            e = step * GROUP + g
-            work(e, pl.ds(pl.multiple_of(e * slots, slots), slots))
+        group = [step * GROUP + g for g in range(GROUP)]
+        for e in group:
+            arrive(e)
+        work(group, [pl.ds(pl.multiple_of(e * slots, slots), slots) for e in group])
         return carry
 
     lax.fori_loop(0, residents // GROUP, some, 0)
 
 
-def half_kernel(slots, place, near, far, meta, wg, wu, *rest):
-    pick_mat, pick_back, slot_weight, gate, up, taken, bg, bu, sems = rest
-    column = pl.multiple_of((place[1] >> 1) * bg.shape[2], bg.shape[2])
+def half_kernel(slots, place, near, far, one, two, three, four, wg, wu, *rest):
+    pick_mat, pick_back, slot_weight, gate, up, taken, table, bg, bu, sems = rest
+    width = bg.shape[2]
+    column = pl.multiple_of((place[1] >> 1) * width, width)
+    residents = bg.shape[0]
     fetch_all((wg, wu), (bg, bu), sems, column)
-    route(place, meta[...], TOPK, slots, pick_mat.shape[0] // slots, pick_mat, slot_weight)
+    route(place, (one, two, three, four), TOPK, slots, residents, table, pick_mat, slot_weight)
     place_rows(place, pick_mat, near, far, taken)
     pick_back[...] = pick_mat[...].T
 
-    def work(e, mine):
+    def arrive(e):
         for copy in fetch((wg, wu), (bg, bu), sems, column, e):
             copy.wait()
-        x = taken[mine, :]
-        gate[mine, :] = dot(x, bg[e], NT)
-        up[mine, :] = dot(x, bu[e], NT)
-
-    over_experts(bg.shape[0], slots, work)
-
-
-def rest_kernel(slots, place, near, far, pick_mat, pick_back, slot_weight, gate, up, wg, wu, wd, *rest):
-    hidden, out, taken, given, bg, bu, bd, sems = rest
+
+    def work(group, places):
+        for e, mine in zip(group, places):
+            x = taken[mine, :]
+            gate[mine, :] = dot(x, bg[e], NT)
+            up[mine, :] = dot(x, bu[e], NT)
+
+    over_experts(residents, slots, arrive, work)
+
+
+def rest_kernel(slots, place, near, far, pick_mat, pick_back, slot_weight, gate, up, down, wg, wu, *rest):
+    hidden, out, taken, given, bg, bu, sems = rest
     column = pl.multiple_of(((place[1] >> 1) ^ 1) * bg.shape[2], bg.shape[2])
-    fetch_all((wg, wu, wd), (bg, bu, bd), sems, column)
+    fetch_all((wg, wu), (bg, bu), sems, column)
     place_rows(place, pick_mat, near, far, taken)
 
-    def work(e, mine):
-        for copy in fetch((wg, wu, wd), (bg, bu, bd), sems, column, e):
+    def arrive(e):
+        for copy in fetch((wg, wu), (bg, bu), sems, column, e):
             copy.wait()
-        x = taken[mine, :]
-        gate_val = gate[mine, :] + dot(x, bg[e], NT)
-        up_val = up[mine, :] + dot(x, bu[e], NT)
-        scaled = gate_val * jax.nn.sigmoid(gate_val) * up_val * slot_weight[mine, :1]
-        scaled = scaled.astype(jnp.bfloat16)
-        hidden[mine, :] = scaled
-        given[mine, :] = dot(scaled, bd[e], NN).astype(jnp.bfloat16)
-
-    over_experts(bg.shape[0], slots, work)
+
+    def work(group, places):
+        ready = []
+        for e, mine in zip(group, places):
+            x = taken[mine, :]
+            gate_val = gate[mine, :] + dot(x, bg[e], NT)
+            up_val = up[mine, :] + dot(x, bu[e], NT)
+            scaled = gate_val * jax.nn.sigmoid(gate_val) * up_val * slot_weight[mine, :1]
+            scaled = scaled.astype(jnp.bfloat16)
+            hidden[mine, :] = scaled
+            ready.append(scaled)
+        for e, mine, scaled in zip(group, places, ready):
+            given[mine, :] = dot(scaled, down[e], NN).astype(jnp.bfloat16)
+
+    over_experts(bg.shape[0], slots, arrive, work)
     add_up(place, pick_back, given, out)
 
 
@@ -194,25 +247,28 @@
     column = pl.multiple_of((place[1] >> 1) * bd.shape[2], bd.shape[2])
     fetch_all((wd,), (bd,), sems, column)
 
-    def work(e, mine):
+    def arrive(e):
         for copy in fetch((wd,), (bd,), sems, column, e):
             copy.wait()
-        given[mine, :] = dot(hidden[mine, :], bd[e], NN).astype(jnp.bfloat16)
-
-    over_experts(bd.shape[0], slots, work)
+
+    def work(group, places):
+        for e, mine in zip(group, places):
+            given[mine, :] = dot(hidden[mine, :], bd[e], NN).astype(jnp.bfloat16)
+
+    over_experts(bd.shape[0], slots, arrive, work)
     add_up(place, pick_back, given, out)
 
 
-def call(kernel, args, fetched, outs, scratch, micros):
+def call(kernel, args, fetched, outs, scratch, micros, room):
     vmem, there = pl.BlockSpec(memory_space=pltpu.VMEM), pl.BlockSpec(memory_space=pl.ANY)
-    local = len(args) - fetched - 1
+    specs = [vmem if a.ndim > 1 else pl.BlockSpec(memory_space=pltpu.SMEM) for a in args[: len(args) - fetched]]
     return pl.pallas_call(
         kernel,
-        in_specs=[pl.BlockSpec(memory_space=pltpu.SMEM)] + [vmem] * local + [there] * fetched,
+        in_specs=specs + [there] * fetched,
         out_specs=jax.tree.map(lambda _: vmem, outs),
         out_shape=outs,
         scratch_shapes=scratch,
-        compiler_params=pltpu.CompilerParams(vmem_limit_bytes=48 << 20),
+        compiler_params=pltpu.CompilerParams(vmem_limit_bytes=room << 20),
         cost_estimate=pl.CostEstimate(flops=micros * 10**9, bytes_accessed=micros * 3 * 10**6, transcendentals=0),
     )(*args)
 
@@ -229,49 +285,65 @@
     residents = w_gate.shape[0]
     block = steps * nrows
     slots = steps * holders * CAP
-    high = lax.reduce_precision(route_weights, 8, 7)
-    meta = jnp.concatenate([expert_ids.astype(jnp.float32), high, route_weights - high], axis=2)
-    meta = jnp.pad(meta, ((0, 0), (0, 0), (0, META - 3 * picks))).reshape(block, META).astype(jnp.bfloat16)
-    mine = jnp.concatenate([tokens.reshape(block, share), meta], axis=1)
+    place = jnp.stack([lax.axis_index("expert") * residents, lax.axis_index("tensor")]).astype(jnp.int32)
+    there = lambda a: pltpu.with_memory_space_constraint(a, pltpu.HBM)
+    wg, wu, wd = there(w_gate.swapaxes(1, 2)), there(w_up.swapaxes(1, 2)), there(w_down)
+    units, rows, total = wg.shape[1], holders * block, residents * slots
+    shape = jax.ShapeDtypeStruct
+    sources = (tokens.reshape(block, share), expert_ids.transpose(2, 0, 1), route_weights.transpose(2, 0, 1))
+    mine = call(
+        pack_kernel,
+        tuple(there(a) for a in sources),
+        3,
+        shape((block + TILE, share), jnp.bfloat16),
+        [
+            pltpu.VMEM((TILE, share), jnp.float32),
+            pltpu.VMEM((picks, steps, nrows), jnp.int32),
+            pltpu.VMEM((picks, steps, nrows), jnp.float32),
+            pltpu.SemaphoreType.DMA((3,)),
+        ],
+        1,
+        2,
+    )
+    sems = lambda n: pltpu.SemaphoreType.DMA((n, residents))
+    down = shape((residents, units, 2 * share), jnp.bfloat16)
+    down = call(early_kernel, (place, mine, wd), 1, down, [sems(1)], 5, 2)
     came = {k: swap(mine, "expert", k) for k in (3, 2, 1)}
-    held = jnp.concatenate([mine, came[1], came[2], came[3]], axis=0)
-    own, meta = held[:, :share], held[:, share:]
+    pieces, down = lax.optimization_barrier(((mine, came[1], came[2], came[3]), down))
+    own = call(join_kernel, pieces, 0, shape((rows, share), jnp.bfloat16), [], 1, 2)
     core = swap(own, "tensor", 1)
     across = swap(own, "tensor", 2)
-    place = jnp.stack([lax.axis_index("expert") * residents, lax.axis_index("tensor")]).astype(jnp.int32)
-    wg, wu, wd = w_gate.swapaxes(1, 2), w_up.swapaxes(1, 2), w_down
-    units, width, rows, total = wg.shape[1], wg.shape[2], holders * block, residents * slots
-    shape = jax.ShapeDtypeStruct
     pick_mat, pick_back = shape((total, rows), jnp.bfloat16), shape((rows, total), jnp.bfloat16)
     slot_weight, part = shape((total, 128), jnp.float32), shape((total, units), jnp.float32)
     hidden, parts = shape((total, units), jnp.bfloat16), shape((2, rows, share), jnp.bfloat16)
     taken = pltpu.VMEM((total, 2 * share), jnp.bfloat16)
-    blocks = pltpu.VMEM((residents, units, 2 * share), jnp.bfloat16)
-    sems = lambda n: pltpu.SemaphoreType.DMA((n, residents))
+    blocks = pltpu.VMEM(down.shape, jnp.bfloat16)
     pick_mat, pick_back, slot_weight, gate, up = call(
         functools.partial(half_kernel, slots),
-        (place, own, core, meta, wg, wu),
+        (place, own, core) + pieces + (wg, wu),
         2,
         (pick_mat, pick_back, slot_weight, part, part),
-        [taken, blocks, blocks, sems(2)],
+        [taken, pltpu.VMEM((3 * TILE, rows), jnp.float32), blocks, blocks, sems(2)],
         9,
+        30,
     )
     across_late, gate = lax.optimization_barrier((across, gate))
     across_core = swap(across_late, "tensor", 1)
     hidden, away_parts = call(
         functools.partial(rest_kernel, slots),
-        (place, across, across_core, pick_mat, pick_back, slot_weight, gate, up, wg, wu, wd),
-        3,
+        (place, across, across_core, pick_mat, pick_back, slot_weight, gate, up, down, wg, wu),
+        2,
         (hidden, parts),
-        [taken, taken, blocks, blocks, blocks, sems(3)],
+        [taken, taken, blocks, blocks, sems(2)],
         12,
+        32,
     )
     wide = lambda a: a.astype(jnp.float32)
     away = (wide(away_parts[0]) + wide(swap(away_parts[1], "tensor", 1))).astype(jnp.bfloat16)
     away, hidden = lax.optimization_barrier((away, hidden))
     back = swap(away, "tensor", 2)
     home_parts = call(
-        functools.partial(down_kernel, slots), (place, hidden, pick_back, wd), 1, parts, [taken, blocks, sems(1)], 5
+        functools.partial(down_kernel, slots), (place, hidden, pick_back, wd), 1, parts, [taken, blocks, sems(1)], 5, 44
     )
     home_parts, back = lax.optimization_barrier((home_parts, back))
     home = wide(home_parts[0]) + wide(swap(home_parts[1], "tensor", 1)) + wide(back)

time: 67.1 us -> 62.9 us (0.937)
  waiting for transfers between devices: 17.5 us -> 12.7 us
  Pallas kernels: 32 us -> 35.9 us
  other arithmetic: 4.04 us -> 0.91 us
    ppermute x12, waiting for transfers between devices: 17.5 us -> 12.7 us  [swap(): return lax.ppermute(a, axis, [(i, i ^ bits) for i in range(n)])]
    pallas_call x3 -> x6, Pallas kernels: 32 us -> 35.9 us  [call(): pl.pallas_call(kernel, in_specs=specs + [there] * fetched, out_specs=jax....]
    concatenate x3 -> x0, other arithmetic: 1.74 us -> none  [the longest x1 0.87 us: small_group(): held = jnp.concatenate([mine, came[1], came[2], came[3]], axis=0)]
    another operation x2 -> x0, other arithmetic: 1.39 us -> none
  transfers between devices with their start and end apart: 12 -> 12, of which waited for: 9 -> 8; matrix products, arithmetic and copies ran while one was open for 0% -> 0% of each run, Pallas kernels for 26% -> 35%
where the time goes in v3:
time: 62.9 us; the launch traced here: 62.7 us
  Pallas kernels  35.9 us (57%)
  starting transfers between devices  13 us (21%)
  waiting for transfers between devices  12.7 us (20%)
  other arithmetic  0.91 us (1%)
    pallas_call x6, Pallas kernels, call(): pl.pallas_call(kernel, in_specs=specs + [there] * fetched, out_specs=jax....  35.9 us
    ppermute x12, starting transfers between devices, swap(): return lax.ppermute(a, axis, [(i, i ^ bits) for i in range(n)])  13 us
    ppermute x12, waiting for transfers between devices, swap(): return lax.ppermute(a, axis, [(i, i ^ bits) for i in range(n)])  12.7 us
  transfers between devices with their start and end apart: 12, of which 8 were waited for; matrix products, arithmetic and copies ran while one was open for 0% of the time, Pallas kernels for 35%

profile of v3, /device:TPU:0, one launch (start us, length us, event | category | flops | bytes accessed | tf_op | source)
XLA Modules:
  0.0 62.7 jit_solution(7367156333412195568)
XLA Ops:
  0.0 0.9 %shard_map.64.packed.first.one = bf16[80,512]{1,0:T(8,128)(2,1)S(1)} custom-call(bf16[64,512]{1,0:T(8,128)(2,1)} %bitcast.23, s32[6,2,32]{2,1,0:T(2,128)} %bitcast.24, f32[6,2,32]{2,1,0:T(2,128)} %bitcast.25), custom_call_target="tpu_custom_call" | custom-call | flops 1000000000 | bytes 3000000 | tf_op jit(solution)/shard_map/pallas_call | solution.py:265
  0.9 5.1 %collective-permute-start.2 = (bf16[80,512]{1,0:T(8,128)(2,1)S(1)}, bf16[80,512]{1,0:T(8,128)(2,1)S(1)}, u32[]{:S(2)}, u32[]{:S(2)}) collective-permute-start(bf16[80,512]{1,0:T(8,128)(2,1)S(1)} %shard_map.64.packed.first.one), channel_id=1, source_target_pairs={{0,12},{4,8},{8,4},{12,0},{1,13},{5,9},{9,5},{13,1},{2,14},{6,10},... | collective-permute-start | bytes 245768 | tf_op jit(solution)/shard_map/ppermute | solution.py:278
  6.0 0.0 collective-permute-start.1
  6.0 0.6 %collective-permute-start = (bf16[80,512]{1,0:T(8,128)(2,1)S(1)}, bf16[80,512]{1,0:T(8,128)(2,1)S(1)}, u32[]{:S(2)}, u32[]{:S(2)}) collective-permute-start(bf16[80,512]{1,0:T(8,128)(2,1)S(1)} %shard_map.64.packed.first.one), channel_id=1, source_target_pairs={{0,4},{4,0},{8,12},{12,8},{1,5},{5,1},{9,13},{13,9},{2,6},{6,2},{1... | collective-permute-start | bytes 245768 | tf_op jit(solution)/shard_map/ppermute | solution.py:278
  6.7 0.1 pad_add_fusion.place
  6.7 5.0 %shard_map.65.down = bf16[16,352,1024]{2,1,0:T(8,128)(2,1)S(1)} custom-call(s32[2]{0:T(128)S(1)} %pad_add_fusion.place, bf16[80,512]{1,0:T(8,128)(2,1)S(1)} %shard_map.64.packed.first.one, bf16[16,352,2048]{2,1,0:T(8,128)(2,1)} %wd.3), custom_call_target="tpu_custom_call" | custom-call | flops 5000000000 | bytes 15000000 | tf_op jit(solution)/shard_map/pallas_call | solution.py:265
  11.7 0.0 collective-permute-done.2.fourth.four
  11.7 1.2 %collective-permute-done.1.third.three = bf16[80,512]{1,0:T(8,128)(2,1)S(1)} collective-permute-done((bf16[80,512]{1,0:T(8,128)(2,1)S(1)}, bf16[80,512]{1,0:T(8,128)(2,1)S(1)}, u32[]{:S(2)}, u32[]{:S(2)}) %collective-permute-start.1) | collective-permute-done | bytes 81952 | tf_op jit(solution)/shard_map/ppermute | solution.py:278
  12.9 0.0 collective-permute-done.second.two
  12.9 0.1 collective-permute-start.4
  13.0 1.6 %collective-permute-start.3 = (bf16[256,512]{1,0:T(8,128)(2,1)S(1)}, bf16[256,512]{1,0:T(8,128)(2,1)S(1)}, u32[]{:S(2)}, u32[]{:S(2)}) collective-permute-start(bf16[256,512]{1,0:T(8,128)(2,1)S(1)} %shard_map.66.near), channel_id=1, source_target_pairs={{0,2},{1,3},{2,0},{3,1},{4,6},{5,7},{6,4},{7,5},{8,10},{9,11},{10,... | collective-permute-start | bytes 786440 | tf_op jit(solution)/shard_map/ppermute | solution.py:278
  14.5 0.0 collective-permute-done.4.far
  14.5 10.8 %shard_map.67 = (bf16[768,256]{1,0:T(8,128)(2,1)S(1)}, bf16[256,768]{1,0:T(8,128)(2,1)S(1)}, f32[768,128]{1,0:T(8,128)S(1)}, f32[768,352]{1,0:T(8,128)S(1)}, f32[768,352]{1,0:T(8,128)S(1)}) custom-call(s32[2]{0:T(128)S(1)} %pad_add_fusion.place, bf16[256,512]{1,0:T(8,128)(2,1)S(1)} %shard_map.66.near, bf16[256,512]{1,0:T(8,128)(2,1)S(1)} %collective-permute-done.4.far, ...), custom_call_target="tpu_custom_call" | custom-call | flops 8999999488 | bytes 27000000 | tf_op jit(solution)/shard_map/pallas_call | solution.py:265
  25.4 0.0 collective-permute-done.3.near
  25.4 0.2 collective-permute-start.5
  25.6 1.4 %collective-permute-done.5.far = bf16[256,512]{1,0:T(8,128)(2,1)S(1)} collective-permute-done((bf16[256,512]{1,0:T(8,128)(2,1)S(1)}, bf16[256,512]{1,0:T(8,128)(2,1)S(1)}, u32[]{:S(2)}, u32[]{:S(2)}) %collective-permute-start.5) | collective-permute-done | bytes 262176 | tf_op jit(solution)/shard_map/ppermute | solution.py:278
  27.0 13.1 %shard_map.68 = (bf16[768,352]{1,0:T(8,128)(2,1)S(1)}, bf16[2,256,512]{2,1,0:T(8,128)(2,1)S(1)}) custom-call(s32[2]{0:T(128)S(1)} %pad_add_fusion.place, bf16[256,512]{1,0:T(8,128)(2,1)S(1)} %collective-permute-done.3.near, bf16[256,512]{1,0:T(8,128)(2,1)S(1)} %collective-permute-done.5.far, bf16[768,256]{1,0:T(8,128)(2,1)S(1)} %get-tuple-element.29.pick_mat, ...), custom_call_target="tpu_custom_call" | custom-call | flops 12000000000 | bytes 36000000 | tf_op jit(solution)/shard_map/pallas_call | solution.py:265
  40.1 0.2 collective-permute-start.6
  40.4 1.4 %collective-permute-done.6 = bf16[256,512]{1,0:T(8,128)(2,1)S(1)} collective-permute-done((bf16[256,512]{1,0:T(8,128)(2,1)S(1)}, bf16[256,512]{1,0:T(8,128)(2,1)S(1)}, u32[]{:S(2)}, u32[]{:S(2)}) %collective-permute-start.6) | collective-permute-done | bytes 262176 | tf_op jit(solution)/shard_map/ppermute | solution.py:278
  41.7 0.1 fusion.1
  41.8 1.5 %collective-permute-start.7 = (bf16[256,512]{1,0:T(8,128)(2,1)S(1)}, bf16[256,512]{1,0:T(8,128)(2,1)S(1)}, u32[]{:S(2)}, u32[]{:S(2)}) collective-permute-start(bf16[256,512]{1,0:T(8,128)(2,1)S(1)} %fusion.1), channel_id=1, source_target_pairs={{0,2},{1,3},{2,0},{3,1},{4,6},{5,7},{6,4},{7,5},{8,10},{9,11},{10,... | collective-permute-start | bytes 786440 | tf_op jit(solution)/shard_map/ppermute | solution.py:278
  43.3 6.1 %shard_map.69 = bf16[2,256,512]{2,1,0:T(8,128)(2,1)S(1)} custom-call(s32[2]{0:T(128)S(1)} %pad_add_fusion.place, bf16[768,352]{1,0:T(8,128)(2,1)S(1)} %get-tuple-element.37.hidden, bf16[256,768]{1,0:T(8,128)(2,1)S(1)} %get-tuple-element.30.pick_back, bf16[16,352,2048]{2,1,0:T(8,128)(2,1)} %wd.3), custom_call_target="tpu_custom_call" | custom-call | flops 5000000000 | bytes 15000000 | tf_op jit(solution)/shard_map/pallas_call | solution.py:265
  49.5 0.8 %collective-permute-done.7 = bf16[256,512]{1,0:T(8,128)(2,1)S(1)} collective-permute-done((bf16[256,512]{1,0:T(8,128)(2,1)S(1)}, bf16[256,512]{1,0:T(8,128)(2,1)S(1)}, u32[]{:S(2)}, u32[]{:S(2)}) %collective-permute-start.7) | collective-permute-done | bytes 262176 | tf_op jit(solution)/shard_map/ppermute | solution.py:278
  50.3 0.1 collective-permute-start.8
  50.3 1.5 %collective-permute-done.8 = bf16[256,512]{1,0:T(8,128)(2,1)S(1)} collective-permute-done((bf16[256,512]{1,0:T(8,128)(2,1)S(1)}, bf16[256,512]{1,0:T(8,128)(2,1)S(1)}, u32[]{:S(2)}, u32[]{:S(2)}) %collective-permute-start.8) | collective-permute-done | bytes 262176 | tf_op jit(solution)/shard_map/ppermute | solution.py:278
  51.9 0.1 fusion.5
  52.0 1.0 %collective-permute-start.9 = (bf16[64,512]{1,0:T(8,128)(2,1)S(1)}, bf16[64,512]{1,0:T(8,128)(2,1)S(1)}, u32[]{:S(2)}, u32[]{:S(2)}) collective-permute-start(bf16[64,512]{1,0:T(8,128)(2,1)S(1)} %get-tuple-element.43), channel_id=1, source_target_pairs={{0,4},{4,0},{8,12},{12,8},{1,5},{5,1},{9,13},{13,9},{2,6},{6,2},{1... | collective-permute-start | bytes 196616 | tf_op jit(solution)/shard_map/ppermute | solution.py:278
  53.0 1.9 %collective-permute-start.11 = (bf16[64,512]{1,0:T(8,128)(2,1)S(1)}, bf16[64,512]{1,0:T(8,128)(2,1)S(1)}, u32[]{:S(2)}, u32[]{:S(2)}) collective-permute-start(bf16[64,512]{1,0:T(8,128)(2,1)S(1)} %get-tuple-element.44), channel_id=1, source_target_pairs={{0,12},{4,8},{8,4},{12,0},{1,13},{5,9},{9,5},{13,1},{2,14},{6,10},... | collective-permute-start | bytes 196616 | tf_op jit(solution)/shard_map/ppermute | solution.py:278
  54.8 0.7 %collective-permute-start.10 = (bf16[64,512]{1,0:T(8,128)(2,1)S(1)}, bf16[64,512]{1,0:T(8,128)(2,1)S(1)}, u32[]{:S(2)}, u32[]{:S(2)}) collective-permute-start(bf16[64,512]{1,0:T(8,128)(2,1)S(1)} %get-tuple-element.45), channel_id=1, source_target_pairs={{0,8},{4,12},{8,0},{12,4},{1,9},{5,13},{9,1},{13,5},{2,10},{6,14},... | collective-permute-start | bytes 196616 | tf_op jit(solution)/shard_map/ppermute | solution.py:278
  55.6 0.8 %collective-permute-done.9 = bf16[64,512]{1,0:T(8,128)(2,1)S(1)} collective-permute-done((bf16[64,512]{1,0:T(8,128)(2,1)S(1)}, bf16[64,512]{1,0:T(8,128)(2,1)S(1)}, u32[]{:S(2)}, u32[]{:S(2)}) %collective-permute-start.9) | collective-permute-done | bytes 65568 | tf_op jit(solution)/shard_map/ppermute | solution.py:278
  56.3 3.3 %collective-permute-done.11 = bf16[64,512]{1,0:T(8,128)(2,1)S(1)} collective-permute-done((bf16[64,512]{1,0:T(8,128)(2,1)S(1)}, bf16[64,512]{1,0:T(8,128)(2,1)S(1)}, u32[]{:S(2)}, u32[]{:S(2)}) %collective-permute-start.11) | collective-permute-done | bytes 65568 | tf_op jit(solution)/shard_map/ppermute | solution.py:278
  59.6 2.4 %collective-permute-done.10 = bf16[64,512]{1,0:T(8,128)(2,1)S(1)} collective-permute-done((bf16[64,512]{1,0:T(8,128)(2,1)S(1)}, bf16[64,512]{1,0:T(8,128)(2,1)S(1)}, u32[]{:S(2)}, u32[]{:S(2)}) %collective-permute-start.10) | collective-permute-done | bytes 65568 | tf_op jit(solution)/shard_map/ppermute | solution.py:278
  62.0 0.7 %fusion.4 = bf16[64,512]{1,0:T(8,128)(2,1)} fusion(f32[256,512]{1,0:T(8,128)S(1)} %get-tuple-element.42, bf16[64,512]{1,0:T(8,128)(2,1)S(1)} %collective-permute-done.11, bf16[64,512]{1,0:T(8,128)(2,1)S(1)} %collective-permute-done.10, bf16[64,512]{1,0:T(8,128)(2,1)S(1)} %collective-permute-done.9), kind=kLoop, calls=%fused_computation.9 | loop fusion | flops 229376 | bytes 393216 | tf_op jit(solution)/shard_map/convert_element_type | solution.py:354
  (4 shorter events, 0.1 us)
Async XLA Ops:
  0.9 10.8 %collective-permute-start.2 = (bf16[80,512]{1,0:T(8,128)(2,1)S(1)}, bf16[80,512]{1,0:T(8,128)(2,1)S(1)}, u32[]{:S(2)}, u32[]{:S(2)}) collective-permute-start(bf16[80,512]{1,0:T(8,128)(2,1)S(1)} %shard_map.64.packed.first.one), channel_id=1, source_target_pairs={{0,12},{4,8},{8,4},{12,0},{1,13},{5,9},{9,5},{13,1},{2,14},{6,10},... | collective-permute-start | bytes 245768 | tf_op jit(solution)/shard_map/ppermute | solution.py:278
  6.0 6.9 %collective-permute-start.1 = (bf16[80,512]{1,0:T(8,128)(2,1)S(1)}, bf16[80,512]{1,0:T(8,128)(2,1)S(1)}, u32[]{:S(2)}, u32[]{:S(2)}) collective-permute-start(bf16[80,512]{1,0:T(8,128)(2,1)S(1)} %shard_map.64.packed.first.one), channel_id=1, source_target_pairs={{0,8},{4,12},{8,0},{12,4},{1,9},{5,13},{9,1},{13,5},{2,10},{6,14},... | collective-permute-start | bytes 245768 | tf_op jit(solution)/shard_map/ppermute | solution.py:278
  6.0 6.9 %collective-permute-start = (bf16[80,512]{1,0:T(8,128)(2,1)S(1)}, bf16[80,512]{1,0:T(8,128)(2,1)S(1)}, u32[]{:S(2)}, u32[]{:S(2)}) collective-permute-start(bf16[80,512]{1,0:T(8,128)(2,1)S(1)} %shard_map.64.packed.first.one), channel_id=1, source_target_pairs={{0,4},{4,0},{8,12},{12,8},{1,5},{5,1},{9,13},{13,9},{2,6},{6,2},{1... | collective-permute-start | bytes 245768 | tf_op jit(solution)/shard_map/ppermute | solution.py:278
  12.9 1.6 %collective-permute-start.4 = (bf16[256,512]{1,0:T(8,128)(2,1)S(1)}, bf16[256,512]{1,0:T(8,128)(2,1)S(1)}, u32[]{:S(2)}, u32[]{:S(2)}) collective-permute-start(bf16[256,512]{1,0:T(8,128)(2,1)S(1)} %shard_map.66.near), channel_id=1, source_target_pairs={{0,1},{1,0},{2,3},{3,2},{4,5},{5,4},{6,7},{7,6},{8,9},{9,8},{10,11... | collective-permute-start | bytes 786440 | tf_op jit(solution)/shard_map/ppermute | solution.py:278
  13.0 12.4 %collective-permute-start.3 = (bf16[256,512]{1,0:T(8,128)(2,1)S(1)}, bf16[256,512]{1,0:T(8,128)(2,1)S(1)}, u32[]{:S(2)}, u32[]{:S(2)}) collective-permute-start(bf16[256,512]{1,0:T(8,128)(2,1)S(1)} %shard_map.66.near), channel_id=1, source_target_pairs={{0,2},{1,3},{2,0},{3,1},{4,6},{5,7},{6,4},{7,5},{8,10},{9,11},{10,... | collective-permute-start | bytes 786440 | tf_op jit(solution)/shard_map/ppermute | solution.py:278
  25.4 1.6 %collective-permute-start.5 = (bf16[256,512]{1,0:T(8,128)(2,1)S(1)}, bf16[256,512]{1,0:T(8,128)(2,1)S(1)}, u32[]{:S(2)}, u32[]{:S(2)}) collective-permute-start(bf16[256,512]{1,0:T(8,128)(2,1)S(1)} %collective-permute-done.3.near), channel_id=1, source_target_pairs={{0,1},{1,0},{2,3},{3,2},{4,5},{5,4},{6,7},{7,6},{8,9},{9,8},{10,11... | collective-permute-start | bytes 786440 | tf_op jit(solution)/shard_map/ppermute | solution.py:278
  40.1 1.6 %collective-permute-start.6 = (bf16[256,512]{1,0:T(8,128)(2,1)S(1)}, bf16[256,512]{1,0:T(8,128)(2,1)S(1)}, u32[]{:S(2)}, u32[]{:S(2)}) collective-permute-start(bf16[256,512]{1,0:T(8,128)(2,1)S(1)} %slice_bitcast_fusion.1), channel_id=1, source_target_pairs={{0,1},{1,0},{2,3},{3,2},{4,5},{5,4},{6,7},{7,6},{8,9},{9,8},{10,11... | collective-permute-start | bytes 786440 | tf_op jit(solution)/shard_map/ppermute | solution.py:278
  41.8 8.4 %collective-permute-start.7 = (bf16[256,512]{1,0:T(8,128)(2,1)S(1)}, bf16[256,512]{1,0:T(8,128)(2,1)S(1)}, u32[]{:S(2)}, u32[]{:S(2)}) collective-permute-start(bf16[256,512]{1,0:T(8,128)(2,1)S(1)} %fusion.1), channel_id=1, source_target_pairs={{0,2},{1,3},{2,0},{3,1},{4,6},{5,7},{6,4},{7,5},{8,10},{9,11},{10,... | collective-permute-start | bytes 786440 | tf_op jit(solution)/shard_map/ppermute | solution.py:278
  50.3 1.6 %collective-permute-start.8 = (bf16[256,512]{1,0:T(8,128)(2,1)S(1)}, bf16[256,512]{1,0:T(8,128)(2,1)S(1)}, u32[]{:S(2)}, u32[]{:S(2)}) collective-permute-start(bf16[256,512]{1,0:T(8,128)(2,1)S(1)} %slice_bitcast_fusion), channel_id=1, source_target_pairs={{0,1},{1,0},{2,3},{3,2},{4,5},{5,4},{6,7},{7,6},{8,9},{9,8},{10,11... | collective-permute-start | bytes 786440 | tf_op jit(solution)/shard_map/ppermute | solution.py:278
  52.0 4.3 %collective-permute-start.9 = (bf16[64,512]{1,0:T(8,128)(2,1)S(1)}, bf16[64,512]{1,0:T(8,128)(2,1)S(1)}, u32[]{:S(2)}, u32[]{:S(2)}) collective-permute-start(bf16[64,512]{1,0:T(8,128)(2,1)S(1)} %get-tuple-element.43), channel_id=1, source_target_pairs={{0,4},{4,0},{8,12},{12,8},{1,5},{5,1},{9,13},{13,9},{2,6},{6,2},{1... | collective-permute-start | bytes 196616 | tf_op jit(solution)/shard_map/ppermute | solution.py:278
  53.0 6.7 %collective-permute-start.11 = (bf16[64,512]{1,0:T(8,128)(2,1)S(1)}, bf16[64,512]{1,0:T(8,128)(2,1)S(1)}, u32[]{:S(2)}, u32[]{:S(2)}) collective-permute-start(bf16[64,512]{1,0:T(8,128)(2,1)S(1)} %get-tuple-element.44), channel_id=1, source_target_pairs={{0,12},{4,8},{8,4},{12,0},{1,13},{5,9},{9,5},{13,1},{2,14},{6,10},... | collective-permute-start | bytes 196616 | tf_op jit(solution)/shard_map/ppermute | solution.py:278
  54.8 7.2 %collective-permute-start.10 = (bf16[64,512]{1,0:T(8,128)(2,1)S(1)}, bf16[64,512]{1,0:T(8,128)(2,1)S(1)}, u32[]{:S(2)}, u32[]{:S(2)}) collective-permute-start(bf16[64,512]{1,0:T(8,128)(2,1)S(1)} %get-tuple-element.45), channel_id=1, source_target_pairs={{0,8},{4,12},{8,0},{12,4},{1,9},{5,13},{9,1},{13,5},{2,10},{6,14},... | collective-permute-start | bytes 196616 | tf_op jit(solution)/shard_map/ppermute | solution.py:278

commit v4 on v3

--- a/solution.py
+++ b/solution.py
@@ -83,6 +83,7 @@
 TILE = 16
 TOPK = 6
 GROUP = 4
+FIRST = 4
 
 
 def dot(a, b, dims):
@@ -111,13 +112,12 @@
     copies[2].wait()
 
 
-def early_kernel(place, packed, wd, down, sems):
-    width = down.shape[2]
-    column = pl.multiple_of(((place[1] >> 1) ^ 1) * width, width)
-    fetch_all((wd,), (down,), sems, column)
-    for e in range(down.shape[0]):
-        for copy in fetch((wd,), (down,), sems, column, e):
-            copy.wait()
+def early_kernel(place, packed, wg, wu, first_g, first_u, sems):
+    copies = fetches((wg, wu), (first_g, first_u), sems, near_pair(place, first_g), 0)
+    for copy in copies:
+        copy.start()
+    for copy in copies:
+        copy.wait()
 
 
 def join_kernel(first, second, third, fourth, out):
@@ -152,18 +152,28 @@
         slot_weight[e * slots : (e + 1) * slots, :] = jnp.broadcast_to(spread, (slots, 128))
 
 
-def fetch(weights, buffers, sems, column, e):
-    width = buffers[0].shape[2]
+def near_pair(place, buffer):
+    width = buffer.shape[2]
+    return pl.multiple_of((place[1] >> 1) * width, width)
+
+
+def far_pair(place, buffer):
+    width = buffer.shape[2]
+    return pl.multiple_of(((place[1] >> 1) ^ 1) * width, width)
+
+
+def fetches(weights, buffers, sems, column, first, one=None):
+    count, _, width = buffers[0].shape
     return [
-        pltpu.make_async_copy(w.at[e, :, pl.ds(column, width)], b.at[e], sems.at[i, e])
+        pltpu.make_async_copy(w.at[first + e, :, pl.ds(column, width)], b.at[e], sems.at[i, e])
+        for e in (range(count) if one is None else (one,))
         for i, (w, b) in enumerate(zip(weights, buffers))
     ]
 
 
-def fetch_all(weights, buffers, sems, column):
-    for e in range(buffers[0].shape[0]):
-        for copy in fetch(weights, buffers, sems, column, e):
-            copy.start()
+def wait_all(copies):
+    for copy in copies:
+        copy.wait()
 
 
 def place_rows(place, pick_mat, near, far, taken):
@@ -182,80 +192,86 @@
         out[j] = dot(pick_back[...], block, NN).astype(jnp.bfloat16)
 
 
-def over_experts(residents, slots, arrive, work):
+def in_groups(first, last, slots, work, after=None, arrive=None, size=2):
     def some(step, carry):
-        group = [step * GROUP + g for g in range(GROUP)]
-        for e in group:
+        group = [first + step * size + g for g in range(size)]
+        places = [pl.ds(pl.multiple_of(e * slots, slots), slots) for e in group]
+        for e in group if arrive else ():
             arrive(e)
-        work(group, [pl.ds(pl.multiple_of(e * slots, slots), slots) for e in group])
+        for e, mine in zip(group, places):
+            work(e, mine)
+        for e, mine in zip(group, places) if after else ():
+            after(e, mine)
         return carry
 
-    lax.fori_loop(0, residents // GROUP, some, 0)
-
-
-def half_kernel(slots, place, near, far, one, two, three, four, wg, wu, *rest):
-    pick_mat, pick_back, slot_weight, gate, up, taken, table, bg, bu, sems = rest
-    width = bg.shape[2]
-    column = pl.multiple_of((place[1] >> 1) * width, width)
-    residents = bg.shape[0]
-    fetch_all((wg, wu), (bg, bu), sems, column)
+    lax.fori_loop(0, (last - first) // size, some, 0)
+
+
+def half_kernel(slots, place, near, far, one, two, three, four, first_g, first_u, wg, wu, wd, *rest):
+    pick_mat, pick_back, slot_weight, gate, up, down, next_g, next_u, taken, table, bg, bu, sems, ahead = rest
+    held = first_g.shape[0]
+    residents = held + bg.shape[0]
+    later = far_pair(place, bg)
+    copies = fetches((wg, wu), (bg, bu), sems, near_pair(place, bg), held)
+    early = fetches((wd,), (down,), ahead.at[2:], later, 0) + fetches((wg, wu), (next_g, next_u), ahead, later, 0)
+    for copy in copies + early:
+        copy.start()
     route(place, (one, two, three, four), TOPK, slots, residents, table, pick_mat, slot_weight)
     place_rows(place, pick_mat, near, far, taken)
     pick_back[...] = pick_mat[...].T
 
+    def work(e, mine, g_block, u_block):
+        x = taken[mine, :]
+        gate[mine, :] = dot(x, g_block, NT)
+        up[mine, :] = dot(x, u_block, NT)
+
+    in_groups(0, held, slots, lambda e, mine: work(e, mine, first_g[e], first_u[e]), size=GROUP)
+    wait_all(copies)
+    in_groups(held, residents, slots, lambda e, mine: work(e, mine, bg[e - held], bu[e - held]), size=GROUP)
+    wait_all(early)
+
+
+def rest_kernel(slots, place, near, far, pick_mat, pick_back, slot_weight, gate, up, down, next_g, next_u, *rest):
+    wg, wu, hidden, out, taken, given, bg, bu, sems = rest
+    held = next_g.shape[0]
+    residents = held + bg.shape[0]
+    copies = fetches((wg, wu), (bg, bu), sems, far_pair(place, bg), held)
+    for copy in copies:
+        copy.start()
+    place_rows(place, pick_mat, near, far, taken)
+
+    def work(e, mine, g_block, u_block):
+        x = taken[mine, :]
+        gate_val = gate[mine, :] + dot(x, g_block, NT)
+        up_val = up[mine, :] + dot(x, u_block, NT)
+        scaled = gate_val * jax.nn.sigmoid(gate_val) * up_val * slot_weight[mine, :1]
+        hidden[mine, :] = scaled.astype(jnp.bfloat16)
+
+    def lower(e, mine):
+        given[mine, :] = dot(hidden[mine, :], down[e], NN).astype(jnp.bfloat16)
+
     def arrive(e):
-        for copy in fetch((wg, wu), (bg, bu), sems, column, e):
+        for copy in fetches((wg, wu), (bg, bu), sems, far_pair(place, bg), held, e - held):
             copy.wait()
 
-    def work(group, places):
-        for e, mine in zip(group, places):
-            x = taken[mine, :]
-            gate[mine, :] = dot(x, bg[e], NT)
-            up[mine, :] = dot(x, bu[e], NT)
-
-    over_experts(residents, slots, arrive, work)
-
-
-def rest_kernel(slots, place, near, far, pick_mat, pick_back, slot_weight, gate, up, down, wg, wu, *rest):
-    hidden, out, taken, given, bg, bu, sems = rest
-    column = pl.multiple_of(((place[1] >> 1) ^ 1) * bg.shape[2], bg.shape[2])
-    fetch_all((wg, wu), (bg, bu), sems, column)
-    place_rows(place, pick_mat, near, far, taken)
+    in_groups(0, held, slots, lambda e, mine: work(e, mine, next_g[e], next_u[e]), lower)
+    in_groups(held, residents, slots, lambda e, mine: work(e, mine, bg[e - held], bu[e - held]), lower, arrive)
+    add_up(place, pick_back, given, out)
+
+
+def down_kernel(slots, place, hidden, pick_back, wd, out, given, bd, sems):
+    copies = fetches((wd,), (bd,), sems, near_pair(place, bd), 0)
+    for copy in copies:
+        copy.start()
 
     def arrive(e):
-        for copy in fetch((wg, wu), (bg, bu), sems, column, e):
+        for copy in fetches((wd,), (bd,), sems, near_pair(place, bd), 0, e):
             copy.wait()
 
-    def work(group, places):
-        ready = []
-        for e, mine in zip(group, places):
-            x = taken[mine, :]
-            gate_val = gate[mine, :] + dot(x, bg[e], NT)
-            up_val = up[mine, :] + dot(x, bu[e], NT)
-            scaled = gate_val * jax.nn.sigmoid(gate_val) * up_val * slot_weight[mine, :1]
-            scaled = scaled.astype(jnp.bfloat16)
-            hidden[mine, :] = scaled
-            ready.append(scaled)
-        for e, mine, scaled in zip(group, places, ready):
-            given[mine, :] = dot(scaled, down[e], NN).astype(jnp.bfloat16)
-
-    over_experts(bg.shape[0], slots, arrive, work)
-    add_up(place, pick_back, given, out)
-
-
-def down_kernel(slots, place, hidden, pick_back, wd, out, given, bd, sems):
-    column = pl.multiple_of((place[1] >> 1) * bd.shape[2], bd.shape[2])
-    fetch_all((wd,), (bd,), sems, column)
-
-    def arrive(e):
-        for copy in fetch((wd,), (bd,), sems, column, e):
-            copy.wait()
-
-    def work(group, places):
-        for e, mine in zip(group, places):
-            given[mine, :] = dot(hidden[mine, :], bd[e], NN).astype(jnp.bfloat16)
-
-    over_experts(bd.shape[0], slots, arrive, work)
+    def lower(e, mine):
+        given[mine, :] = dot(hidden[mine, :], bd[e], NN).astype(jnp.bfloat16)
+
+    in_groups(0, bd.shape[0], slots, lower, None, arrive)
     add_up(place, pick_back, given, out)
 
 
@@ -306,10 +322,13 @@
         2,
     )
     sems = lambda n: pltpu.SemaphoreType.DMA((n, residents))
-    down = shape((residents, units, 2 * share), jnp.bfloat16)
-    down = call(early_kernel, (place, mine, wd), 1, down, [sems(1)], 5, 2)
+    several = lambda n: shape((n, units, 2 * share), jnp.bfloat16)
+    scratch = lambda n: pltpu.VMEM(several(n).shape, jnp.bfloat16)
+    first = residents - FIRST
+    first_pair = call(early_kernel, (place, mine, wg, wu), 2, (several(first), several(first)), [sems(2)], 7, 2)
     came = {k: swap(mine, "expert", k) for k in (3, 2, 1)}
-    pieces, down = lax.optimization_barrier(((mine, came[1], came[2], came[3]), down))
+    pieces = (mine, came[1], came[2], came[3])
+    pieces, first_pair = lax.optimization_barrier((pieces, first_pair))
     own = call(join_kernel, pieces, 0, shape((rows, share), jnp.bfloat16), [], 1, 2)
     core = swap(own, "tensor", 1)
     across = swap(own, "tensor", 2)
@@ -317,33 +336,32 @@
     slot_weight, part = shape((total, 128), jnp.float32), shape((total, units), jnp.float32)
     hidden, parts = shape((total, units), jnp.bfloat16), shape((2, rows, share), jnp.bfloat16)
     taken = pltpu.VMEM((total, 2 * share), jnp.bfloat16)
-    blocks = pltpu.VMEM(down.shape, jnp.bfloat16)
-    pick_mat, pick_back, slot_weight, gate, up = call(
+    pick_mat, pick_back, slot_weight, gate, up, down, *next_pair = call(
         functools.partial(half_kernel, slots),
-        (place, own, core) + pieces + (wg, wu),
-        2,
-        (pick_mat, pick_back, slot_weight, part, part),
-        [taken, pltpu.VMEM((3 * TILE, rows), jnp.float32), blocks, blocks, sems(2)],
+        (place, own, core) + pieces + tuple(first_pair) + (wg, wu, wd),
+        3,
+        (pick_mat, pick_back, slot_weight, part, part, several(residents), several(FIRST), several(FIRST)),
+        [taken, pltpu.VMEM((3 * TILE, rows), jnp.float32), scratch(FIRST), scratch(FIRST), sems(2), sems(3)],
         9,
-        30,
+        10,
     )
     across_late, gate = lax.optimization_barrier((across, gate))
     across_core = swap(across_late, "tensor", 1)
     hidden, away_parts = call(
         functools.partial(rest_kernel, slots),
-        (place, across, across_core, pick_mat, pick_back, slot_weight, gate, up, down, wg, wu),
+        (place, across, across_core, pick_mat, pick_back, slot_weight, gate, up, down, *next_pair, wg, wu),
         2,
         (hidden, parts),
-        [taken, taken, blocks, blocks, sems(2)],
+        [taken, taken, scratch(first), scratch(first), sems(2)],
         12,
-        32,
+        24,
     )
     wide = lambda a: a.astype(jnp.float32)
     away = (wide(away_parts[0]) + wide(swap(away_parts[1], "tensor", 1))).astype(jnp.bfloat16)
     away, hidden = lax.optimization_barrier((away, hidden))
     back = swap(away, "tensor", 2)
     home_parts = call(
-        functools.partial(down_kernel, slots), (place, hidden, pick_back, wd), 1, parts, [taken, blocks, sems(1)], 5, 44
+        functools.partial(down_kernel, slots), (place, hidden, pick_back, wd), 1, parts, [taken, scratch(residents), sems(1)], 5, 16
     )
     home_parts, back = lax.optimization_barrier((home_parts, back))
     home = wide(home_parts[0]) + wide(swap(home_parts[1], "tensor", 1)) + wide(back)

time: 62.9 us -> 61.8 us (0.983)
  waiting for transfers between devices: 12.7 us -> 10.5 us
  starting transfers between devices: 13 us -> 13.9 us
    ppermute x12, waiting for transfers between devices: 12.7 us -> 10.5 us  [swap(): return lax.ppermute(a, axis, [(i, i ^ bits) for i in range(n)])]
    ppermute x12, starting transfers between devices: 13 us -> 13.9 us  [swap(): return lax.ppermute(a, axis, [(i, i ^ bits) for i in range(n)])]
  transfers between devices with their start and end apart: 12 -> 12, of which waited for: 8 -> 7; matrix products, arithmetic and copies ran while one was open for 0% -> 0% of each run, Pallas kernels for 35% -> 38%
where the time goes in v4:
time: 61.8 us; the launch traced here: 61.6 us
  Pallas kernels  36.2 us (59%)
  starting transfers between devices  13.9 us (22%)
  waiting for transfers between devices  10.5 us (17%)
  other arithmetic  0.9 us (1%)
    pallas_call x6, Pallas kernels, call(): pl.pallas_call(kernel, in_specs=specs + [there] * fetched, out_specs=jax....  36.2 us
    ppermute x12, starting transfers between devices, swap(): return lax.ppermute(a, axis, [(i, i ^ bits) for i in range(n)])  13.9 us
    ppermute x12, waiting for transfers between devices, swap(): return lax.ppermute(a, axis, [(i, i ^ bits) for i in range(n)])  10.5 us
  transfers between devices with their start and end apart: 12, of which 7 were waited for; matrix products, arithmetic and copies ran while one was open for 0% of the time, Pallas kernels for 38%

profile of v4, /device:TPU:0, one launch (start us, length us, event | category | flops | bytes accessed | tf_op | source)
XLA Modules:
  0.0 61.6 jit_solution(16574758572277072893)
XLA Ops:
  0.0 0.9 %shard_map.64.packed.first.one = bf16[80,512]{1,0:T(8,128)(2,1)S(1)} custom-call(bf16[64,512]{1,0:T(8,128)(2,1)} %bitcast.25, s32[6,2,32]{2,1,0:T(2,128)} %bitcast.26, f32[6,2,32]{2,1,0:T(2,128)} %bitcast.27), custom_call_target="tpu_custom_call" | custom-call | flops 1000000000 | bytes 3000000 | tf_op jit(solution)/shard_map/pallas_call | solution.py:281
  0.9 3.1 %collective-permute-start = (bf16[80,512]{1,0:T(8,128)(2,1)S(1)}, bf16[80,512]{1,0:T(8,128)(2,1)S(1)}, u32[]{:S(2)}, u32[]{:S(2)}) collective-permute-start(bf16[80,512]{1,0:T(8,128)(2,1)S(1)} %shard_map.64.packed.first.one), channel_id=1, source_target_pairs={{0,4},{4,0},{8,12},{12,8},{1,5},{5,1},{9,13},{13,9},{2,6},{6,2},{1... | collective-permute-start | bytes 245768 | tf_op jit(solution)/shard_map/ppermute | solution.py:294
  4.0 2.6 %collective-permute-start.1 = (bf16[80,512]{1,0:T(8,128)(2,1)S(1)}, bf16[80,512]{1,0:T(8,128)(2,1)S(1)}, u32[]{:S(2)}, u32[]{:S(2)}) collective-permute-start(bf16[80,512]{1,0:T(8,128)(2,1)S(1)} %shard_map.64.packed.first.one), channel_id=1, source_target_pairs={{0,8},{4,12},{8,0},{12,4},{1,9},{5,13},{9,1},{13,5},{2,10},{6,14},... | collective-permute-start | bytes 245768 | tf_op jit(solution)/shard_map/ppermute | solution.py:294
  6.6 0.0 collective-permute-start.2
  6.6 0.1 pad_add_fusion.place
  6.7 6.7 %shard_map.65 = (bf16[12,352,1024]{2,1,0:T(8,128)(2,1)S(1)}, bf16[12,352,1024]{2,1,0:T(8,128)(2,1)S(1)}) custom-call(s32[2]{0:T(128)S(1)} %pad_add_fusion.place, bf16[80,512]{1,0:T(8,128)(2,1)S(1)} %shard_map.64.packed.first.one, bf16[16,352,2048]{2,1,0:T(8,128)(2,1)} %bitcast.19, bf16[16,352,2048]{2,1,0:T(8,128)(2,1)} %bitcast.22), custom_call_target="tpu_custom_call" | custom-call | flops 7000000000 | bytes 21000000 | tf_op jit(solution)/shard_map/pallas_call | solution.py:281
  13.4 0.0 collective-permute-done.second.two
  13.4 0.0 collective-permute-done.1.third.three
  13.4 0.0 collective-permute-done.2.fourth.four
  13.5 0.1 collective-permute-start.4
  13.6 1.8 %collective-permute-start.3 = (bf16[256,512]{1,0:T(8,128)(2,1)S(1)}, bf16[256,512]{1,0:T(8,128)(2,1)S(1)}, u32[]{:S(2)}, u32[]{:S(2)}) collective-permute-start(bf16[256,512]{1,0:T(8,128)(2,1)S(1)} %shard_map.66.near), channel_id=1, source_target_pairs={{0,2},{1,3},{2,0},{3,1},{4,6},{5,7},{6,4},{7,5},{8,10},{9,11},{10,... | collective-permute-start | bytes 786440 | tf_op jit(solution)/shard_map/ppermute | solution.py:294
  15.4 0.0 collective-permute-done.4.far
  15.4 10.8 %shard_map.67 = (bf16[768,256]{1,0:T(8,128)(2,1)S(1)}, bf16[256,768]{1,0:T(8,128)(2,1)S(1)}, f32[768,128]{1,0:T(8,128)S(1)}, f32[768,352]{1,0:T(8,128)S(1)}, f32...) custom-call(s32[2]{0:T(128)S(1)} %pad_add_fusion.place, ...), custom_call_target="tpu_custom_call" | custom-call | flops 8999999488 | bytes 27000000 | tf_op jit(solution)/shard_map/pallas_call | solution.py:281
  26.2 0.0 collective-permute-done.3.near
  26.2 0.2 collective-permute-start.5
  26.5 1.4 %collective-permute-done.5.far = bf16[256,512]{1,0:T(8,128)(2,1)S(1)} collective-permute-done((bf16[256,512]{1,0:T(8,128)(2,1)S(1)}, bf16[256,512]{1,0:T(8,128)(2,1)S(1)}, u32[]{:S(2)}, u32[]{:S(2)}) %collective-permute-start.5) | collective-permute-done | bytes 262176 | tf_op jit(solution)/shard_map/ppermute | solution.py:294
  27.8 11.8 %shard_map.68 = (bf16[768,352]{1,0:T(8,128)(2,1)S(1)}, bf16[2,256,512]{2,1,0:T(8,128)(2,1)S(1)}) custom-call(s32[2]{0:T(128)S(1)} %pad_add_fusion.place, bf16[256,512]{1,0:T(8,128)(2,1)S(1)} %collective-permute-done.3.near, bf16[256,512]{1,0:T(8,128)(2,1)S(1)} %collective-permute-done.5.far, bf16[768,256]{1,0:T(8,128)(2,1)S(1)} %get-tuple-element.39.pick_mat, ...), custom_call_target="tpu_custom_call" | custom-call | flops 12000000000 | bytes 36000000 | tf_op jit(solution)/shard_map/pallas_call | solution.py:281
  39.6 0.3 collective-permute-start.6
  39.9 1.3 %collective-permute-done.6 = bf16[256,512]{1,0:T(8,128)(2,1)S(1)} collective-permute-done((bf16[256,512]{1,0:T(8,128)(2,1)S(1)}, bf16[256,512]{1,0:T(8,128)(2,1)S(1)}, u32[]{:S(2)}, u32[]{:S(2)}) %collective-permute-start.6) | collective-permute-done | bytes 262176 | tf_op jit(solution)/shard_map/ppermute | solution.py:294
  41.2 0.1 fusion.1
  41.3 1.5 %collective-permute-start.7 = (bf16[256,512]{1,0:T(8,128)(2,1)S(1)}, bf16[256,512]{1,0:T(8,128)(2,1)S(1)}, u32[]{:S(2)}, u32[]{:S(2)}) collective-permute-start(bf16[256,512]{1,0:T(8,128)(2,1)S(1)} %fusion.1), channel_id=1, source_target_pairs={{0,2},{1,3},{2,0},{3,1},{4,6},{5,7},{6,4},{7,5},{8,10},{9,11},{10,... | collective-permute-start | bytes 786440 | tf_op jit(solution)/shard_map/ppermute | solution.py:294
  42.8 5.9 %shard_map.69 = bf16[2,256,512]{2,1,0:T(8,128)(2,1)S(1)} custom-call(s32[2]{0:T(128)S(1)} %pad_add_fusion.place, bf16[768,352]{1,0:T(8,128)(2,1)S(1)} %get-tuple-element.49.hidden, bf16[256,768]{1,0:T(8,128)(2,1)S(1)} %get-tuple-element.40.pick_back, bf16[16,352,2048]{2,1,0:T(8,128)(2,1)} %wd.3), custom_call_target="tpu_custom_call" | custom-call | flops 5000000000 | bytes 15000000 | tf_op jit(solution)/shard_map/pallas_call | solution.py:281
  48.8 1.0 %collective-permute-done.7 = bf16[256,512]{1,0:T(8,128)(2,1)S(1)} collective-permute-done((bf16[256,512]{1,0:T(8,128)(2,1)S(1)}, bf16[256,512]{1,0:T(8,128)(2,1)S(1)}, u32[]{:S(2)}, u32[]{:S(2)}) %collective-permute-start.7) | collective-permute-done | bytes 262176 | tf_op jit(solution)/shard_map/ppermute | solution.py:294
  49.8 0.1 collective-permute-start.8
  49.9 1.5 %collective-permute-done.8 = bf16[256,512]{1,0:T(8,128)(2,1)S(1)} collective-permute-done((bf16[256,512]{1,0:T(8,128)(2,1)S(1)}, bf16[256,512]{1,0:T(8,128)(2,1)S(1)}, u32[]{:S(2)}, u32[]{:S(2)}) %collective-permute-start.8) | collective-permute-done | bytes 262176 | tf_op jit(solution)/shard_map/ppermute | solution.py:294
  51.4 0.1 fusion.5
  51.5 2.0 %collective-permute-start.10 = (bf16[64,512]{1,0:T(8,128)(2,1)S(1)}, bf16[64,512]{1,0:T(8,128)(2,1)S(1)}, u32[]{:S(2)}, u32[]{:S(2)}) collective-permute-start(bf16[64,512]{1,0:T(8,128)(2,1)S(1)} %get-tuple-element.57), channel_id=1, source_target_pairs={{0,8},{4,12},{8,0},{12,4},{1,9},{5,13},{9,1},{13,5},{2,10},{6,14},... | collective-permute-start | bytes 196616 | tf_op jit(solution)/shard_map/ppermute | solution.py:294
  53.5 1.7 %collective-permute-start.11 = (bf16[64,512]{1,0:T(8,128)(2,1)S(1)}, bf16[64,512]{1,0:T(8,128)(2,1)S(1)}, u32[]{:S(2)}, u32[]{:S(2)}) collective-permute-start(bf16[64,512]{1,0:T(8,128)(2,1)S(1)} %get-tuple-element.56), channel_id=1, source_target_pairs={{0,12},{4,8},{8,4},{12,0},{1,13},{5,9},{9,5},{13,1},{2,14},{6,10},... | collective-permute-start | bytes 196616 | tf_op jit(solution)/shard_map/ppermute | solution.py:294
  55.3 0.5 collective-permute-start.9
  55.7 4.1 %collective-permute-done.10 = bf16[64,512]{1,0:T(8,128)(2,1)S(1)} collective-permute-done((bf16[64,512]{1,0:T(8,128)(2,1)S(1)}, bf16[64,512]{1,0:T(8,128)(2,1)S(1)}, u32[]{:S(2)}, u32[]{:S(2)}) %collective-permute-start.10) | collective-permute-done | bytes 65568 | tf_op jit(solution)/shard_map/ppermute | solution.py:294
  59.8 0.4 collective-permute-done.11
  60.2 0.8 %collective-permute-done.9 = bf16[64,512]{1,0:T(8,128)(2,1)S(1)} collective-permute-done((bf16[64,512]{1,0:T(8,128)(2,1)S(1)}, bf16[64,512]{1,0:T(8,128)(2,1)S(1)}, u32[]{:S(2)}, u32[]{:S(2)}) %collective-permute-start.9) | collective-permute-done | bytes 65568 | tf_op jit(solution)/shard_map/ppermute | solution.py:294
  61.0 0.7 %fusion.4 = bf16[64,512]{1,0:T(8,128)(2,1)} fusion(f32[256,512]{1,0:T(8,128)S(1)} %get-tuple-element.54, bf16[64,512]{1,0:T(8,128)(2,1)S(1)} %collective-permute-done.11, bf16[64,512]{1,0:T(8,128)(2,1)S(1)} %collective-permute-done.10, bf16[64,512]{1,0:T(8,128)(2,1)S(1)} %collective-permute-done.9), kind=kLoop, calls=%fused_computation.9 | loop fusion | flops 229376 | bytes 393216 | tf_op jit(solution)/shard_map/convert_element_type | solution.py:372
  (4 shorter events, 0.1 us)
Async XLA Ops:
  0.9 12.5 %collective-permute-start = (bf16[80,512]{1,0:T(8,128)(2,1)S(1)}, bf16[80,512]{1,0:T(8,128)(2,1)S(1)}, u32[]{:S(2)}, u32[]{:S(2)}) collective-permute-start(bf16[80,512]{1,0:T(8,128)(2,1)S(1)} %shard_map.64.packed.first.one), channel_id=1, source_target_pairs={{0,4},{4,0},{8,12},{12,8},{1,5},{5,1},{9,13},{13,9},{2,6},{6,2},{1... | collective-permute-start | bytes 245768 | tf_op jit(solution)/shard_map/ppermute | solution.py:294
  4.0 9.4 %collective-permute-start.1 = (bf16[80,512]{1,0:T(8,128)(2,1)S(1)}, bf16[80,512]{1,0:T(8,128)(2,1)S(1)}, u32[]{:S(2)}, u32[]{:S(2)}) collective-permute-start(bf16[80,512]{1,0:T(8,128)(2,1)S(1)} %shard_map.64.packed.first.one), channel_id=1, source_target_pairs={{0,8},{4,12},{8,0},{12,4},{1,9},{5,13},{9,1},{13,5},{2,10},{6,14},... | collective-permute-start | bytes 245768 | tf_op jit(solution)/shard_map/ppermute | solution.py:294
  6.6 6.9 %collective-permute-start.2 = (bf16[80,512]{1,0:T(8,128)(2,1)S(1)}, bf16[80,512]{1,0:T(8,128)(2,1)S(1)}, u32[]{:S(2)}, u32[]{:S(2)}) collective-permute-start(bf16[80,512]{1,0:T(8,128)(2,1)S(1)} %shard_map.64.packed.first.one), channel_id=1, source_target_pairs={{0,12},{4,8},{8,4},{12,0},{1,13},{5,9},{9,5},{13,1},{2,14},{6,10},... | collective-permute-start | bytes 245768 | tf_op jit(solution)/shard_map/ppermute | solution.py:294
  13.5 1.9 %collective-permute-start.4 = (bf16[256,512]{1,0:T(8,128)(2,1)S(1)}, bf16[256,512]{1,0:T(8,128)(2,1)S(1)}, u32[]{:S(2)}, u32[]{:S(2)}) collective-permute-start(bf16[256,512]{1,0:T(8,128)(2,1)S(1)} %shard_map.66.near), channel_id=1, source_target_pairs={{0,1},{1,0},{2,3},{3,2},{4,5},{5,4},{6,7},{7,6},{8,9},{9,8},{10,11... | collective-permute-start | bytes 786440 | tf_op jit(solution)/shard_map/ppermute | solution.py:294
  13.6 12.7 %collective-permute-start.3 = (bf16[256,512]{1,0:T(8,128)(2,1)S(1)}, bf16[256,512]{1,0:T(8,128)(2,1)S(1)}, u32[]{:S(2)}, u32[]{:S(2)}) collective-permute-start(bf16[256,512]{1,0:T(8,128)(2,1)S(1)} %shard_map.66.near), channel_id=1, source_target_pairs={{0,2},{1,3},{2,0},{3,1},{4,6},{5,7},{6,4},{7,5},{8,10},{9,11},{10,... | collective-permute-start | bytes 786440 | tf_op jit(solution)/shard_map/ppermute | solution.py:294
  26.2 1.6 %collective-permute-start.5 = (bf16[256,512]{1,0:T(8,128)(2,1)S(1)}, bf16[256,512]{1,0:T(8,128)(2,1)S(1)}, u32[]{:S(2)}, u32[]{:S(2)}) collective-permute-start(bf16[256,512]{1,0:T(8,128)(2,1)S(1)} %collective-permute-done.3.near), channel_id=1, source_target_pairs={{0,1},{1,0},{2,3},{3,2},{4,5},{5,4},{6,7},{7,6},{8,9},{9,8},{10,11... | collective-permute-start | bytes 786440 | tf_op jit(solution)/shard_map/ppermute | solution.py:294
  39.6 1.6 %collective-permute-start.6 = (bf16[256,512]{1,0:T(8,128)(2,1)S(1)}, bf16[256,512]{1,0:T(8,128)(2,1)S(1)}, u32[]{:S(2)}, u32[]{:S(2)}) collective-permute-start(bf16[256,512]{1,0:T(8,128)(2,1)S(1)} %slice_bitcast_fusion.1), channel_id=1, source_target_pairs={{0,1},{1,0},{2,3},{3,2},{4,5},{5,4},{6,7},{7,6},{8,9},{9,8},{10,11... | collective-permute-start | bytes 786440 | tf_op jit(solution)/shard_map/ppermute | solution.py:294
  41.3 8.5 %collective-permute-start.7 = (bf16[256,512]{1,0:T(8,128)(2,1)S(1)}, bf16[256,512]{1,0:T(8,128)(2,1)S(1)}, u32[]{:S(2)}, u32[]{:S(2)}) collective-permute-start(bf16[256,512]{1,0:T(8,128)(2,1)S(1)} %fusion.1), channel_id=1, source_target_pairs={{0,2},{1,3},{2,0},{3,1},{4,6},{5,7},{6,4},{7,5},{8,10},{9,11},{10,... | collective-permute-start | bytes 786440 | tf_op jit(solution)/shard_map/ppermute | solution.py:294
  49.8 1.6 %collective-permute-start.8 = (bf16[256,512]{1,0:T(8,128)(2,1)S(1)}, bf16[256,512]{1,0:T(8,128)(2,1)S(1)}, u32[]{:S(2)}, u32[]{:S(2)}) collective-permute-start(bf16[256,512]{1,0:T(8,128)(2,1)S(1)} %slice_bitcast_fusion), channel_id=1, source_target_pairs={{0,1},{1,0},{2,3},{3,2},{4,5},{5,4},{6,7},{7,6},{8,9},{9,8},{10,11... | collective-permute-start | bytes 786440 | tf_op jit(solution)/shard_map/ppermute | solution.py:294
  51.5 8.3 %collective-permute-start.10 = (bf16[64,512]{1,0:T(8,128)(2,1)S(1)}, bf16[64,512]{1,0:T(8,128)(2,1)S(1)}, u32[]{:S(2)}, u32[]{:S(2)}) collective-permute-start(bf16[64,512]{1,0:T(8,128)(2,1)S(1)} %get-tuple-element.57), channel_id=1, source_target_pairs={{0,8},{4,12},{8,0},{12,4},{1,9},{5,13},{9,1},{13,5},{2,10},{6,14},... | collective-permute-start | bytes 196616 | tf_op jit(solution)/shard_map/ppermute | solution.py:294
  53.5 6.7 %collective-permute-start.11 = (bf16[64,512]{1,0:T(8,128)(2,1)S(1)}, bf16[64,512]{1,0:T(8,128)(2,1)S(1)}, u32[]{:S(2)}, u32[]{:S(2)}) collective-permute-start(bf16[64,512]{1,0:T(8,128)(2,1)S(1)} %get-tuple-element.56), channel_id=1, source_target_pairs={{0,12},{4,8},{8,4},{12,0},{1,13},{5,9},{9,5},{13,1},{2,14},{6,10},... | collective-permute-start | bytes 196616 | tf_op jit(solution)/shard_map/ppermute | solution.py:294
  55.3 5.7 %collective-permute-start.9 = (bf16[64,512]{1,0:T(8,128)(2,1)S(1)}, bf16[64,512]{1,0:T(8,128)(2,1)S(1)}, u32[]{:S(2)}, u32[]{:S(2)}) collective-permute-start(bf16[64,512]{1,0:T(8,128)(2,1)S(1)} %get-tuple-element.55), channel_id=1, source_target_pairs={{0,4},{4,0},{8,12},{12,8},{1,5},{5,1},{9,13},{13,9},{2,6},{6,2},{1... | collective-permute-start | bytes 196616 | tf_op jit(solution)/shard_map/ppermute | solution.py:294

commit v5 on v4

--- a/solution.py
+++ b/solution.py
@@ -91,25 +91,30 @@
 
 
 def pack_kernel(tokens, ids_there, weights_there, out, table, ids, weights, sems):
-    nrows = tokens.shape[0]
+    share = tokens.shape[1]
+    wide = out.shape[1] - table.shape[1]
     copies = [
         pltpu.make_async_copy(ids_there, ids, sems.at[0]),
         pltpu.make_async_copy(weights_there, weights, sems.at[1]),
-        pltpu.make_async_copy(tokens, out.at[:nrows], sems.at[2]),
     ]
+    for j in range(wide // share):
+        tile = tokens.at[j * TILE : (j + 1) * TILE]
+        copies.append(pltpu.make_async_copy(tile, out.at[:, j * share : (j + 1) * share], sems.at[2 + j]))
     for copy in copies:
         copy.start()
     table[...] = jnp.zeros_like(table)
-    for copy in copies[:2]:
-        copy.wait()
+    wait_all(copies[:2])
     picks, steps, step_rows = ids.shape
+    half = steps * step_rows
     for s in range(steps):
         high = weights[:, s, :].astype(jnp.bfloat16).astype(jnp.float32)
         low = weights[:, s, :] - high
-        for c, part in enumerate((ids[:, s, :].astype(jnp.float32), high, low)):
-            table[:picks, c * 128 + s * step_rows : c * 128 + (s + 1) * step_rows] = part
-    out[nrows:, :] = table[...].astype(jnp.bfloat16)
-    copies[2].wait()
+        at = s * step_rows
+        table[:picks, at : at + step_rows] = ids[:, s, :].astype(jnp.float32)
+        table[8 : 8 + picks, at : at + step_rows] = high
+        table[:picks, half + at : half + at + step_rows] = low
+    out[:, wide:] = table[...].astype(jnp.bfloat16)
+    wait_all(copies[2:])
 
 
 def early_kernel(place, packed, wg, wu, first_g, first_u, sems):
@@ -121,18 +126,22 @@
 
 
 def join_kernel(first, second, third, fourth, out):
+    share = out.shape[1]
     block = out.shape[0] // 4
-    for j, piece in enumerate((first, second, third, fourth)):
-        out[j * block : (j + 1) * block, :] = piece[:block, :]
+    for i, piece in enumerate((first, second, third, fourth)):
+        for j in range(block // TILE):
+            out[i * block + j * TILE : i * block + (j + 1) * TILE, :] = piece[:, j * share : (j + 1) * share]
 
 
 def route(place, pieces, picks, slots, residents, table, pick_mat, slot_weight):
-    block = pieces[0].shape[0] - TILE
-    rows = block * len(pieces)
+    rows = table.shape[1]
+    block = rows // len(pieces)
     for j, piece in enumerate(pieces):
-        for c in range(3):
-            part = piece[block:, c * 128 : c * 128 + block].astype(jnp.float32)
-            table[c * TILE : (c + 1) * TILE, j * block : (j + 1) * block] = part
+        packed = piece[:, piece.shape[1] - 2 * block :].astype(jnp.float32)
+        here = slice(j * block, (j + 1) * block)
+        table[:8, here] = packed[:8, :block]
+        table[TILE : TILE + 8, here] = packed[8:, :block]
+        table[2 * TILE : 2 * TILE + 8, here] = packed[:8, block:]
     labels = (place[0] + lax.broadcasted_iota(jnp.int32, (residents, rows), 0)).astype(jnp.float32)
     chosen = jnp.zeros((residents, rows), jnp.float32)
     weight = jnp.zeros((residents, rows), jnp.float32)
@@ -225,7 +234,7 @@
         gate[mine, :] = dot(x, g_block, NT)
         up[mine, :] = dot(x, u_block, NT)
 
-    in_groups(0, held, slots, lambda e, mine: work(e, mine, first_g[e], first_u[e]), size=GROUP)
+    in_groups(0, held, slots, lambda e, mine: work(e, mine, first_g[e], first_u[e]), size=3)
     wait_all(copies)
     in_groups(held, residents, slots, lambda e, mine: work(e, mine, bg[e - held], bu[e - held]), size=GROUP)
     wait_all(early)
@@ -255,7 +264,7 @@
             copy.wait()
 
     in_groups(0, held, slots, lambda e, mine: work(e, mine, next_g[e], next_u[e]), lower)
-    in_groups(held, residents, slots, lambda e, mine: work(e, mine, bg[e - held], bu[e - held]), lower, arrive)
+    in_groups(held, residents, slots, lambda e, mine: work(e, mine, bg[e - held], bu[e - held]), lower, arrive, 3)
     add_up(place, pick_back, given, out)
 
 
@@ -311,12 +320,12 @@
         pack_kernel,
         tuple(there(a) for a in sources),
         3,
-        shape((block + TILE, share), jnp.bfloat16),
+        shape((TILE, block // TILE * share + 2 * block), jnp.bfloat16),
         [
-            pltpu.VMEM((TILE, share), jnp.float32),
+            pltpu.VMEM((TILE, 2 * block), jnp.float32),
             pltpu.VMEM((picks, steps, nrows), jnp.int32),
             pltpu.VMEM((picks, steps, nrows), jnp.float32),
-            pltpu.SemaphoreType.DMA((3,)),
+            pltpu.SemaphoreType.DMA((2 + block // TILE,)),
         ],
         1,
         2,
@@ -375,7 +384,8 @@
 def pick_plan(*arrays):
     holders, splits = lax.axis_size("expert"), lax.axis_size("tensor")
     residents = arrays[3].shape[0]
-    small = holders == 4 and splits == 4 and residents == 16
+    block = arrays[0].shape[0] * arrays[0].shape[1]
+    small = holders == 4 and splits == 4 and residents == 16 and block == 64
     return (small_group if small else per_device)(*arrays)
 
 

time: 61.8 us -> 61.6 us (level)
  transfers between devices with their start and end apart: 12 -> 12, of which waited for: 7 -> 6; matrix products, arithmetic and copies ran while one was open for 0% -> 0% of each run, Pallas kernels for 38% -> 39%
where the time goes in v5:
time: 61.6 us; the launch traced here: 61.3 us
  Pallas kernels  35.9 us (58%)
  starting transfers between devices  13.9 us (23%)
  waiting for transfers between devices  10.4 us (17%)
  other arithmetic  0.9 us (1%)
    pallas_call x6, Pallas kernels, call(): pl.pallas_call(kernel, in_specs=specs + [there] * fetched, out_specs=jax....  35.9 us
    ppermute x12, starting transfers between devices, swap(): return lax.ppermute(a, axis, [(i, i ^ bits) for i in range(n)])  13.9 us
    ppermute x12, waiting for transfers between devices, swap(): return lax.ppermute(a, axis, [(i, i ^ bits) for i in range(n)])  10.4 us
  transfers between devices with their start and end apart: 12, of which 6 were waited for; matrix products, arithmetic and copies ran while one was open for 0% of the time, Pallas kernels for 39%

profile of v5, /device:TPU:0, one launch (start us, length us, event | category | flops | bytes accessed | tf_op | source)
XLA Modules:
  0.0 61.3 jit_solution(12159044483948321363)
XLA Ops:
  0.0 0.9 %shard_map.64.packed.first.one = bf16[16,2176]{1,0:T(8,128)(2,1)S(1)} custom-call(bf16[64,512]{1,0:T(8,128)(2,1)} %bitcast.25, s32[6,2,32]{2,1,0:T(2,128)} %bitcast.26, f32[6,2,32]{2,1,0:T(2,128)} %bitcast.27), custom_call_target="tpu_custom_call" | custom-call | flops 1000000000 | bytes 3000000 | tf_op jit(solution)/shard_map/pallas_call | solution.py:290
  0.9 3.1 %collective-permute-start = (bf16[16,2176]{1,0:T(8,128)(2,1)S(1)}, bf16[16,2176]{1,0:T(8,128)(2,1)S(1)}, u32[]{:S(2)}, u32[]{:S(2)}) collective-permute-start(bf16[16,2176]{1,0:T(8,128)(2,1)S(1)} %shard_map.64.packed.first.one), channel_id=1, source_target_pairs={{0,4},{4,0},{8,12},{12,8},{1,5},{5,1},{9,13},{13,9},{2,6},{6,2},{1... | collective-permute-start | bytes 208904 | tf_op jit(solution)/shard_map/ppermute | solution.py:303
  4.0 2.6 %collective-permute-start.1 = (bf16[16,2176]{1,0:T(8,128)(2,1)S(1)}, bf16[16,2176]{1,0:T(8,128)(2,1)S(1)}, u32[]{:S(2)}, u32[]{:S(2)}) collective-permute-start(bf16[16,2176]{1,0:T(8,128)(2,1)S(1)} %shard_map.64.packed.first.one), channel_id=1, source_target_pairs={{0,8},{4,12},{8,0},{12,4},{1,9},{5,13},{9,1},{13,5},{2,10},{6,14},... | collective-permute-start | bytes 208904 | tf_op jit(solution)/shard_map/ppermute | solution.py:303
  6.5 0.0 collective-permute-start.2
  6.5 0.1 pad_add_fusion.place
  6.6 6.7 %shard_map.65 = (bf16[12,352,1024]{2,1,0:T(8,128)(2,1)S(1)}, bf16[12,352,1024]{2,1,0:T(8,128)(2,1)S(1)}) custom-call(s32[2]{0:T(128)S(1)} %pad_add_fusion.place, bf16[16,2176]{1,0:T(8,128)(2,1)S(1)} %shard_map.64.packed.first.one, bf16[16,352,2048]{2,1,0:T(8,128)(2,1)} %bitcast.19, bf16[16,352,2048]{2,1,0:T(8,128)(2,1)} %bitcast.22), custom_call_target="tpu_custom_call" | custom-call | flops 7000000000 | bytes 21000000 | tf_op jit(solution)/shard_map/pallas_call | solution.py:290
  13.4 0.0 collective-permute-done.second.two
  13.4 0.0 collective-permute-done.1.third.three
  13.4 0.0 collective-permute-done.2.fourth.four
  13.4 0.1 collective-permute-start.4
  13.5 1.8 %collective-permute-start.3 = (bf16[256,512]{1,0:T(8,128)(2,1)S(1)}, bf16[256,512]{1,0:T(8,128)(2,1)S(1)}, u32[]{:S(2)}, u32[]{:S(2)}) collective-permute-start(bf16[256,512]{1,0:T(8,128)(2,1)S(1)} %shard_map.66.near), channel_id=1, source_target_pairs={{0,2},{1,3},{2,0},{3,1},{4,6},{5,7},{6,4},{7,5},{8,10},{9,11},{10,... | collective-permute-start | bytes 786440 | tf_op jit(solution)/shard_map/ppermute | solution.py:303
  15.3 0.0 collective-permute-done.4.far
  15.3 11.0 %shard_map.67 = (bf16[768,256]{1,0:T(8,128)(2,1)S(1)}, bf16[256,768]{1,0:T(8,128)(2,1)S(1)}, f32[768,128]{1,0:T(8,128)S(1)}, f32[768,352]{1,0:T(8,128)S(1)}, f32...) custom-call(s32[2]{0:T(128)S(1)} %pad_add_fusion.place, ...), custom_call_target="tpu_custom_call" | custom-call | flops 8999999488 | bytes 27000000 | tf_op jit(solution)/shard_map/pallas_call | solution.py:290
  26.3 0.0 collective-permute-done.3.near
  26.4 0.2 collective-permute-start.5
  26.6 1.4 %collective-permute-done.5.far = bf16[256,512]{1,0:T(8,128)(2,1)S(1)} collective-permute-done((bf16[256,512]{1,0:T(8,128)(2,1)S(1)}, bf16[256,512]{1,0:T(8,128)(2,1)S(1)}, u32[]{:S(2)}, u32[]{:S(2)}) %collective-permute-start.5) | collective-permute-done | bytes 262176 | tf_op jit(solution)/shard_map/ppermute | solution.py:303
  28.0 11.4 %shard_map.68 = (bf16[768,352]{1,0:T(8,128)(2,1)S(1)}, bf16[2,256,512]{2,1,0:T(8,128)(2,1)S(1)}) custom-call(s32[2]{0:T(128)S(1)} %pad_add_fusion.place, bf16[256,512]{1,0:T(8,128)(2,1)S(1)} %collective-permute-done.3.near, bf16[256,512]{1,0:T(8,128)(2,1)S(1)} %collective-permute-done.5.far, bf16[768,256]{1,0:T(8,128)(2,1)S(1)} %get-tuple-element.39.pick_mat, ...), custom_call_target="tpu_custom_call" | custom-call | flops 12000000000 | bytes 36000000 | tf_op jit(solution)/shard_map/pallas_call | solution.py:290
  39.4 0.2 collective-permute-start.6
  39.6 1.4 %collective-permute-done.6 = bf16[256,512]{1,0:T(8,128)(2,1)S(1)} collective-permute-done((bf16[256,512]{1,0:T(8,128)(2,1)S(1)}, bf16[256,512]{1,0:T(8,128)(2,1)S(1)}, u32[]{:S(2)}, u32[]{:S(2)}) %collective-permute-start.6) | collective-permute-done | bytes 262176 | tf_op jit(solution)/shard_map/ppermute | solution.py:303
  41.0 0.1 fusion.1
  41.0 1.6 %collective-permute-start.7 = (bf16[256,512]{1,0:T(8,128)(2,1)S(1)}, bf16[256,512]{1,0:T(8,128)(2,1)S(1)}, u32[]{:S(2)}, u32[]{:S(2)}) collective-permute-start(bf16[256,512]{1,0:T(8,128)(2,1)S(1)} %fusion.1), channel_id=1, source_target_pairs={{0,2},{1,3},{2,0},{3,1},{4,6},{5,7},{6,4},{7,5},{8,10},{9,11},{10,... | collective-permute-start | bytes 786440 | tf_op jit(solution)/shard_map/ppermute | solution.py:303
  42.6 5.9 %shard_map.69 = bf16[2,256,512]{2,1,0:T(8,128)(2,1)S(1)} custom-call(s32[2]{0:T(128)S(1)} %pad_add_fusion.place, bf16[768,352]{1,0:T(8,128)(2,1)S(1)} %get-tuple-element.49.hidden, bf16[256,768]{1,0:T(8,128)(2,1)S(1)} %get-tuple-element.40.pick_back, bf16[16,352,2048]{2,1,0:T(8,128)(2,1)} %wd.3), custom_call_target="tpu_custom_call" | custom-call | flops 5000000000 | bytes 15000000 | tf_op jit(solution)/shard_map/pallas_call | solution.py:290
  48.5 1.0 %collective-permute-done.7 = bf16[256,512]{1,0:T(8,128)(2,1)S(1)} collective-permute-done((bf16[256,512]{1,0:T(8,128)(2,1)S(1)}, bf16[256,512]{1,0:T(8,128)(2,1)S(1)}, u32[]{:S(2)}, u32[]{:S(2)}) %collective-permute-start.7) | collective-permute-done | bytes 262176 | tf_op jit(solution)/shard_map/ppermute | solution.py:303
  49.5 0.1 collective-permute-start.8
  49.6 1.5 %collective-permute-done.8 = bf16[256,512]{1,0:T(8,128)(2,1)S(1)} collective-permute-done((bf16[256,512]{1,0:T(8,128)(2,1)S(1)}, bf16[256,512]{1,0:T(8,128)(2,1)S(1)}, u32[]{:S(2)}, u32[]{:S(2)}) %collective-permute-start.8) | collective-permute-done | bytes 262176 | tf_op jit(solution)/shard_map/ppermute | solution.py:303
  51.1 0.1 fusion.5
  51.2 1.8 %collective-permute-start.10 = (bf16[64,512]{1,0:T(8,128)(2,1)S(1)}, bf16[64,512]{1,0:T(8,128)(2,1)S(1)}, u32[]{:S(2)}, u32[]{:S(2)}) collective-permute-start(bf16[64,512]{1,0:T(8,128)(2,1)S(1)} %get-tuple-element.57), channel_id=1, source_target_pairs={{0,8},{4,12},{8,0},{12,4},{1,9},{5,13},{9,1},{13,5},{2,10},{6,14},... | collective-permute-start | bytes 196616 | tf_op jit(solution)/shard_map/ppermute | solution.py:303
  53.0 2.0 %collective-permute-start.11 = (bf16[64,512]{1,0:T(8,128)(2,1)S(1)}, bf16[64,512]{1,0:T(8,128)(2,1)S(1)}, u32[]{:S(2)}, u32[]{:S(2)}) collective-permute-start(bf16[64,512]{1,0:T(8,128)(2,1)S(1)} %get-tuple-element.56), channel_id=1, source_target_pairs={{0,12},{4,8},{8,4},{12,0},{1,13},{5,9},{9,5},{13,1},{2,14},{6,10},... | collective-permute-start | bytes 196616 | tf_op jit(solution)/shard_map/ppermute | solution.py:303
  55.0 0.5 collective-permute-start.9
  55.5 4.3 %collective-permute-done.10 = bf16[64,512]{1,0:T(8,128)(2,1)S(1)} collective-permute-done((bf16[64,512]{1,0:T(8,128)(2,1)S(1)}, bf16[64,512]{1,0:T(8,128)(2,1)S(1)}, u32[]{:S(2)}, u32[]{:S(2)}) %collective-permute-start.10) | collective-permute-done | bytes 65568 | tf_op jit(solution)/shard_map/ppermute | solution.py:303
  59.8 0.0 collective-permute-done.11
  59.8 0.9 %collective-permute-done.9 = bf16[64,512]{1,0:T(8,128)(2,1)S(1)} collective-permute-done((bf16[64,512]{1,0:T(8,128)(2,1)S(1)}, bf16[64,512]{1,0:T(8,128)(2,1)S(1)}, u32[]{:S(2)}, u32[]{:S(2)}) %collective-permute-start.9) | collective-permute-done | bytes 65568 | tf_op jit(solution)/shard_map/ppermute | solution.py:303
  60.6 0.7 %fusion.4 = bf16[64,512]{1,0:T(8,128)(2,1)} fusion(f32[256,512]{1,0:T(8,128)S(1)} %get-tuple-element.54, bf16[64,512]{1,0:T(8,128)(2,1)S(1)} %collective-permute-done.11, bf16[64,512]{1,0:T(8,128)(2,1)S(1)} %collective-permute-done.10, bf16[64,512]{1,0:T(8,128)(2,1)S(1)} %collective-permute-done.9), kind=kLoop, calls=%fused_computation.9 | loop fusion | flops 229376 | bytes 393216 | tf_op jit(solution)/shard_map/convert_element_type | solution.py:381
  (4 shorter events, 0.1 us)
Async XLA Ops:
  0.9 12.5 %collective-permute-start = (bf16[16,2176]{1,0:T(8,128)(2,1)S(1)}, bf16[16,2176]{1,0:T(8,128)(2,1)S(1)}, u32[]{:S(2)}, u32[]{:S(2)}) collective-permute-start(bf16[16,2176]{1,0:T(8,128)(2,1)S(1)} %shard_map.64.packed.first.one), channel_id=1, source_target_pairs={{0,4},{4,0},{8,12},{12,8},{1,5},{5,1},{9,13},{13,9},{2,6},{6,2},{1... | collective-permute-start | bytes 208904 | tf_op jit(solution)/shard_map/ppermute | solution.py:303
  4.0 9.4 %collective-permute-start.1 = (bf16[16,2176]{1,0:T(8,128)(2,1)S(1)}, bf16[16,2176]{1,0:T(8,128)(2,1)S(1)}, u32[]{:S(2)}, u32[]{:S(2)}) collective-permute-start(bf16[16,2176]{1,0:T(8,128)(2,1)S(1)} %shard_map.64.packed.first.one), channel_id=1, source_target_pairs={{0,8},{4,12},{8,0},{12,4},{1,9},{5,13},{9,1},{13,5},{2,10},{6,14},... | collective-permute-start | bytes 208904 | tf_op jit(solution)/shard_map/ppermute | solution.py:303
  6.5 6.9 %collective-permute-start.2 = (bf16[16,2176]{1,0:T(8,128)(2,1)S(1)}, bf16[16,2176]{1,0:T(8,128)(2,1)S(1)}, u32[]{:S(2)}, u32[]{:S(2)}) collective-permute-start(bf16[16,2176]{1,0:T(8,128)(2,1)S(1)} %shard_map.64.packed.first.one), channel_id=1, source_target_pairs={{0,12},{4,8},{8,4},{12,0},{1,13},{5,9},{9,5},{13,1},{2,14},{6,10},... | collective-permute-start | bytes 208904 | tf_op jit(solution)/shard_map/ppermute | solution.py:303
  13.4 1.9 %collective-permute-start.4 = (bf16[256,512]{1,0:T(8,128)(2,1)S(1)}, bf16[256,512]{1,0:T(8,128)(2,1)S(1)}, u32[]{:S(2)}, u32[]{:S(2)}) collective-permute-start(bf16[256,512]{1,0:T(8,128)(2,1)S(1)} %shard_map.66.near), channel_id=1, source_target_pairs={{0,1},{1,0},{2,3},{3,2},{4,5},{5,4},{6,7},{7,6},{8,9},{9,8},{10,11... | collective-permute-start | bytes 786440 | tf_op jit(solution)/shard_map/ppermute | solution.py:303
  13.5 12.8 %collective-permute-start.3 = (bf16[256,512]{1,0:T(8,128)(2,1)S(1)}, bf16[256,512]{1,0:T(8,128)(2,1)S(1)}, u32[]{:S(2)}, u32[]{:S(2)}) collective-permute-start(bf16[256,512]{1,0:T(8,128)(2,1)S(1)} %shard_map.66.near), channel_id=1, source_target_pairs={{0,2},{1,3},{2,0},{3,1},{4,6},{5,7},{6,4},{7,5},{8,10},{9,11},{10,... | collective-permute-start | bytes 786440 | tf_op jit(solution)/shard_map/ppermute | solution.py:303
  26.4 1.6 %collective-permute-start.5 = (bf16[256,512]{1,0:T(8,128)(2,1)S(1)}, bf16[256,512]{1,0:T(8,128)(2,1)S(1)}, u32[]{:S(2)}, u32[]{:S(2)}) collective-permute-start(bf16[256,512]{1,0:T(8,128)(2,1)S(1)} %collective-permute-done.3.near), channel_id=1, source_target_pairs={{0,1},{1,0},{2,3},{3,2},{4,5},{5,4},{6,7},{7,6},{8,9},{9,8},{10,11... | collective-permute-start | bytes 786440 | tf_op jit(solution)/shard_map/ppermute | solution.py:303
  39.4 1.6 %collective-permute-start.6 = (bf16[256,512]{1,0:T(8,128)(2,1)S(1)}, bf16[256,512]{1,0:T(8,128)(2,1)S(1)}, u32[]{:S(2)}, u32[]{:S(2)}) collective-permute-start(bf16[256,512]{1,0:T(8,128)(2,1)S(1)} %slice_bitcast_fusion.1), channel_id=1, source_target_pairs={{0,1},{1,0},{2,3},{3,2},{4,5},{5,4},{6,7},{7,6},{8,9},{9,8},{10,11... | collective-permute-start | bytes 786440 | tf_op jit(solution)/shard_map/ppermute | solution.py:303
  41.0 8.5 %collective-permute-start.7 = (bf16[256,512]{1,0:T(8,128)(2,1)S(1)}, bf16[256,512]{1,0:T(8,128)(2,1)S(1)}, u32[]{:S(2)}, u32[]{:S(2)}) collective-permute-start(bf16[256,512]{1,0:T(8,128)(2,1)S(1)} %fusion.1), channel_id=1, source_target_pairs={{0,2},{1,3},{2,0},{3,1},{4,6},{5,7},{6,4},{7,5},{8,10},{9,11},{10,... | collective-permute-start | bytes 786440 | tf_op jit(solution)/shard_map/ppermute | solution.py:303
  49.5 1.6 %collective-permute-start.8 = (bf16[256,512]{1,0:T(8,128)(2,1)S(1)}, bf16[256,512]{1,0:T(8,128)(2,1)S(1)}, u32[]{:S(2)}, u32[]{:S(2)}) collective-permute-start(bf16[256,512]{1,0:T(8,128)(2,1)S(1)} %slice_bitcast_fusion), channel_id=1, source_target_pairs={{0,1},{1,0},{2,3},{3,2},{4,5},{5,4},{6,7},{7,6},{8,9},{9,8},{10,11... | collective-permute-start | bytes 786440 | tf_op jit(solution)/shard_map/ppermute | solution.py:303
  51.2 8.5 %collective-permute-start.10 = (bf16[64,512]{1,0:T(8,128)(2,1)S(1)}, bf16[64,512]{1,0:T(8,128)(2,1)S(1)}, u32[]{:S(2)}, u32[]{:S(2)}) collective-permute-start(bf16[64,512]{1,0:T(8,128)(2,1)S(1)} %get-tuple-element.57), channel_id=1, source_target_pairs={{0,8},{4,12},{8,0},{12,4},{1,9},{5,13},{9,1},{13,5},{2,10},{6,14},... | collective-permute-start | bytes 196616 | tf_op jit(solution)/shard_map/ppermute | solution.py:303
  53.0 6.8 %collective-permute-start.11 = (bf16[64,512]{1,0:T(8,128)(2,1)S(1)}, bf16[64,512]{1,0:T(8,128)(2,1)S(1)}, u32[]{:S(2)}, u32[]{:S(2)}) collective-permute-start(bf16[64,512]{1,0:T(8,128)(2,1)S(1)} %get-tuple-element.56), channel_id=1, source_target_pairs={{0,12},{4,8},{8,4},{12,0},{1,13},{5,9},{9,5},{13,1},{2,14},{6,10},... | collective-permute-start | bytes 196616 | tf_op jit(solution)/shard_map/ppermute | solution.py:303
  55.0 5.7 %collective-permute-start.9 = (bf16[64,512]{1,0:T(8,128)(2,1)S(1)}, bf16[64,512]{1,0:T(8,128)(2,1)S(1)}, u32[]{:S(2)}, u32[]{:S(2)}) collective-permute-start(bf16[64,512]{1,0:T(8,128)(2,1)S(1)} %get-tuple-element.55), channel_id=1, source_target_pairs={{0,4},{4,0},{8,12},{12,8},{1,5},{5,1},{9,13},{13,9},{2,6},{6,2},{1... | collective-permute-start | bytes 196616 | tf_op jit(solution)/shard_map/ppermute | solution.py:303

commit v6 on v5

--- a/solution.py
+++ b/solution.py
@@ -193,14 +193,6 @@
         taken[:, pl.ds(pl.multiple_of(column * share, share), share)] = rows
 
 
-def add_up(place, pick_back, given, out):
-    share = out.shape[2]
-    low = place[1] & 1
-    for j, column in enumerate((low, 1 - low)):
-        block = given[:, pl.ds(pl.multiple_of(column * share, share), share)]
-        out[j] = dot(pick_back[...], block, NN).astype(jnp.bfloat16)
-
-
 def in_groups(first, last, slots, work, after=None, arrive=None, size=2):
     def some(step, carry):
         group = [first + step * size + g for g in range(size)]
@@ -222,7 +214,17 @@
     residents = held + bg.shape[0]
     later = far_pair(place, bg)
     copies = fetches((wg, wu), (bg, bu), sems, near_pair(place, bg), held)
-    early = fetches((wd,), (down,), ahead.at[2:], later, 0) + fetches((wg, wu), (next_g, next_u), ahead, later, 0)
+    share = near.shape[1]
+    early = [
+        pltpu.make_async_copy(
+            wd.at[e, :, pl.ds(pl.multiple_of((place[1] ^ (3 - 2 * j)) * share, share), share)],
+            down.at[e, :, j * share : (j + 1) * share],
+            ahead.at[2 + j, e],
+        )
+        for e in range(residents)
+        for j in range(2)
+    ]
+    early = early + fetches((wg, wu), (next_g, next_u), ahead, later, 0)
     for copy in copies + early:
         copy.start()
     route(place, (one, two, three, four), TOPK, slots, residents, table, pick_mat, slot_weight)
@@ -241,11 +243,13 @@
 
 
 def rest_kernel(slots, place, near, far, pick_mat, pick_back, slot_weight, gate, up, down, next_g, next_u, *rest):
-    wg, wu, hidden, out, taken, given, bg, bu, sems = rest
+    wg, wu, wd, hidden, out, away_down, taken, given, bg, bu, sems, ahead = rest
     held = next_g.shape[0]
     residents = held + bg.shape[0]
-    copies = fetches((wg, wu), (bg, bu), sems, far_pair(place, bg), held)
-    for copy in copies:
+    share = out.shape[2]
+    away_columns = pl.multiple_of((place[1] ^ 2) * share, share)
+    early = fetches((wd,), (away_down,), ahead, away_columns, 0)
+    for copy in fetches((wg, wu), (bg, bu), sems, far_pair(place, bg), held) + early:
         copy.start()
     place_rows(place, pick_mat, near, far, taken)
 
@@ -260,28 +264,38 @@
         given[mine, :] = dot(hidden[mine, :], down[e], NN).astype(jnp.bfloat16)
 
     def arrive(e):
-        for copy in fetches((wg, wu), (bg, bu), sems, far_pair(place, bg), held, e - held):
-            copy.wait()
+        wait_all(fetches((wg, wu), (bg, bu), sems, far_pair(place, bg), held, e - held))
 
     in_groups(0, held, slots, lambda e, mine: work(e, mine, next_g[e], next_u[e]), lower)
     in_groups(held, residents, slots, lambda e, mine: work(e, mine, bg[e - held], bu[e - held]), lower, arrive, 3)
-    add_up(place, pick_back, given, out)
-
-
-def down_kernel(slots, place, hidden, pick_back, wd, out, given, bd, sems):
-    copies = fetches((wd,), (bd,), sems, near_pair(place, bd), 0)
-    for copy in copies:
+    wait_all(early)
+    for j in range(2):
+        out[j] = dot(pick_back[...], given[:, j * share : (j + 1) * share], NN).astype(jnp.bfloat16)
+
+
+def lower_kernel(slots, place, hidden, pick_back, down, out, given):
+    def lower(e, mine):
+        given[mine, :] = dot(hidden[mine, :], down[e], NN).astype(jnp.bfloat16)
+
+    in_groups(0, down.shape[0], slots, lower, size=4)
+    out[...] = dot(pick_back[...], given[...], NN).astype(jnp.bfloat16)
+
+
+def own_kernel(slots, place, hidden, pick_back, wd, out, given, down, sems):
+    share = out.shape[1]
+    column = pl.multiple_of(place[1] * share, share)
+    for copy in fetches((wd,), (down,), sems, column, 0):
         copy.start()
 
     def arrive(e):
-        for copy in fetches((wd,), (bd,), sems, near_pair(place, bd), 0, e):
+        for copy in fetches((wd,), (down,), sems, column, 0, e):
             copy.wait()
 
     def lower(e, mine):
-        given[mine, :] = dot(hidden[mine, :], bd[e], NN).astype(jnp.bfloat16)
-
-    in_groups(0, bd.shape[0], slots, lower, None, arrive)
-    add_up(place, pick_back, given, out)
+        given[mine, :] = dot(hidden[mine, :], down[e], NN).astype(jnp.bfloat16)
+
+    in_groups(0, down.shape[0], slots, lower, None, arrive)
+    out[...] = dot(pick_back[...], given[...], NN).astype(jnp.bfloat16)
 
 
 def call(kernel, args, fetched, outs, scratch, micros, room):
@@ -343,37 +357,46 @@
     across = swap(own, "tensor", 2)
     pick_mat, pick_back = shape((total, rows), jnp.bfloat16), shape((rows, total), jnp.bfloat16)
     slot_weight, part = shape((total, 128), jnp.float32), shape((total, units), jnp.float32)
-    hidden, parts = shape((total, units), jnp.bfloat16), shape((2, rows, share), jnp.bfloat16)
+    hidden, part_out = shape((total, units), jnp.bfloat16), shape((rows, share), jnp.bfloat16)
     taken = pltpu.VMEM((total, 2 * share), jnp.bfloat16)
     pick_mat, pick_back, slot_weight, gate, up, down, *next_pair = call(
         functools.partial(half_kernel, slots),
         (place, own, core) + pieces + tuple(first_pair) + (wg, wu, wd),
         3,
         (pick_mat, pick_back, slot_weight, part, part, several(residents), several(FIRST), several(FIRST)),
-        [taken, pltpu.VMEM((3 * TILE, rows), jnp.float32), scratch(FIRST), scratch(FIRST), sems(2), sems(3)],
+        [taken, pltpu.VMEM((3 * TILE, rows), jnp.float32), scratch(FIRST), scratch(FIRST), sems(2), sems(4)],
         9,
-        10,
+        8,
     )
     across_late, gate = lax.optimization_barrier((across, gate))
     across_core = swap(across_late, "tensor", 1)
-    hidden, away_parts = call(
+    given = pltpu.VMEM((total, share), jnp.bfloat16)
+    narrow = pltpu.VMEM((residents, units, share), jnp.bfloat16)
+    hidden, core_parts, away_down = call(
         functools.partial(rest_kernel, slots),
-        (place, across, across_core, pick_mat, pick_back, slot_weight, gate, up, down, *next_pair, wg, wu),
-        2,
-        (hidden, parts),
-        [taken, taken, scratch(first), scratch(first), sems(2)],
+        (place, across, across_core, pick_mat, pick_back, slot_weight, gate, up, down, *next_pair, wg, wu, wd),
+        3,
+        (hidden, shape((2, rows, share), jnp.bfloat16), shape((residents, units, share), jnp.bfloat16)),
+        [taken, taken, scratch(first), scratch(first), sems(2), sems(1)],
         12,
-        24,
+        21,
     )
     wide = lambda a: a.astype(jnp.float32)
-    away = (wide(away_parts[0]) + wide(swap(away_parts[1], "tensor", 1))).astype(jnp.bfloat16)
+    came_core = swap(core_parts, "tensor", 1)
+    away = call(functools.partial(lower_kernel, slots), (place, hidden, pick_back, away_down), 0, part_out, [given], 3, 3)
+    away = (wide(away) + wide(came_core[0])).astype(jnp.bfloat16)
     away, hidden = lax.optimization_barrier((away, hidden))
     back = swap(away, "tensor", 2)
-    home_parts = call(
-        functools.partial(down_kernel, slots), (place, hidden, pick_back, wd), 1, parts, [taken, scratch(residents), sems(1)], 5, 16
-    )
-    home_parts, back = lax.optimization_barrier((home_parts, back))
-    home = wide(home_parts[0]) + wide(swap(home_parts[1], "tensor", 1)) + wide(back)
+    home = call(
+        functools.partial(own_kernel, slots),
+        (place, hidden, pick_back, wd),
+        1,
+        part_out,
+        [given, narrow, sems(1)],
+        4,
+        8,
+    )
+    home = wide(home) + wide(came_core[1]) + wide(back)
     home = home.reshape(holders, block, share)
     sent = home.astype(jnp.bfloat16)
     came = {k: swap(sent[k], "expert", k) for k in (3, 2, 1)}

time: 61.6 us -> 61.1 us (level)
  waiting for transfers between devices: 10.4 us -> 8.75 us
  Pallas kernels: 35.9 us -> 36.9 us
    ppermute x12 -> x11, waiting for transfers between devices: 10.4 us -> 8.75 us  [swap(): return lax.ppermute(a, axis, [(i, i ^ bits) for i in range(n)])]
    pallas_call x6 -> x7, Pallas kernels: 35.9 us -> 36.9 us  [call(): pl.pallas_call(kernel, in_specs=specs + [there] * fetched, out_specs=jax....]
    ppermute x12 -> x11, starting transfers between devices: 13.9 us -> 14.1 us  [swap(): return lax.ppermute(a, axis, [(i, i ^ bits) for i in range(n)])]
  transfers between devices with their start and end apart: 12 -> 11, of which waited for: 6 -> 5; matrix products, arithmetic and copies ran while one was open for 0% -> 0% of each run, Pallas kernels for 39% -> 40%
where the time goes in v6:
time: 61.1 us; the launch traced here: 60.7 us
  Pallas kernels  36.9 us (60%)
  starting transfers between devices  14.1 us (23%)
  waiting for transfers between devices  8.75 us (14%)
  other arithmetic  0.9 us (1%)
    pallas_call x7, Pallas kernels, call(): pl.pallas_call(kernel, in_specs=specs + [there] * fetched, out_specs=jax....  36.9 us
    ppermute x11, starting transfers between devices, swap(): return lax.ppermute(a, axis, [(i, i ^ bits) for i in range(n)])  14.1 us
    ppermute x11, waiting for transfers between devices, swap(): return lax.ppermute(a, axis, [(i, i ^ bits) for i in range(n)])  8.75 us
  transfers between devices with their start and end apart: 11, of which 5 were waited for; matrix products, arithmetic and copies ran while one was open for 0% of the time, Pallas kernels for 40%

profile of v6, /device:TPU:0, one launch (start us, length us, event | category | flops | bytes accessed | tf_op | source)
XLA Modules:
  0.0 60.7 jit_solution(5162957114207213890)
XLA Ops:
  0.0 0.9 %shard_map.64.packed.first.one = bf16[16,2176]{1,0:T(8,128)(2,1)S(1)} custom-call(bf16[64,512]{1,0:T(8,128)(2,1)} %bitcast.25, s32[6,2,32]{2,1,0:T(2,128)} %bitcast.26, f32[6,2,32]{2,1,0:T(2,128)} %bitcast.27), custom_call_target="tpu_custom_call" | custom-call | flops 1000000000 | bytes 3000000 | tf_op jit(solution)/shard_map/pallas_call | solution.py:304
  0.9 3.1 %collective-permute-start = (bf16[16,2176]{1,0:T(8,128)(2,1)S(1)}, bf16[16,2176]{1,0:T(8,128)(2,1)S(1)}, u32[]{:S(2)}, u32[]{:S(2)}) collective-permute-start(bf16[16,2176]{1,0:T(8,128)(2,1)S(1)} %shard_map.64.packed.first.one), channel_id=1, source_target_pairs={{0,4},{4,0},{8,12},{12,8},{1,5},{5,1},{9,13},{13,9},{2,6},{6,2},{1... | collective-permute-start | bytes 208904 | tf_op jit(solution)/shard_map/ppermute | solution.py:317
  4.0 2.6 %collective-permute-start.1 = (bf16[16,2176]{1,0:T(8,128)(2,1)S(1)}, bf16[16,2176]{1,0:T(8,128)(2,1)S(1)}, u32[]{:S(2)}, u32[]{:S(2)}) collective-permute-start(bf16[16,2176]{1,0:T(8,128)(2,1)S(1)} %shard_map.64.packed.first.one), channel_id=1, source_target_pairs={{0,8},{4,12},{8,0},{12,4},{1,9},{5,13},{9,1},{13,5},{2,10},{6,14},... | collective-permute-start | bytes 208904 | tf_op jit(solution)/shard_map/ppermute | solution.py:317
  6.5 0.0 collective-permute-start.2
  6.5 0.1 pad_add_fusion.place
  6.6 6.7 %shard_map.65 = (bf16[12,352,1024]{2,1,0:T(8,128)(2,1)S(1)}, bf16[12,352,1024]{2,1,0:T(8,128)(2,1)S(1)}) custom-call(s32[2]{0:T(128)S(1)} %pad_add_fusion.place, bf16[16,2176]{1,0:T(8,128)(2,1)S(1)} %shard_map.64.packed.first.one, bf16[16,352,2048]{2,1,0:T(8,128)(2,1)} %bitcast.19, bf16[16,352,2048]{2,1,0:T(8,128)(2,1)} %bitcast.22), custom_call_target="tpu_custom_call" | custom-call | flops 7000000000 | bytes 21000000 | tf_op jit(solution)/shard_map/pallas_call | solution.py:304
  13.4 0.0 collective-permute-done.second.two
  13.4 0.0 collective-permute-done.1.third.three
  13.4 0.0 collective-permute-done.2.fourth.four
  13.4 0.1 collective-permute-start.4
  13.5 1.8 %collective-permute-start.3 = (bf16[256,512]{1,0:T(8,128)(2,1)S(1)}, bf16[256,512]{1,0:T(8,128)(2,1)S(1)}, u32[]{:S(2)}, u32[]{:S(2)}) collective-permute-start(bf16[256,512]{1,0:T(8,128)(2,1)S(1)} %shard_map.66.near), channel_id=1, source_target_pairs={{0,2},{1,3},{2,0},{3,1},{4,6},{5,7},{6,4},{7,5},{8,10},{9,11},{10,... | collective-permute-start | bytes 786440 | tf_op jit(solution)/shard_map/ppermute | solution.py:317
  15.3 0.0 collective-permute-done.4.far
  15.3 11.2 %shard_map.67 = (bf16[768,256]{1,0:T(8,128)(2,1)S(1)}, bf16[256,768]{1,0:T(8,128)(2,1)S(1)}, f32[768,128]{1,0:T(8,128)S(1)}, f32[768,352]{1,0:T(8,128)S(1)}, f32...) custom-call(s32[2]{0:T(128)S(1)} %pad_add_fusion.place, ...), custom_call_target="tpu_custom_call" | custom-call | flops 8999999488 | bytes 27000000 | tf_op jit(solution)/shard_map/pallas_call | solution.py:304
  26.6 0.0 collective-permute-done.3.near
  26.6 0.3 collective-permute-start.5
  26.9 1.3 %collective-permute-done.5.far = bf16[256,512]{1,0:T(8,128)(2,1)S(1)} collective-permute-done((bf16[256,512]{1,0:T(8,128)(2,1)S(1)}, bf16[256,512]{1,0:T(8,128)(2,1)S(1)}, u32[]{:S(2)}, u32[]{:S(2)}) %collective-permute-start.5) | collective-permute-done | bytes 262176 | tf_op jit(solution)/shard_map/ppermute | solution.py:317
  28.2 11.5 %shard_map.68 = (bf16[768,352]{1,0:T(8,128)(2,1)S(1)}, bf16[2,256,512]{2,1,0:T(8,128)(2,1)S(1)}, bf16[16,352,512]{2,1,0:T(8,128)(2,1)S(1)}) custom-call(s32[2]{0:T(128)S(1)} %pad_add_fusion.place, bf16[256,512]{1,0:T(8,128)(2,1)S(1)} %collective-permute-done.3.near, bf16[256,512]{1,0:T(8,128)(2,1)S(1)} %collective-permute-done.5.far, ...), custom_call_target="tpu_custom_call" | custom-call | flops 12000000000 | bytes 36000000 | tf_op jit(solution)/shard_map/pallas_call | solution.py:304
  39.7 0.3 collective-permute-start.6
  40.1 2.3 %shard_map.69 = bf16[256,512]{1,0:T(8,128)(2,1)S(1)} custom-call(s32[2]{0:T(128)S(1)} %pad_add_fusion.place, bf16[768,352]{1,0:T(8,128)(2,1)S(1)} %get-tuple-element.49.hidden, bf16[256,768]{1,0:T(8,128)(2,1)S(1)} %get-tuple-element.39.pick_back, bf16[16,352,512]{2,1,0:T(8,128)(2,1)S(1)} %get-tuple-element.47.down), custom_call_target="tpu_custom_call" | custom-call | flops 3000000000 | bytes 9000000 | tf_op jit(solution)/shard_map/pallas_call | solution.py:304
  42.4 0.0 collective-permute-done.6
  42.4 0.1 fusion.1
  42.5 1.4 %collective-permute-start.7 = (bf16[256,512]{1,0:T(8,128)(2,1)S(1)}, bf16[256,512]{1,0:T(8,128)(2,1)S(1)}, u32[]{:S(2)}, u32[]{:S(2)}) collective-permute-start(bf16[256,512]{1,0:T(8,128)(2,1)S(1)} %fusion.1), channel_id=1, source_target_pairs={{0,2},{1,3},{2,0},{3,1},{4,6},{5,7},{6,4},{7,5},{8,10},{9,11},{10,... | collective-permute-start | bytes 786440 | tf_op jit(solution)/shard_map/ppermute | solution.py:317
  43.9 4.1 %shard_map.70 = bf16[256,512]{1,0:T(8,128)(2,1)S(1)} custom-call(s32[2]{0:T(128)S(1)} %pad_add_fusion.place, bf16[768,352]{1,0:T(8,128)(2,1)S(1)} %get-tuple-element.49.hidden, bf16[256,768]{1,0:T(8,128)(2,1)S(1)} %get-tuple-element.39.pick_back, bf16[16,352,2048]{2,1,0:T(8,128)(2,1)} %wd.3), custom_call_target="tpu_custom_call" | custom-call | flops 4000000000 | bytes 12000000 | tf_op jit(solution)/shard_map/pallas_call | solution.py:304
  48.0 3.0 %collective-permute-done.7 = bf16[256,512]{1,0:T(8,128)(2,1)S(1)} collective-permute-done((bf16[256,512]{1,0:T(8,128)(2,1)S(1)}, bf16[256,512]{1,0:T(8,128)(2,1)S(1)}, u32[]{:S(2)}, u32[]{:S(2)}) %collective-permute-start.7) | collective-permute-done | bytes 262176 | tf_op jit(solution)/shard_map/ppermute | solution.py:317
  51.0 0.1 fusion.5
  51.2 3.7 %collective-permute-start.10 = (bf16[64,512]{1,0:T(8,128)(2,1)S(1)}, bf16[64,512]{1,0:T(8,128)(2,1)S(1)}, u32[]{:S(2)}, u32[]{:S(2)}) collective-permute-start(bf16[64,512]{1,0:T(8,128)(2,1)S(1)} %get-tuple-element.54), channel_id=1, source_target_pairs={{0,12},{4,8},{8,4},{12,0},{1,13},{5,9},{9,5},{13,1},{2,14},{6,10},... | collective-permute-start | bytes 196616 | tf_op jit(solution)/shard_map/ppermute | solution.py:317
  54.8 0.0 collective-permute-start.8
  54.8 0.8 %collective-permute-start.9 = (bf16[64,512]{1,0:T(8,128)(2,1)S(1)}, bf16[64,512]{1,0:T(8,128)(2,1)S(1)}, u32[]{:S(2)}, u32[]{:S(2)}) collective-permute-start(bf16[64,512]{1,0:T(8,128)(2,1)S(1)} %get-tuple-element.55), channel_id=1, source_target_pairs={{0,8},{4,12},{8,0},{12,4},{1,9},{5,13},{9,1},{13,5},{2,10},{6,14},... | collective-permute-start | bytes 196616 | tf_op jit(solution)/shard_map/ppermute | solution.py:317
  55.6 1.8 %collective-permute-done.10 = bf16[64,512]{1,0:T(8,128)(2,1)S(1)} collective-permute-done((bf16[64,512]{1,0:T(8,128)(2,1)S(1)}, bf16[64,512]{1,0:T(8,128)(2,1)S(1)}, u32[]{:S(2)}, u32[]{:S(2)}) %collective-permute-start.10) | collective-permute-done | bytes 65568 | tf_op jit(solution)/shard_map/ppermute | solution.py:317
  57.4 2.0 %collective-permute-done.8 = bf16[64,512]{1,0:T(8,128)(2,1)S(1)} collective-permute-done((bf16[64,512]{1,0:T(8,128)(2,1)S(1)}, bf16[64,512]{1,0:T(8,128)(2,1)S(1)}, u32[]{:S(2)}, u32[]{:S(2)}) %collective-permute-start.8) | collective-permute-done | bytes 65568 | tf_op jit(solution)/shard_map/ppermute | solution.py:317
  59.4 0.7 %collective-permute-done.9 = bf16[64,512]{1,0:T(8,128)(2,1)S(1)} collective-permute-done((bf16[64,512]{1,0:T(8,128)(2,1)S(1)}, bf16[64,512]{1,0:T(8,128)(2,1)S(1)}, u32[]{:S(2)}, u32[]{:S(2)}) %collective-permute-start.9) | collective-permute-done | bytes 65568 | tf_op jit(solution)/shard_map/ppermute | solution.py:317
  60.1 0.7 %fusion.4 = bf16[64,512]{1,0:T(8,128)(2,1)} fusion(f32[256,512]{1,0:T(8,128)S(1)} %get-tuple-element.52, bf16[64,512]{1,0:T(8,128)(2,1)S(1)} %collective-permute-done.10, bf16[64,512]{1,0:T(8,128)(2,1)S(1)} %collective-permute-done.9, bf16[64,512]{1,0:T(8,128)(2,1)S(1)} %collective-permute-done.8), kind=kLoop, calls=%fused_computation.9 | loop fusion | flops 229376 | bytes 393216 | tf_op jit(solution)/shard_map/convert_element_type | solution.py:404
  (2 shorter events, 0.0 us)
Async XLA Ops:
  0.9 12.5 %collective-permute-start = (bf16[16,2176]{1,0:T(8,128)(2,1)S(1)}, bf16[16,2176]{1,0:T(8,128)(2,1)S(1)}, u32[]{:S(2)}, u32[]{:S(2)}) collective-permute-start(bf16[16,2176]{1,0:T(8,128)(2,1)S(1)} %shard_map.64.packed.first.one), channel_id=1, source_target_pairs={{0,4},{4,0},{8,12},{12,8},{1,5},{5,1},{9,13},{13,9},{2,6},{6,2},{1... | collective-permute-start | bytes 208904 | tf_op jit(solution)/shard_map/ppermute | solution.py:317
  4.0 9.4 %collective-permute-start.1 = (bf16[16,2176]{1,0:T(8,128)(2,1)S(1)}, bf16[16,2176]{1,0:T(8,128)(2,1)S(1)}, u32[]{:S(2)}, u32[]{:S(2)}) collective-permute-start(bf16[16,2176]{1,0:T(8,128)(2,1)S(1)} %shard_map.64.packed.first.one), channel_id=1, source_target_pairs={{0,8},{4,12},{8,0},{12,4},{1,9},{5,13},{9,1},{13,5},{2,10},{6,14},... | collective-permute-start | bytes 208904 | tf_op jit(solution)/shard_map/ppermute | solution.py:317
  6.5 6.9 %collective-permute-start.2 = (bf16[16,2176]{1,0:T(8,128)(2,1)S(1)}, bf16[16,2176]{1,0:T(8,128)(2,1)S(1)}, u32[]{:S(2)}, u32[]{:S(2)}) collective-permute-start(bf16[16,2176]{1,0:T(8,128)(2,1)S(1)} %shard_map.64.packed.first.one), channel_id=1, source_target_pairs={{0,12},{4,8},{8,4},{12,0},{1,13},{5,9},{9,5},{13,1},{2,14},{6,10},... | collective-permute-start | bytes 208904 | tf_op jit(solution)/shard_map/ppermute | solution.py:317
  13.4 1.9 %collective-permute-start.4 = (bf16[256,512]{1,0:T(8,128)(2,1)S(1)}, bf16[256,512]{1,0:T(8,128)(2,1)S(1)}, u32[]{:S(2)}, u32[]{:S(2)}) collective-permute-start(bf16[256,512]{1,0:T(8,128)(2,1)S(1)} %shard_map.66.near), channel_id=1, source_target_pairs={{0,1},{1,0},{2,3},{3,2},{4,5},{5,4},{6,7},{7,6},{8,9},{9,8},{10,11... | collective-permute-start | bytes 786440 | tf_op jit(solution)/shard_map/ppermute | solution.py:317
  13.5 13.1 %collective-permute-start.3 = (bf16[256,512]{1,0:T(8,128)(2,1)S(1)}, bf16[256,512]{1,0:T(8,128)(2,1)S(1)}, u32[]{:S(2)}, u32[]{:S(2)}) collective-permute-start(bf16[256,512]{1,0:T(8,128)(2,1)S(1)} %shard_map.66.near), channel_id=1, source_target_pairs={{0,2},{1,3},{2,0},{3,1},{4,6},{5,7},{6,4},{7,5},{8,10},{9,11},{10,... | collective-permute-start | bytes 786440 | tf_op jit(solution)/shard_map/ppermute | solution.py:317
  26.6 1.6 %collective-permute-start.5 = (bf16[256,512]{1,0:T(8,128)(2,1)S(1)}, bf16[256,512]{1,0:T(8,128)(2,1)S(1)}, u32[]{:S(2)}, u32[]{:S(2)}) collective-permute-start(bf16[256,512]{1,0:T(8,128)(2,1)S(1)} %collective-permute-done.3.near), channel_id=1, source_target_pairs={{0,1},{1,0},{2,3},{3,2},{4,5},{5,4},{6,7},{7,6},{8,9},{9,8},{10,11... | collective-permute-start | bytes 786440 | tf_op jit(solution)/shard_map/ppermute | solution.py:317
  39.7 2.7 %collective-permute-start.6 = (bf16[2,256,512]{2,1,0:T(8,128)(2,1)S(1)}, bf16[2,256,512]{2,1,0:T(8,128)(2,1)S(1)}, u32[]{:S(2)}, u32[]{:S(2)}) collective-permute-start(bf16[2,256,512]{2,1,0:T(8,128)(2,1)S(1)} %get-tuple-element.48), channel_id=1, source_target_pairs={{0,1},{1,0},{2,3},{3,2},{4,5},{5,4},{6,7},{7,6},{8,9},{9,8},{10,11... | collective-permute-start | bytes 1572872 | tf_op jit(solution)/shard_map/ppermute | solution.py:317
  42.5 8.5 %collective-permute-start.7 = (bf16[256,512]{1,0:T(8,128)(2,1)S(1)}, bf16[256,512]{1,0:T(8,128)(2,1)S(1)}, u32[]{:S(2)}, u32[]{:S(2)}) collective-permute-start(bf16[256,512]{1,0:T(8,128)(2,1)S(1)} %fusion.1), channel_id=1, source_target_pairs={{0,2},{1,3},{2,0},{3,1},{4,6},{5,7},{6,4},{7,5},{8,10},{9,11},{10,... | collective-permute-start | bytes 786440 | tf_op jit(solution)/shard_map/ppermute | solution.py:317
  51.2 6.2 %collective-permute-start.10 = (bf16[64,512]{1,0:T(8,128)(2,1)S(1)}, bf16[64,512]{1,0:T(8,128)(2,1)S(1)}, u32[]{:S(2)}, u32[]{:S(2)}) collective-permute-start(bf16[64,512]{1,0:T(8,128)(2,1)S(1)} %get-tuple-element.54), channel_id=1, source_target_pairs={{0,12},{4,8},{8,4},{12,0},{1,13},{5,9},{9,5},{13,1},{2,14},{6,10},... | collective-permute-start | bytes 196616 | tf_op jit(solution)/shard_map/ppermute | solution.py:317
  54.8 4.6 %collective-permute-start.8 = (bf16[64,512]{1,0:T(8,128)(2,1)S(1)}, bf16[64,512]{1,0:T(8,128)(2,1)S(1)}, u32[]{:S(2)}, u32[]{:S(2)}) collective-permute-start(bf16[64,512]{1,0:T(8,128)(2,1)S(1)} %get-tuple-element.53), channel_id=1, source_target_pairs={{0,4},{4,0},{8,12},{12,8},{1,5},{5,1},{9,13},{13,9},{2,6},{6,2},{1... | collective-permute-start | bytes 196616 | tf_op jit(solution)/shard_map/ppermute | solution.py:317
  54.8 5.2 %collective-permute-start.9 = (bf16[64,512]{1,0:T(8,128)(2,1)S(1)}, bf16[64,512]{1,0:T(8,128)(2,1)S(1)}, u32[]{:S(2)}, u32[]{:S(2)}) collective-permute-start(bf16[64,512]{1,0:T(8,128)(2,1)S(1)} %get-tuple-element.55), channel_id=1, source_target_pairs={{0,8},{4,12},{8,0},{12,4},{1,9},{5,13},{9,1},{13,5},{2,10},{6,14},... | collective-permute-start | bytes 196616 | tf_op jit(solution)/shard_map/ppermute | solution.py:317

commit v7 on v6

--- a/solution.py
+++ b/solution.py
@@ -277,7 +277,7 @@
     def lower(e, mine):
         given[mine, :] = dot(hidden[mine, :], down[e], NN).astype(jnp.bfloat16)
 
-    in_groups(0, down.shape[0], slots, lower, size=4)
+    in_groups(0, down.shape[0], slots, lower, size=8)
     out[...] = dot(pick_back[...], given[...], NN).astype(jnp.bfloat16)
 
 

time: 61.1 us -> 60.8 us (level)
  no operation moved by 1% of the time
where the time goes in v7:
time: 60.8 us; the launch traced here: 60.5 us
  Pallas kernels  36.6 us (60%)
  starting transfers between devices  14.1 us (23%)
  waiting for transfers between devices  8.75 us (14%)
  other arithmetic  0.9 us (1%)
    pallas_call x7, Pallas kernels, call(): pl.pallas_call(kernel, in_specs=specs + [there] * fetched, out_specs=jax....  36.6 us
    ppermute x11, starting transfers between devices, swap(): return lax.ppermute(a, axis, [(i, i ^ bits) for i in range(n)])  14.1 us
    ppermute x11, waiting for transfers between devices, swap(): return lax.ppermute(a, axis, [(i, i ^ bits) for i in range(n)])  8.75 us
  transfers between devices with their start and end apart: 11, of which 5 were waited for; matrix products, arithmetic and copies ran while one was open for 0% of the time, Pallas kernels for 40%

profile of v7, /device:TPU:0, one launch (start us, length us, event | category | flops | bytes accessed | tf_op | source)
XLA Modules:
  0.0 60.5 jit_solution(17356434780906796847)
XLA Ops:
  0.0 0.9 %shard_map.64.packed.first.one = bf16[16,2176]{1,0:T(8,128)(2,1)S(1)} custom-call(bf16[64,512]{1,0:T(8,128)(2,1)} %bitcast.25, s32[6,2,32]{2,1,0:T(2,128)} %bitcast.26, f32[6,2,32]{2,1,0:T(2,128)} %bitcast.27), custom_call_target="tpu_custom_call" | custom-call | flops 1000000000 | bytes 3000000 | tf_op jit(solution)/shard_map/pallas_call | solution.py:304
  0.9 3.1 %collective-permute-start = (bf16[16,2176]{1,0:T(8,128)(2,1)S(1)}, bf16[16,2176]{1,0:T(8,128)(2,1)S(1)}, u32[]{:S(2)}, u32[]{:S(2)}) collective-permute-start(bf16[16,2176]{1,0:T(8,128)(2,1)S(1)} %shard_map.64.packed.first.one), channel_id=1, source_target_pairs={{0,4},{4,0},{8,12},{12,8},{1,5},{5,1},{9,13},{13,9},{2,6},{6,2},{1... | collective-permute-start | bytes 208904 | tf_op jit(solution)/shard_map/ppermute | solution.py:317
  4.0 2.6 %collective-permute-start.1 = (bf16[16,2176]{1,0:T(8,128)(2,1)S(1)}, bf16[16,2176]{1,0:T(8,128)(2,1)S(1)}, u32[]{:S(2)}, u32[]{:S(2)}) collective-permute-start(bf16[16,2176]{1,0:T(8,128)(2,1)S(1)} %shard_map.64.packed.first.one), channel_id=1, source_target_pairs={{0,8},{4,12},{8,0},{12,4},{1,9},{5,13},{9,1},{13,5},{2,10},{6,14},... | collective-permute-start | bytes 208904 | tf_op jit(solution)/shard_map/ppermute | solution.py:317
  6.5 0.0 collective-permute-start.2
  6.5 0.1 pad_add_fusion.place
  6.6 6.7 %shard_map.65 = (bf16[12,352,1024]{2,1,0:T(8,128)(2,1)S(1)}, bf16[12,352,1024]{2,1,0:T(8,128)(2,1)S(1)}) custom-call(s32[2]{0:T(128)S(1)} %pad_add_fusion.place, bf16[16,2176]{1,0:T(8,128)(2,1)S(1)} %shard_map.64.packed.first.one, bf16[16,352,2048]{2,1,0:T(8,128)(2,1)} %bitcast.19, bf16[16,352,2048]{2,1,0:T(8,128)(2,1)} %bitcast.22), custom_call_target="tpu_custom_call" | custom-call | flops 7000000000 | bytes 21000000 | tf_op jit(solution)/shard_map/pallas_call | solution.py:304
  13.4 0.0 collective-permute-done.second.two
  13.4 0.0 collective-permute-done.1.third.three
  13.4 0.0 collective-permute-done.2.fourth.four
  13.4 0.1 collective-permute-start.4
  13.5 1.8 %collective-permute-start.3 = (bf16[256,512]{1,0:T(8,128)(2,1)S(1)}, bf16[256,512]{1,0:T(8,128)(2,1)S(1)}, u32[]{:S(2)}, u32[]{:S(2)}) collective-permute-start(bf16[256,512]{1,0:T(8,128)(2,1)S(1)} %shard_map.66.near), channel_id=1, source_target_pairs={{0,2},{1,3},{2,0},{3,1},{4,6},{5,7},{6,4},{7,5},{8,10},{9,11},{10,... | collective-permute-start | bytes 786440 | tf_op jit(solution)/shard_map/ppermute | solution.py:317
  15.3 0.0 collective-permute-done.4.far
  15.3 11.2 %shard_map.67 = (bf16[768,256]{1,0:T(8,128)(2,1)S(1)}, bf16[256,768]{1,0:T(8,128)(2,1)S(1)}, f32[768,128]{1,0:T(8,128)S(1)}, f32[768,352]{1,0:T(8,128)S(1)}, f32...) custom-call(s32[2]{0:T(128)S(1)} %pad_add_fusion.place, ...), custom_call_target="tpu_custom_call" | custom-call | flops 8999999488 | bytes 27000000 | tf_op jit(solution)/shard_map/pallas_call | solution.py:304
  26.6 0.0 collective-permute-done.3.near
  26.6 0.3 collective-permute-start.5
  26.9 1.3 %collective-permute-done.5.far = bf16[256,512]{1,0:T(8,128)(2,1)S(1)} collective-permute-done((bf16[256,512]{1,0:T(8,128)(2,1)S(1)}, bf16[256,512]{1,0:T(8,128)(2,1)S(1)}, u32[]{:S(2)}, u32[]{:S(2)}) %collective-permute-start.5) | collective-permute-done | bytes 262176 | tf_op jit(solution)/shard_map/ppermute | solution.py:317
  28.2 11.5 %shard_map.68 = (bf16[768,352]{1,0:T(8,128)(2,1)S(1)}, bf16[2,256,512]{2,1,0:T(8,128)(2,1)S(1)}, bf16[16,352,512]{2,1,0:T(8,128)(2,1)S(1)}) custom-call(s32[2]{0:T(128)S(1)} %pad_add_fusion.place, bf16[256,512]{1,0:T(8,128)(2,1)S(1)} %collective-permute-done.3.near, bf16[256,512]{1,0:T(8,128)(2,1)S(1)} %collective-permute-done.5.far, ...), custom_call_target="tpu_custom_call" | custom-call | flops 12000000000 | bytes 36000000 | tf_op jit(solution)/shard_map/pallas_call | solution.py:304
  39.7 0.3 collective-permute-start.6
  40.1 2.1 %shard_map.69 = bf16[256,512]{1,0:T(8,128)(2,1)S(1)} custom-call(s32[2]{0:T(128)S(1)} %pad_add_fusion.place, bf16[768,352]{1,0:T(8,128)(2,1)S(1)} %get-tuple-element.49.hidden, bf16[256,768]{1,0:T(8,128)(2,1)S(1)} %get-tuple-element.39.pick_back, bf16[16,352,512]{2,1,0:T(8,128)(2,1)S(1)} %get-tuple-element.47.down), custom_call_target="tpu_custom_call" | custom-call | flops 3000000000 | bytes 9000000 | tf_op jit(solution)/shard_map/pallas_call | solution.py:304
  42.2 0.0 collective-permute-done.6
  42.2 0.1 fusion.1
  42.3 1.4 %collective-permute-start.7 = (bf16[256,512]{1,0:T(8,128)(2,1)S(1)}, bf16[256,512]{1,0:T(8,128)(2,1)S(1)}, u32[]{:S(2)}, u32[]{:S(2)}) collective-permute-start(bf16[256,512]{1,0:T(8,128)(2,1)S(1)} %fusion.1), channel_id=1, source_target_pairs={{0,2},{1,3},{2,0},{3,1},{4,6},{5,7},{6,4},{7,5},{8,10},{9,11},{10,... | collective-permute-start | bytes 786440 | tf_op jit(solution)/shard_map/ppermute | solution.py:317
  43.7 4.1 %shard_map.70 = bf16[256,512]{1,0:T(8,128)(2,1)S(1)} custom-call(s32[2]{0:T(128)S(1)} %pad_add_fusion.place, bf16[768,352]{1,0:T(8,128)(2,1)S(1)} %get-tuple-element.49.hidden, bf16[256,768]{1,0:T(8,128)(2,1)S(1)} %get-tuple-element.39.pick_back, bf16[16,352,2048]{2,1,0:T(8,128)(2,1)} %wd.3), custom_call_target="tpu_custom_call" | custom-call | flops 4000000000 | bytes 12000000 | tf_op jit(solution)/shard_map/pallas_call | solution.py:304
  47.8 3.0 %collective-permute-done.7 = bf16[256,512]{1,0:T(8,128)(2,1)S(1)} collective-permute-done((bf16[256,512]{1,0:T(8,128)(2,1)S(1)}, bf16[256,512]{1,0:T(8,128)(2,1)S(1)}, u32[]{:S(2)}, u32[]{:S(2)}) %collective-permute-start.7) | collective-permute-done | bytes 262176 | tf_op jit(solution)/shard_map/ppermute | solution.py:317
  50.8 0.1 fusion.5
  50.9 3.7 %collective-permute-start.10 = (bf16[64,512]{1,0:T(8,128)(2,1)S(1)}, bf16[64,512]{1,0:T(8,128)(2,1)S(1)}, u32[]{:S(2)}, u32[]{:S(2)}) collective-permute-start(bf16[64,512]{1,0:T(8,128)(2,1)S(1)} %get-tuple-element.54), channel_id=1, source_target_pairs={{0,12},{4,8},{8,4},{12,0},{1,13},{5,9},{9,5},{13,1},{2,14},{6,10},... | collective-permute-start | bytes 196616 | tf_op jit(solution)/shard_map/ppermute | solution.py:317
  54.6 0.0 collective-permute-start.8
  54.6 0.8 %collective-permute-start.9 = (bf16[64,512]{1,0:T(8,128)(2,1)S(1)}, bf16[64,512]{1,0:T(8,128)(2,1)S(1)}, u32[]{:S(2)}, u32[]{:S(2)}) collective-permute-start(bf16[64,512]{1,0:T(8,128)(2,1)S(1)} %get-tuple-element.55), channel_id=1, source_target_pairs={{0,8},{4,12},{8,0},{12,4},{1,9},{5,13},{9,1},{13,5},{2,10},{6,14},... | collective-permute-start | bytes 196616 | tf_op jit(solution)/shard_map/ppermute | solution.py:317
  55.4 1.8 %collective-permute-done.10 = bf16[64,512]{1,0:T(8,128)(2,1)S(1)} collective-permute-done((bf16[64,512]{1,0:T(8,128)(2,1)S(1)}, bf16[64,512]{1,0:T(8,128)(2,1)S(1)}, u32[]{:S(2)}, u32[]{:S(2)}) %collective-permute-start.10) | collective-permute-done | bytes 65568 | tf_op jit(solution)/shard_map/ppermute | solution.py:317
  57.2 2.0 %collective-permute-done.8 = bf16[64,512]{1,0:T(8,128)(2,1)S(1)} collective-permute-done((bf16[64,512]{1,0:T(8,128)(2,1)S(1)}, bf16[64,512]{1,0:T(8,128)(2,1)S(1)}, u32[]{:S(2)}, u32[]{:S(2)}) %collective-permute-start.8) | collective-permute-done | bytes 65568 | tf_op jit(solution)/shard_map/ppermute | solution.py:317
  59.2 0.7 %collective-permute-done.9 = bf16[64,512]{1,0:T(8,128)(2,1)S(1)} collective-permute-done((bf16[64,512]{1,0:T(8,128)(2,1)S(1)}, bf16[64,512]{1,0:T(8,128)(2,1)S(1)}, u32[]{:S(2)}, u32[]{:S(2)}) %collective-permute-start.9) | collective-permute-done | bytes 65568 | tf_op jit(solution)/shard_map/ppermute | solution.py:317
  59.8 0.7 %fusion.4 = bf16[64,512]{1,0:T(8,128)(2,1)} fusion(f32[256,512]{1,0:T(8,128)S(1)} %get-tuple-element.52, bf16[64,512]{1,0:T(8,128)(2,1)S(1)} %collective-permute-done.10, bf16[64,512]{1,0:T(8,128)(2,1)S(1)} %collective-permute-done.9, bf16[64,512]{1,0:T(8,128)(2,1)S(1)} %collective-permute-done.8), kind=kLoop, calls=%fused_computation.9 | loop fusion | flops 229376 | bytes 393216 | tf_op jit(solution)/shard_map/convert_element_type | solution.py:404
  (2 shorter events, 0.0 us)
Async XLA Ops:
  0.9 12.5 %collective-permute-start = (bf16[16,2176]{1,0:T(8,128)(2,1)S(1)}, bf16[16,2176]{1,0:T(8,128)(2,1)S(1)}, u32[]{:S(2)}, u32[]{:S(2)}) collective-permute-start(bf16[16,2176]{1,0:T(8,128)(2,1)S(1)} %shard_map.64.packed.first.one), channel_id=1, source_target_pairs={{0,4},{4,0},{8,12},{12,8},{1,5},{5,1},{9,13},{13,9},{2,6},{6,2},{1... | collective-permute-start | bytes 208904 | tf_op jit(solution)/shard_map/ppermute | solution.py:317
  4.0 9.4 %collective-permute-start.1 = (bf16[16,2176]{1,0:T(8,128)(2,1)S(1)}, bf16[16,2176]{1,0:T(8,128)(2,1)S(1)}, u32[]{:S(2)}, u32[]{:S(2)}) collective-permute-start(bf16[16,2176]{1,0:T(8,128)(2,1)S(1)} %shard_map.64.packed.first.one), channel_id=1, source_target_pairs={{0,8},{4,12},{8,0},{12,4},{1,9},{5,13},{9,1},{13,5},{2,10},{6,14},... | collective-permute-start | bytes 208904 | tf_op jit(solution)/shard_map/ppermute | solution.py:317
  6.5 6.9 %collective-permute-start.2 = (bf16[16,2176]{1,0:T(8,128)(2,1)S(1)}, bf16[16,2176]{1,0:T(8,128)(2,1)S(1)}, u32[]{:S(2)}, u32[]{:S(2)}) collective-permute-start(bf16[16,2176]{1,0:T(8,128)(2,1)S(1)} %shard_map.64.packed.first.one), channel_id=1, source_target_pairs={{0,12},{4,8},{8,4},{12,0},{1,13},{5,9},{9,5},{13,1},{2,14},{6,10},... | collective-permute-start | bytes 208904 | tf_op jit(solution)/shard_map/ppermute | solution.py:317
  13.4 1.9 %collective-permute-start.4 = (bf16[256,512]{1,0:T(8,128)(2,1)S(1)}, bf16[256,512]{1,0:T(8,128)(2,1)S(1)}, u32[]{:S(2)}, u32[]{:S(2)}) collective-permute-start(bf16[256,512]{1,0:T(8,128)(2,1)S(1)} %shard_map.66.near), channel_id=1, source_target_pairs={{0,1},{1,0},{2,3},{3,2},{4,5},{5,4},{6,7},{7,6},{8,9},{9,8},{10,11... | collective-permute-start | bytes 786440 | tf_op jit(solution)/shard_map/ppermute | solution.py:317
  13.5 13.1 %collective-permute-start.3 = (bf16[256,512]{1,0:T(8,128)(2,1)S(1)}, bf16[256,512]{1,0:T(8,128)(2,1)S(1)}, u32[]{:S(2)}, u32[]{:S(2)}) collective-permute-start(bf16[256,512]{1,0:T(8,128)(2,1)S(1)} %shard_map.66.near), channel_id=1, source_target_pairs={{0,2},{1,3},{2,0},{3,1},{4,6},{5,7},{6,4},{7,5},{8,10},{9,11},{10,... | collective-permute-start | bytes 786440 | tf_op jit(solution)/shard_map/ppermute | solution.py:317
  26.6 1.6 %collective-permute-start.5 = (bf16[256,512]{1,0:T(8,128)(2,1)S(1)}, bf16[256,512]{1,0:T(8,128)(2,1)S(1)}, u32[]{:S(2)}, u32[]{:S(2)}) collective-permute-start(bf16[256,512]{1,0:T(8,128)(2,1)S(1)} %collective-permute-done.3.near), channel_id=1, source_target_pairs={{0,1},{1,0},{2,3},{3,2},{4,5},{5,4},{6,7},{7,6},{8,9},{9,8},{10,11... | collective-permute-start | bytes 786440 | tf_op jit(solution)/shard_map/ppermute | solution.py:317
  39.7 2.5 %collective-permute-start.6 = (bf16[2,256,512]{2,1,0:T(8,128)(2,1)S(1)}, bf16[2,256,512]{2,1,0:T(8,128)(2,1)S(1)}, u32[]{:S(2)}, u32[]{:S(2)}) collective-permute-start(bf16[2,256,512]{2,1,0:T(8,128)(2,1)S(1)} %get-tuple-element.48), channel_id=1, source_target_pairs={{0,1},{1,0},{2,3},{3,2},{4,5},{5,4},{6,7},{7,6},{8,9},{9,8},{10,11... | collective-permute-start | bytes 1572872 | tf_op jit(solution)/shard_map/ppermute | solution.py:317
  42.3 8.5 %collective-permute-start.7 = (bf16[256,512]{1,0:T(8,128)(2,1)S(1)}, bf16[256,512]{1,0:T(8,128)(2,1)S(1)}, u32[]{:S(2)}, u32[]{:S(2)}) collective-permute-start(bf16[256,512]{1,0:T(8,128)(2,1)S(1)} %fusion.1), channel_id=1, source_target_pairs={{0,2},{1,3},{2,0},{3,1},{4,6},{5,7},{6,4},{7,5},{8,10},{9,11},{10,... | collective-permute-start | bytes 786440 | tf_op jit(solution)/shard_map/ppermute | solution.py:317
  50.9 6.2 %collective-permute-start.10 = (bf16[64,512]{1,0:T(8,128)(2,1)S(1)}, bf16[64,512]{1,0:T(8,128)(2,1)S(1)}, u32[]{:S(2)}, u32[]{:S(2)}) collective-permute-start(bf16[64,512]{1,0:T(8,128)(2,1)S(1)} %get-tuple-element.54), channel_id=1, source_target_pairs={{0,12},{4,8},{8,4},{12,0},{1,13},{5,9},{9,5},{13,1},{2,14},{6,10},... | collective-permute-start | bytes 196616 | tf_op jit(solution)/shard_map/ppermute | solution.py:317
  54.6 4.6 %collective-permute-start.8 = (bf16[64,512]{1,0:T(8,128)(2,1)S(1)}, bf16[64,512]{1,0:T(8,128)(2,1)S(1)}, u32[]{:S(2)}, u32[]{:S(2)}) collective-permute-start(bf16[64,512]{1,0:T(8,128)(2,1)S(1)} %get-tuple-element.53), channel_id=1, source_target_pairs={{0,4},{4,0},{8,12},{12,8},{1,5},{5,1},{9,13},{13,9},{2,6},{6,2},{1... | collective-permute-start | bytes 196616 | tf_op jit(solution)/shard_map/ppermute | solution.py:317
  54.6 5.2 %collective-permute-start.9 = (bf16[64,512]{1,0:T(8,128)(2,1)S(1)}, bf16[64,512]{1,0:T(8,128)(2,1)S(1)}, u32[]{:S(2)}, u32[]{:S(2)}) collective-permute-start(bf16[64,512]{1,0:T(8,128)(2,1)S(1)} %get-tuple-element.55), channel_id=1, source_target_pairs={{0,8},{4,12},{8,0},{12,4},{1,9},{5,13},{9,1},{13,5},{2,10},{6,14},... | collective-permute-start | bytes 196616 | tf_op jit(solution)/shard_map/ppermute | solution.py:317
